TPU v7x, 128 devices: a whole 4x4x4 slice. The times are simulated.
128 devices in a mesh: row: 8 (over y, core), col: 16 (over x, z).
Axes of the slice: x: 4, y: 4, z: 4, core: 2. Of those that a mesh axis runs over, the one named last changes fastest.
Arguments:
- rhs_tile: float32 [18432, 18432], P('row', 'col'), may hold values from -6 to 6
- factor: float32 [18432, 1536], P('row', 'col'), may hold values from -1 to 2.5, as said below
Outputs:
- whitened: float32 [18432, 18432], P('row', 'col')
Inputs may be any that keep to these rules, and one draw needn't show every extreme that they name: In elimination order factor is lower triangular: entries above the diagonal are zero, diagonal entries are at least 0.7.
All inputs are finite; a program needn't handle non-finite values.
Results may differ from a plain program's by a relative error of at most 0.0001.
Values sent between devices are 32-bit elements; how exact they have to be, the bound alone decides.
No kernel may reach another device: no remote copies, remote signals or barrier semaphores. Data moves between devices by JAX's collectives and lax.ppermute only.
A program may use at most 128 MiB of HBM per device.

v0:
```python
import jax
import jax.numpy as jnp
from jax import lax
from jax.experimental import pallas as pl
from jax.experimental.pallas import tpu as pltpu
from jax.sharding import PartitionSpec as P

F32, BF16 = jnp.float32, jnp.bfloat16
NX, NY, NZ = 4, 4, 4
ROWS, NCOL = 2304, 1152
PB, CB, PANEL, PANELS = 64, 32, 512, 3
WIN = PB * PANELS
TRAIL = ROWS - WIN
GROUPS = 4
GR = TRAIL // GROUPS
SLOTS = 6
MIB = 1024 * 1024
GROUP_ORDER = (0, 1, 3, 2)


def joint(v, dest):
    pairs = []
    for y in range(NY):
        for c in range(2):
            for x in range(NX):
                for z in range(NZ):
                    ty, tc, tx, tz = dest(y, c, x, z)
                    pairs.append(
                        (
                            (y * 2 + c) * 16 + x * 4 + z,
                            ((ty % NY) * 2 + tc % 2) * 16 + (tx % NX) * 4 + tz % NZ,
                        )
                    )
    return lax.ppermute(v, ("row", "col"), pairs)


def from_first(v, d):
    return joint(v, lambda y, c, x, z: (y, c, x - d, z) if c == 0 else (y, c, x, z - d))


def from_second(v, d):
    return joint(v, lambda y, c, x, z: (y, c, x, z - d) if c == 0 else (y, c, x - d, z))


def from_y(v, d):
    return joint(v, lambda y, c, x, z: (y - d, c, x, z))


def from_core(v):
    return joint(v, lambda y, c, x, z: (y, 1 - c, x, z))


def pack_kernel(f_ref, r_ref, l_ref, w_ref, b_ref, sem):
    copy = pltpu.make_async_copy(r_ref.at[0:WIN, :], b_ref, sem)
    copy.start()
    for p in range(PANELS):
        l_ref[p * GR : (p + 1) * GR, :] = jnp.concatenate(
            [
                f_ref[WIN + g * GR : WIN + (g + 1) * GR, p * CB : (p + 1) * CB]
                for g in range(GROUPS)
            ],
            axis=1,
        )

    def block(i, j):
        return f_ref[i * PB : (i + 1) * PB, j * CB : (j + 1) * CB]

    w_ref[0:PB, :] = jnp.concatenate([block(0, 0), block(1, 1), block(2, 2), block(1, 0)], axis=1)
    zero = jnp.zeros((PB, CB), F32)
    w_ref[PB : 2 * PB, :] = jnp.concatenate([block(2, 0), block(2, 1), zero, zero], axis=1)
    copy.wait()


def source(pos, i, j):
    core, x, z = pos[1], pos[2], pos[3]
    xs = jnp.where(core == 0, x + j, x + i) % NX
    zs = jnp.where(core == 0, z + i, z + j) % NZ
    return xs * NZ + zs


def rows_kernel(pos, g0, g1, g2, g3, out, canon, diag):
    y, core = pos[0], pos[1]
    for i, ref in enumerate((g0, g1, g2, g3)):
        for j in range(4):
            canon[source(pos, i, j)] = ref[j]
    lane = lax.broadcasted_iota(jnp.int32, (PB, 128), 1)
    row = lax.broadcasted_iota(jnp.int32, (PB, 128), 0)
    for s in range(SLOTS):
        half, q = divmod(s, 4)
        for xs in range(NX):
            total = None
            for zs in range(NZ):
                v = canon[xs * NZ + zs, half * PB : (half + 1) * PB, :]
                shift = (zs - q) % 4 * CB
                v = pltpu.roll(v, shift, 1) if shift else v
                total = v if total is None else jnp.where(lane // CB == zs, v, total)
            out[s, :, xs * 128 : (xs + 1) * 128] = total
            if s < PANELS:
                diag[s, xs] = total
    eye = (lane == row).astype(F32)
    blocks, mats, sols = [], [], []
    for p in range(PANELS):
        blk = diag[p, y]
        blocks.append(blk)
        a = jnp.where(core == 1, pltpu.roll(blk, PB, 1), blk)
        mats.append((a, a - eye))
        sols.append([eye[8 * k : 8 * k + 8] for k in range(PB // 8)])
    for i in range(PB):
        for p in range(PANELS):
            a, am = mats[p]
            k0, r0 = divmod(i, 8)
            top = sols[p][k0][r0 : r0 + 1, :] * (1.0 / a[i : i + 1, i : i + 1])
            for k in range(k0, PB // 8):
                sols[p][k] = sols[p][k] - am[8 * k : 8 * k + 8, i : i + 1] * top
    for p in range(PANELS):
        inv = jnp.concatenate(sols[p], axis=0)
        inv = jnp.where(core == 1, pltpu.roll(inv, PB, 1), inv)
        inv = jnp.where(lane // PB == core, inv, blocks[p])
        for k in range(NY):

            @pl.when(y == k)
            def _(p=p, k=k, inv=inv):
                out[p, :, k * 128 : (k + 1) * 128] = inv


def exact_dot(a, b):
    return jnp.dot(a, b, precision=lax.Precision.HIGHEST, preferred_element_type=F32)


def split(v):
    hi = v.astype(BF16)
    return hi, (v - hi.astype(F32)).astype(BF16)


def dot3(a, b):
    return jnp.dot(
        jnp.concatenate([a[0], a[0], a[1]], axis=1),
        jnp.concatenate([b[0], b[1], b[0]], axis=0),
        preferred_element_type=F32,
    )


COLS = [slice(c, min(c + 256, NCOL)) for c in range(0, NCOL, 256)]


def solve_kernel(
    pos, mine, other, bmine, bother, xh, xl, base, mat, b_ref, lh, ll, oh, ol, rh, rl, ah, al, xs, own, sem, last
):
    y, core = pos[0], pos[1]

    def copies(to, sources, sems):
        made = []
        for which, src in enumerate(sources):
            c = core if which == 0 else 1 - core
            for d in range(NY):
                r = pl.multiple_of((y + d) % NY * 128 + c * PB, PB)
                made.append(
                    pltpu.make_async_copy(
                        src.at[d], to.at[:, pl.ds(r, PB), :], sems.at[which * NY + d]
                    )
                )
        return made

    mat_copies = copies(mat, (mine, other), sem.at[0])
    b_copies = copies(b_ref, (bmine, bother), sem.at[1])
    for copy in mat_copies + b_copies:
        copy.start()
    for copy in mat_copies:
        copy.wait()

    row = lax.broadcasted_iota(jnp.int32, (128, 128), 0) // PB
    col = lax.broadcasted_iota(jnp.int32, (128, 128), 1) // PB
    inv = {}
    for p in range(PANELS):
        for b in range(4):
            blk = mat[p, b * 128 : (b + 1) * 128, b * 128 : (b + 1) * 128]
            diag = jnp.where(row == col, blk, 0.0)
            low = jnp.where(row > col, blk, 0.0)
            inv[p, b] = diag - exact_dot(diag, exact_dot(low, diag))
    for p in range(PANELS):
        for b in range(4):
            mat[p, b * 128 : (b + 1) * 128, b * 128 : (b + 1) * 128] = inv[p, b]
    for size in (128, 256):
        for p in range(PANELS):
            for b in range(0, PANEL // size, 2):
                lo, mid, hi = b * size, (b + 1) * size, (b + 2) * size
                off = exact_dot(
                    mat[p, mid:hi, mid:hi],
                    exact_dot(mat[p, mid:hi, lo:mid], mat[p, lo:mid, lo:mid]),
                )
                mat[p, mid:hi, lo:mid] = -off
    for p in range(PANELS):
        lh[p], ll[p] = split(mat[p])
        oh[p], ol[p] = split(mat[PANELS + p])

    for copy in b_copies:
        copy.wait()
    left = {1: (0,), 2: (1, 2)}
    half = PANEL // 2
    for p in range(PANELS):
        for w in COLS:
            rhs = b_ref[p, :, w]
            if p:
                o = [jnp.concatenate([v[k] for k in left[p]], axis=1) for v in (oh, ol)]
                rhs = rhs - dot3(o, [v[: p * PANEL, w] for v in (ah, al)])
            rh[p, :, w], rl[p, :, w] = split(rhs)
        for w in COLS:
            for top, depth in ((0, half), (half, PANEL)):
                x = dot3(
                    [v[p, top : top + half, :depth] for v in (lh, ll)],
                    [v[p, :depth, w] for v in (rh, rl)],
                )
                part = slice(p * PANEL + top, p * PANEL + top + half)
                xs[top : top + half, w] = x
                ah[part, w], al[part, w] = split(x)
        mine_rows = pl.multiple_of((y * 2 + core) * PB, PB)
        own[p * PB : (p + 1) * PB, :] = xs[pl.ds(mine_rows, PB), :]
        for k, i in enumerate(GROUP_ORDER):
            for j in range(4):
                src = pl.multiple_of(p * PANEL + source(pos, i, j) * CB, CB)
                dst = (k * PANELS + p) * 128 + j * CB
                xh[dst : dst + CB, :] = ah[pl.ds(src, CB), :]
                xl[dst : dst + CB, :] = al[pl.ds(src, CB), :]
    copy = pltpu.make_async_copy(own, base.at[0:WIN, :], last)
    copy.start()
    copy.wait()


def assemble_kernel(*refs):
    lrefs, (lh, ll) = refs[:-2], refs[-2:]
    g = pl.program_id(0)
    lane = lax.broadcasted_iota(jnp.int32, (GR, 128), 1) // CB
    blocks = [(ref, b) for ref in lrefs for b in range(ref.shape[0])]
    for p in range(PANELS):
        total = None
        for j, (ref, b) in enumerate(blocks):
            v = pltpu.roll(ref[b, p * GR : (p + 1) * GR, :], (j - g) % 4 * CB, 1)
            total = v if total is None else jnp.where(lane == j, v, total)
        k = p * 128
        lh[:, k : k + 128], ll[:, k : k + 128] = split(total)


def update_kernel(*refs):
    his, los, (xh, xl, r_ref, _base, out) = refs[:4], refs[4:8], refs[8:]
    a = [jnp.concatenate([v[...] for v in part], axis=1) for part in (his, los)]
    for w in COLS:
        out[:, w] = r_ref[:, w] - dot3(a, (xh[:, w], xl[:, w]))


VM = pl.BlockSpec(memory_space=pltpu.VMEM)
SM = pl.BlockSpec(memory_space=pltpu.SMEM)
ANY = pl.BlockSpec(memory_space=pl.ANY)
SUB = PANELS * 128
DEPTH = PANELS * PANEL


def params(limit):
    return pltpu.CompilerParams(vmem_limit_bytes=limit * MIB)


def cost(flops, moved):
    return pl.CostEstimate(flops=int(flops), bytes_accessed=int(moved), transcendentals=0)


def assemble(*blocks):
    out = jax.ShapeDtypeStruct((GROUPS, GR, SUB), BF16)
    spec = pl.BlockSpec((None, GR, SUB), lambda g: (g, 0, 0))
    return pl.pallas_call(
        assemble_kernel,
        grid=(GROUPS,),
        out_shape=(out, out),
        in_specs=[pl.BlockSpec(v.shape, lambda g: (0, 0, 0)) for v in blocks],
        out_specs=(spec, spec),
        compiler_params=params(20),
        cost_estimate=cost(4e6, 7e6),
    )(*blocks)


def update(rows_in, base, parts, xh, xl):
    strip = pl.BlockSpec(
        (pl.Element(GR), pl.Element(NCOL)), lambda g: (pl.multiple_of(WIN + g * GR, 16), 0)
    )
    spec = pl.BlockSpec((None, GR, SUB), lambda g: (g, 0, 0))
    whole = pl.BlockSpec((DEPTH, NCOL), lambda g: (0, 0))
    return pl.pallas_call(
        update_kernel,
        grid=(GROUPS,),
        out_shape=jax.ShapeDtypeStruct((ROWS, NCOL), F32),
        in_specs=[spec] * 8 + [whole, whole, strip, ANY],
        out_specs=strip,
        input_output_aliases={11: 0},
        compiler_params=params(48),
        cost_estimate=cost(6 * TRAIL * DEPTH * NCOL, 30e6),
    )(*[v[0] for v in parts], *[v[1] for v in parts], xh, xl, rows_in, base)


def local(rhs_tile, factor):
    row_i, col_i = lax.axis_index("row"), lax.axis_index("col")
    pos = jnp.stack([row_i // 2, row_i % 2, col_i // NZ, col_i % NZ]).astype(jnp.int32)

    packed, w, b0 = pl.pallas_call(
        pack_kernel,
        out_shape=(
            jax.ShapeDtypeStruct((PANELS * GR, 128), F32),
            jax.ShapeDtypeStruct((2 * PB, 128), F32),
            jax.ShapeDtypeStruct((WIN, NCOL), F32),
        ),
        in_specs=[VM, ANY],
        out_specs=(VM, VM, VM),
        scratch_shapes=[pltpu.SemaphoreType.DMA],
        compiler_params=params(57),
    )(factor, rhs_tile)

    w1 = jnp.stack([w] + [from_first(w, d) for d in (1, 2, 3)])
    groups = [w1] + [from_second(w1, d) for d in (1, 2, 3)]

    mine = pl.pallas_call(
        rows_kernel,
        out_shape=jax.ShapeDtypeStruct((SLOTS, PB, PANEL), F32),
        in_specs=[SM] + [VM] * 4,
        out_specs=VM,
        scratch_shapes=[
            pltpu.VMEM((16, 2 * PB, 128), F32),
            pltpu.VMEM((PANELS, NX, PB, 128), F32),
        ],
        compiler_params=params(8),
    )(pos, *groups)

    b1, b3 = from_y(b0, 1), from_y(b0, 3)
    hb = WIN // 2
    b2 = jnp.concatenate([from_y(b1[:hb], 1), from_y(b3[hb:], 3)])
    bchip = jnp.stack([b0, b1, b2, b3]).reshape(NY, PANELS, PB, NCOL)
    bother = from_core(bchip)

    u1, u3 = from_first(packed, 1), from_first(packed, 3)
    h = PANELS * GR // 2
    u2 = jnp.concatenate([from_first(u1[:h], 1), from_first(u3[h:], 3)])
    q0 = jnp.stack([packed, u1, u2, u3])
    q1, q3 = from_second(q0, 1), from_second(q0, 3)
    q2 = (from_second(q1[:2], 1), from_second(q3[2:], 3))

    m1, m3 = from_y(mine, 1), from_y(mine, 3)
    m1, m3, _ = lax.optimization_barrier((m1, m3, q0[0, 0, 0]))
    hs = SLOTS // 2
    m2 = jnp.concatenate([from_y(m1[:hs], 1), from_y(m3[hs:], 3)])
    chip = jnp.stack([mine, m1, m2, m3])
    other = from_core(chip)

    parts = [assemble(q0), assemble(q1), assemble(q3)]
    pos_late, _, _ = lax.optimization_barrier((pos, q1[0, 0, 0], q3[0, 0, 0]))
    xh, xl, base = pl.pallas_call(
        solve_kernel,
        out_shape=(
            jax.ShapeDtypeStruct((DEPTH, NCOL), BF16),
            jax.ShapeDtypeStruct((DEPTH, NCOL), BF16),
            jax.ShapeDtypeStruct((ROWS, NCOL), F32),
        ),
        in_specs=[SM, ANY, ANY, ANY, ANY],
        out_specs=(VM, VM, ANY),
        scratch_shapes=[
            pltpu.VMEM((SLOTS, PANEL, PANEL), F32),
            pltpu.VMEM((PANELS, PANEL, NCOL), F32),
        ]
        + [pltpu.VMEM((PANELS, PANEL, PANEL), BF16)] * 4
        + [pltpu.VMEM((PANELS, PANEL, NCOL), BF16)] * 2
        + [pltpu.VMEM((DEPTH, NCOL), BF16)] * 2
        + [
            pltpu.VMEM((PANEL, NCOL), F32),
            pltpu.VMEM((WIN, NCOL), F32),
            pltpu.SemaphoreType.DMA((2, 2 * NY)),
            pltpu.SemaphoreType.DMA,
        ],
        compiler_params=params(48),
        cost_estimate=cost(36 * PANEL * PANEL * NCOL, 20e6),
    )(pos_late, chip, other, bchip, bother)

    return update(rhs_tile, base, parts + [assemble(*q2)], xh, xl)


def solution(mesh):
    spec = P("row", "col")
    return jax.shard_map(
        local, mesh=mesh, in_specs=(spec, spec), out_specs=spec, check_vma=False
    )
```

profile of v0, /device:TPU:0, one launch (start us, length us, event | category | flops | bytes accessed | tf_op | source)
XLA Modules:
  0.0 200.4 jit_solution(4799959792791145895)
XLA Ops:
  0.0 2.6 %copy.4.f_ref = f32[2304,96]{1,0:T(8,128)} copy(f32[2304,96]{0,1:T(8,128)} %param.3) | data formatting | bytes 1769472 | tf_op args[1]
  2.6 3.7 %shard_map.28 = (f32[1584,128]{1,0:T(8,128)}, f32[128,128]{1,0:T(8,128)}, f32[192,1152]{1,0:T(8,128)}) custom-call(f32[2304,96]{1,0:T(8,128)} %copy.4.f_ref, f32[2304,1152]{1,0:T(8,128)} %refs_10_.1), custom_call_target="tpu_custom_call" | custom-call | tf_op jit(solution)/shard_map/pallas_call | solution.py:301
  6.2 2.9 %collective-permute-start = (f32[1584,128]{1,0:T(8,128)}, f32[1584,128]{1,0:T(8,128)S(1)}, u32[]{:S(2)}, u32[]{:S(2)}) collective-permute-start(f32[1584,128]{1,0:T(8,128)} %get-tuple-element.21), channel_id=1, source_target_pairs={{0,12},{1,13},{2,14},{3,15},{4,0},{5,1},{6,2},{7,3},{8,4},{9,5},{1... | collective-permute-start | bytes 2433032 | tf_op jit(solution)/shard_map/ppermute | solution.py:34
  9.1 0.8 collective-permute-start.9
  9.9 0.9 collective-permute-start.10
  10.8 2.4 %collective-permute-start.8 = (f32[128,128]{1,0:T(8,128)}, f32[128,128]{1,0:T(8,128)S(1)}, u32[]{:S(2)}, u32[]{:S(2)}) collective-permute-start(f32[128,128]{1,0:T(8,128)} %get-tuple-element.30), channel_id=1, source_target_pairs={{0,12},{1,13},{2,14},{3,15},{4,0},{5,1},{6,2},{7,3},{8,4},{9,5},{1... | collective-permute-start | bytes 196616 | tf_op jit(solution)/shard_map/ppermute | solution.py:34
  13.2 2.0 collective-permute-done.9
  15.1 0.7 collective-permute-done.10
  15.8 4.8 %collective-permute-done.8 = f32[128,128]{1,0:T(8,128)S(1)} collective-permute-done((f32[128,128]{1,0:T(8,128)}, f32[128,128]{1,0:T(8,128)S(1)}, u32[]{:S(2)}, u32[]{:S(2)}) %collective-permute-start.8) | collective-permute-done | bytes 65568 | tf_op jit(solution)/shard_map/ppermute | solution.py:34
  20.6 0.9 pad_maximum_fusion.4.g0
  21.5 4.1 %collective-permute-start.11 = (f32[4,128,128]{2,1,0:T(8,128)S(1)}, f32[4,128,128]{2,1,0:T(8,128)S(1)}, u32[]{:S(2)}, u32[]{:S(2)}) collective-permute-start(f32[4,128,128]{2,1,0:T(8,128)S(1)} %pad_maximum_fusion.4.g0), channel_id=1, source_target_pairs={{0,3},{1,0},{2,1},{3,2},{4,7},{5,4},{6,5},{7,6},{8,11},{9,8},{10,9... | collective-permute-start | bytes 786440 | tf_op jit(solution)/shard_map/ppermute | solution.py:34
  25.6 3.0 %collective-permute-start.19 = (f32[192,1152]{1,0:T(8,128)}, f32[192,1152]{1,0:T(8,128)S(1)}, u32[]{:S(2)}, u32[]{:S(2)}) collective-permute-start(f32[192,1152]{1,0:T(8,128)} %get-tuple-element.33), channel_id=1, source_target_pairs={{0,96},{1,97},{2,98},{3,99},{4,100},{5,101},{6,102},{7,103},{8,104... | collective-permute-start | bytes 2654216 | tf_op jit(solution)/shard_map/ppermute | solution.py:34
  28.6 1.3 collective-permute-start.2
  30.0 1.3 collective-permute-start.13
  31.2 9.5 %collective-permute-done.12.g2 = f32[4,128,128]{2,1,0:T(8,128)S(1)} collective-permute-done((f32[4,128,128]{2,1,0:T(8,128)S(1)}, f32[4,128,128]{2,1,0:T(8,128)S(1)}, u32[]{:S(2)}, u32[]{:S(2)}) %collective-permute-start.12) | collective-permute-done | bytes 262176 | tf_op jit(solution)/shard_map/ppermute | solution.py:34
  40.8 2.4 %collective-permute-done.13.g3 = f32[4,128,128]{2,1,0:T(8,128)S(1)} collective-permute-done((f32[4,128,128]{2,1,0:T(8,128)S(1)}, f32[4,128,128]{2,1,0:T(8,128)S(1)}, u32[]{:S(2)}, u32[]{:S(2)}) %collective-permute-start.13) | collective-permute-done | bytes 262176 | tf_op jit(solution)/shard_map/ppermute | solution.py:34
  43.2 2.8 %shard_map.33 = f32[6,64,512]{2,1,0:T(8,128)S(1)} custom-call(s32[4]{0:T(128)S(1)} %pad_add_fusion.pos, f32[4,128,128]{2,1,0:T(8,128)S(1)} %pad_maximum_fusion.4.g0, f32[4,128,128]{2,1,0:T(8,128)S(1)} %collective-permute-done.11.g1, f32[4,128,128]{2,1,0:T(8,128)S(1)} %collective-permute-done.12.g2, f32[4,128,128]{2,1,0:T(8,128)S(1)} %collective-permute-done.13.g3), custom_call_target="tpu_custom_call" | custom-call | tf_op jit(solution)/shard_map/pallas_call | solution.py:317
  46.0 2.1 %collective-permute-start.14 = (f32[6,64,512]{2,1,0:T(8,128)S(1)}, f32[6,64,512]{2,1,0:T(8,128)S(1)}, u32[]{:S(2)}, u32[]{:S(2)}) collective-permute-start(f32[6,64,512]{2,1,0:T(8,128)S(1)} %shard_map.33), channel_id=1, source_target_pairs={{0,96},{1,97},{2,98},{3,99},{4,100},{5,101},{6,102},{7,103},{8,104... | collective-permute-start | bytes 2359304 | tf_op jit(solution)/shard_map/ppermute | solution.py:34
  48.2 3.1 %collective-permute-start.1 = (f32[792,128]{1,0:T(8,128)S(1)}, f32[792,128]{1,0:T(8,128)S(1)}, u32[]{:S(2)}, u32[]{:S(2)}) collective-permute-start(f32[792,128]{1,0:T(8,128)S(1)} %slice.35), channel_id=1, source_target_pairs={{0,12},{1,13},{2,14},{3,15},{4,0},{5,1},{6,2},{7,3},{8,4},{9,5},{1... | collective-permute-start | bytes 1216520 | tf_op jit(solution)/shard_map/ppermute | solution.py:34
  51.5 13.2 %collective-permute-done.21 = f32[192,1152]{1,0:T(8,128)S(1)} collective-permute-done((f32[192,1152]{1,0:T(8,128)}, f32[192,1152]{1,0:T(8,128)S(1)}, u32[]{:S(2)}, u32[]{:S(2)}) %collective-permute-start.21) | collective-permute-done | bytes 884768 | tf_op jit(solution)/shard_map/ppermute | solution.py:34
  64.7 1.8 collective-permute-done.14
  66.6 1.8 collective-permute-start.22
  68.4 13.2 %collective-permute-done.15 = f32[6,64,512]{2,1,0:T(8,128)S(1)} collective-permute-done((f32[6,64,512]{2,1,0:T(8,128)S(1)}, f32[6,64,512]{2,1,0:T(8,128)S(1)}, u32[]{:S(2)}, u32[]{:S(2)}) %collective-permute-start.15) | collective-permute-done | bytes 786464 | tf_op jit(solution)/shard_map/ppermute | solution.py:34
  81.7 2.1 %collective-permute-start.17 = (f32[3,64,512]{2,1,0:T(8,128)S(1)}, f32[3,64,512]{2,1,0:T(8,128)S(1)}, u32[]{:S(2)}, u32[]{:S(2)}) collective-permute-start(f32[3,64,512]{2,1,0:T(8,128)S(1)} %slice.32), channel_id=1, source_target_pairs={{0,32},{1,33},{2,34},{3,35},{4,36},{5,37},{6,38},{7,39},{8,40},{9,... | collective-permute-start | bytes 1179656 | tf_op jit(solution)/shard_map/ppermute | solution.py:34
  83.9 0.4 pad_maximum_fusion.1.refs_0_
  84.3 2.0 %collective-permute-start.5 = (f32[4,1584,128]{2,1,0:T(8,128)S(1)}, f32[4,1584,128]{2,1,0:T(8,128)S(1)}, u32[]{:S(2)}, u32[]{:S(2)}) collective-permute-start(f32[4,1584,128]{2,1,0:T(8,128)S(1)} %pad_maximum_fusion.1.refs_0_), channel_id=1, source_target_pairs={{0,1},{1,2},{2,3},{3,0},{4,5},{5,6},{6,7},{7,4},{8,9},{9,10},{10,1... | collective-permute-start | bytes 9732104 | tf_op jit(solution)/shard_map/ppermute | solution.py:34
  86.3 1.7 collective-permute-done.22
  88.1 0.3 pad_maximum_fusion.bmine
  88.4 0.1 collective-permute-start.23
  88.5 0.9 collective-permute-done.16
  89.4 2.8 %collective-permute-done.17 = f32[3,64,512]{2,1,0:T(8,128)S(1)} collective-permute-done((f32[3,64,512]{2,1,0:T(8,128)S(1)}, f32[3,64,512]{2,1,0:T(8,128)S(1)}, u32[]{:S(2)}, u32[]{:S(2)}) %collective-permute-start.17) | collective-permute-done | bytes 393248 | tf_op jit(solution)/shard_map/ppermute | solution.py:34
  92.3 0.4 pad_maximum_fusion.2.mine
  92.7 0.3 collective-permute-start.18
  93.0 29.7 %collective-permute-done.4.refs_0_ = f32[4,1584,128]{2,1,0:T(8,128)S(1)} collective-permute-done((f32[4,1584,128]{2,1,0:T(8,128)S(1)}, f32[4,1584,128]{2,1,0:T(8,128)S(1)}, u32[]{:S(2)}, u32[]{:S(2)}) %collective-permute-start.4) | collective-permute-done | bytes 3244064 | tf_op jit(solution)/shard_map/ppermute | solution.py:34
  122.6 0.1 slice.37
  122.7 1.3 collective-permute-start.6
  124.0 0.1 slice.38
  124.1 0.9 collective-permute-start.7
  125.0 3.8 %shard_map.29 = (bf16[4,528,384]{2,1,0:T(8,128)(2,1)S(1)}, bf16[4,528,384]{2,1,0:T(8,128)(2,1)S(1)}) custom-call(f32[4,1584,128]{2,1,0:T(8,128)S(1)} %pad_maximum_fusion.1.refs_0_), custom_call_target="tpu_custom_call" | custom-call | flops 4000000 | bytes 7000000 | tf_op jit(solution)/shard_map/pallas_call | solution.py:268
  128.8 3.8 %shard_map.30 = (bf16[4,528,384]{2,1,0:T(8,128)(2,1)S(1)}, bf16[4,528,384]{2,1,0:T(8,128)(2,1)S(1)}) custom-call(f32[4,1584,128]{2,1,0:T(8,128)S(1)} %collective-permute-done.4.refs_0_), custom_call_target="tpu_custom_call" | custom-call | flops 4000000 | bytes 7000000 | tf_op jit(solution)/shard_map/pallas_call | solution.py:268
  132.6 3.8 %shard_map.31 = (bf16[4,528,384]{2,1,0:T(8,128)(2,1)S(1)}, bf16[4,528,384]{2,1,0:T(8,128)(2,1)S(1)}) custom-call(f32[4,1584,128]{2,1,0:T(8,128)S(1)} %collective-permute-done.5.refs_0_), custom_call_target="tpu_custom_call" | custom-call | flops 4000000 | bytes 7000000 | tf_op jit(solution)/shard_map/pallas_call | solution.py:268
  136.4 1.2 copy-done.2
  137.6 1.6 copy-done.8
  139.3 22.7 %shard_map.34 = (bf16[1536,1152]{1,0:T(8,128)(2,1)}, bf16[1536,1152]{1,0:T(8,128)(2,1)}, f32[2304,1152]{1,0:T(8,128)}) custom-call(s32[4]{0:T(128)S(1)} %pad_add_fusion.pos, f32[4,6,64,512]{3,2,1,0:T(8,128)S(1)} %pad_maximum_fusion.2.mine, f32[4,6,64,512]{3,2,1,0:T(8,128)} %copy-done.8, f32[4,3,64,1152]{3,2,1,0:T(8,128)} %copy-done.5, ...), custom_call_target="tpu_custom_call" | custom-call | flops 10871635968 | bytes 20000000 | tf_op jit(solution)/shard_map/pallas_call | solution.py:351
  162.0 3.8 %shard_map.32 = (bf16[4,528,384]{2,1,0:T(8,128)(2,1)S(1)}, bf16[4,528,384]{2,1,0:T(8,128)(2,1)S(1)}) custom-call(f32[2,1584,128]{2,1,0:T(8,128)S(1)} %collective-permute-done.6.refs_0_, f32[2,1584,128]{2,1,0:T(8,128)S(1)} %collective-permute-done.7.refs_1_), custom_call_target="tpu_custom_call" | custom-call | flops 4000000 | bytes 7000000 | tf_op jit(solution)/shard_map/pallas_call | solution.py:268
  165.8 1.2 copy-done.3
  167.0 1.2 copy-done.4
  168.2 32.2 %shard_map.35 = f32[2304,1152]{1,0:T(8,128)} custom-call(bf16[4,528,384]{2,1,0:T(8,128)(2,1)S(1)} %get-tuple-element.22.refs_0_, bf16[4,528,384]{2,1,0:T(8,128)(2,1)S(1)} %get-tuple-element.23.refs_1_, bf16[4,528,384]{2,1,0:T(8,128)(2,1)S(1)} %get-tuple-element.24.refs_2_, bf16[4,528,384]{2,1,0:T(8,128)(2,1)} %copy-done.3, ...), custom_call_target="tpu_custom_call", output_to_operand_aliasing={{}: (11, {})} | custom-call | flops 22422749184 | bytes 30000000 | tf_op jit(solution)/shard_map/pallas_call | solution.py:285
  (43 shorter events, 0.7 us)
Async XLA Ops:
  6.2 42.0 %collective-permute-start = (f32[1584,128]{1,0:T(8,128)}, f32[1584,128]{1,0:T(8,128)S(1)}, u32[]{:S(2)}, u32[]{:S(2)}) collective-permute-start(f32[1584,128]{1,0:T(8,128)} %get-tuple-element.21), channel_id=1, source_target_pairs={{0,12},{1,13},{2,14},{3,15},{4,0},{5,1},{6,2},{7,3},{8,4},{9,5},{1... | collective-permute-start | bytes 2433032 | tf_op jit(solution)/shard_map/ppermute | solution.py:34
  9.1 6.0 %collective-permute-start.9 = (f32[128,128]{1,0:T(8,128)}, f32[128,128]{1,0:T(8,128)S(1)}, u32[]{:S(2)}, u32[]{:S(2)}) collective-permute-start(f32[128,128]{1,0:T(8,128)} %get-tuple-element.30), channel_id=1, source_target_pairs={{0,8},{1,9},{2,10},{3,11},{4,12},{5,13},{6,14},{7,15},{8,0},{9,1},... | collective-permute-start | bytes 196616 | tf_op jit(solution)/shard_map/ppermute | solution.py:34
  9.9 5.9 %collective-permute-start.10 = (f32[128,128]{1,0:T(8,128)}, f32[128,128]{1,0:T(8,128)S(1)}, u32[]{:S(2)}, u32[]{:S(2)}) collective-permute-start(f32[128,128]{1,0:T(8,128)} %get-tuple-element.30), channel_id=1, source_target_pairs={{0,4},{1,5},{2,6},{3,7},{4,8},{5,9},{6,10},{7,11},{8,12},{9,13},{1... | collective-permute-start | bytes 196616 | tf_op jit(solution)/shard_map/ppermute | solution.py:34
  10.8 9.8 %collective-permute-start.8 = (f32[128,128]{1,0:T(8,128)}, f32[128,128]{1,0:T(8,128)S(1)}, u32[]{:S(2)}, u32[]{:S(2)}) collective-permute-start(f32[128,128]{1,0:T(8,128)} %get-tuple-element.30), channel_id=1, source_target_pairs={{0,12},{1,13},{2,14},{3,15},{4,0},{5,1},{6,2},{7,3},{8,4},{9,5},{1... | collective-permute-start | bytes 196616 | tf_op jit(solution)/shard_map/ppermute | solution.py:34
  21.5 8.5 %collective-permute-start.11 = (f32[4,128,128]{2,1,0:T(8,128)S(1)}, f32[4,128,128]{2,1,0:T(8,128)S(1)}, u32[]{:S(2)}, u32[]{:S(2)}) collective-permute-start(f32[4,128,128]{2,1,0:T(8,128)S(1)} %pad_maximum_fusion.4.g0), channel_id=1, source_target_pairs={{0,3},{1,0},{2,1},{3,2},{4,7},{5,4},{6,5},{7,6},{8,11},{9,8},{10,9... | collective-permute-start | bytes 786440 | tf_op jit(solution)/shard_map/ppermute | solution.py:34
  25.6 25.8 %collective-permute-start.19 = (f32[192,1152]{1,0:T(8,128)}, f32[192,1152]{1,0:T(8,128)S(1)}, u32[]{:S(2)}, u32[]{:S(2)}) collective-permute-start(f32[192,1152]{1,0:T(8,128)} %get-tuple-element.33), channel_id=1, source_target_pairs={{0,96},{1,97},{2,98},{3,99},{4,100},{5,101},{6,102},{7,103},{8,104... | collective-permute-start | bytes 2654216 | tf_op jit(solution)/shard_map/ppermute | solution.py:34
  28.6 19.6 %collective-permute-start.2 = (f32[1584,128]{1,0:T(8,128)}, f32[1584,128]{1,0:T(8,128)S(1)}, u32[]{:S(2)}, u32[]{:S(2)}) collective-permute-start(f32[1584,128]{1,0:T(8,128)} %get-tuple-element.21), channel_id=1, source_target_pairs={{0,4},{1,5},{2,6},{3,7},{4,8},{5,9},{6,10},{7,11},{8,12},{9,13},{1... | collective-permute-start | bytes 2433032 | tf_op jit(solution)/shard_map/ppermute | solution.py:34
  30.0 10.8 %collective-permute-start.12 = (f32[4,128,128]{2,1,0:T(8,128)S(1)}, f32[4,128,128]{2,1,0:T(8,128)S(1)}, u32[]{:S(2)}, u32[]{:S(2)}) collective-permute-start(f32[4,128,128]{2,1,0:T(8,128)S(1)} %pad_maximum_fusion.4.g0), channel_id=1, source_target_pairs={{0,2},{1,3},{2,0},{3,1},{4,6},{5,7},{6,4},{7,5},{8,10},{9,11},{10,... | collective-permute-start | bytes 786440 | tf_op jit(solution)/shard_map/ppermute | solution.py:34
  30.0 13.3 %collective-permute-start.13 = (f32[4,128,128]{2,1,0:T(8,128)S(1)}, f32[4,128,128]{2,1,0:T(8,128)S(1)}, u32[]{:S(2)}, u32[]{:S(2)}) collective-permute-start(f32[4,128,128]{2,1,0:T(8,128)S(1)} %pad_maximum_fusion.4.g0), channel_id=1, source_target_pairs={{0,1},{1,2},{2,3},{3,0},{4,5},{5,6},{6,7},{7,4},{8,9},{9,10},{10,1... | collective-permute-start | bytes 786440 | tf_op jit(solution)/shard_map/ppermute | solution.py:34
  40.7 24.0 %collective-permute-start.21 = (f32[192,1152]{1,0:T(8,128)}, f32[192,1152]{1,0:T(8,128)S(1)}, u32[]{:S(2)}, u32[]{:S(2)}) collective-permute-start(f32[192,1152]{1,0:T(8,128)} %get-tuple-element.33), channel_id=1, source_target_pairs={{0,32},{1,33},{2,34},{3,35},{4,36},{5,37},{6,38},{7,39},{8,40},{9,... | collective-permute-start | bytes 2654216 | tf_op jit(solution)/shard_map/ppermute | solution.py:34
  46.0 37.8 %copy-start.7 = (f32[1584,128]{1,0:T(8,128)S(1)}, f32[1584,128]{1,0:T(8,128)}, u32[]{:S(2)}) copy-start(f32[1584,128]{1,0:T(8,128)} %get-tuple-element.21) | copy-start | bytes 2433028
  46.0 20.5 %collective-permute-start.14 = (f32[6,64,512]{2,1,0:T(8,128)S(1)}, f32[6,64,512]{2,1,0:T(8,128)S(1)}, u32[]{:S(2)}, u32[]{:S(2)}) collective-permute-start(f32[6,64,512]{2,1,0:T(8,128)S(1)} %shard_map.33), channel_id=1, source_target_pairs={{0,96},{1,97},{2,98},{3,99},{4,100},{5,101},{6,102},{7,103},{8,104... | collective-permute-start | bytes 2359304 | tf_op jit(solution)/shard_map/ppermute | solution.py:34
  48.2 33.4 %collective-permute-start.15 = (f32[6,64,512]{2,1,0:T(8,128)S(1)}, f32[6,64,512]{2,1,0:T(8,128)S(1)}, u32[]{:S(2)}, u32[]{:S(2)}) collective-permute-start(f32[6,64,512]{2,1,0:T(8,128)S(1)} %shard_map.33), channel_id=1, source_target_pairs={{0,32},{1,33},{2,34},{3,35},{4,36},{5,37},{6,38},{7,39},{8,40},{9,... | collective-permute-start | bytes 2359304 | tf_op jit(solution)/shard_map/ppermute | solution.py:34
  48.2 33.5 %collective-permute-start.1 = (f32[792,128]{1,0:T(8,128)S(1)}, f32[792,128]{1,0:T(8,128)S(1)}, u32[]{:S(2)}, u32[]{:S(2)}) collective-permute-start(f32[792,128]{1,0:T(8,128)S(1)} %slice.35), channel_id=1, source_target_pairs={{0,12},{1,13},{2,14},{3,15},{4,0},{5,1},{6,2},{7,3},{8,4},{9,5},{1... | collective-permute-start | bytes 1216520 | tf_op jit(solution)/shard_map/ppermute | solution.py:34
  51.4 32.4 %collective-permute-start.3 = (f32[792,128]{1,0:T(8,128)S(1)}, f32[792,128]{1,0:T(8,128)S(1)}, u32[]{:S(2)}, u32[]{:S(2)}) collective-permute-start(f32[792,128]{1,0:T(8,128)S(1)} %slice.36), channel_id=1, source_target_pairs={{0,4},{1,5},{2,6},{3,7},{4,8},{5,9},{6,10},{7,11},{8,12},{9,13},{1... | collective-permute-start | bytes 1216520 | tf_op jit(solution)/shard_map/ppermute | solution.py:34
  64.7 19.6 %collective-permute-start.20 = (f32[96,1152]{1,0:T(8,128)S(1)}, f32[96,1152]{1,0:T(8,128)S(1)}, u32[]{:S(2)}, u32[]{:S(2)}) collective-permute-start(f32[96,1152]{1,0:T(8,128)S(1)} %slice.39), channel_id=1, source_target_pairs={{0,96},{1,97},{2,98},{3,99},{4,100},{5,101},{6,102},{7,103},{8,104... | collective-permute-start | bytes 1327112 | tf_op jit(solution)/shard_map/ppermute | solution.py:34
  66.6 21.4 %collective-permute-start.22 = (f32[96,1152]{1,0:T(8,128)S(1)}, f32[96,1152]{1,0:T(8,128)S(1)}, u32[]{:S(2)}, u32[]{:S(2)}) collective-permute-start(f32[96,1152]{1,0:T(8,128)S(1)} %slice.40), channel_id=1, source_target_pairs={{0,32},{1,33},{2,34},{3,35},{4,36},{5,37},{6,38},{7,39},{8,40},{9,... | collective-permute-start | bytes 1327112 | tf_op jit(solution)/shard_map/ppermute | solution.py:34
  81.6 7.8 %collective-permute-start.16 = (f32[3,64,512]{2,1,0:T(8,128)S(1)}, f32[3,64,512]{2,1,0:T(8,128)S(1)}, u32[]{:S(2)}, u32[]{:S(2)}) collective-permute-start(f32[3,64,512]{2,1,0:T(8,128)S(1)} %slice.31), channel_id=1, source_target_pairs={{0,96},{1,97},{2,98},{3,99},{4,100},{5,101},{6,102},{7,103},{8,104... | collective-permute-start | bytes 1179656 | tf_op jit(solution)/shard_map/ppermute | solution.py:34
  81.7 10.5 %collective-permute-start.17 = (f32[3,64,512]{2,1,0:T(8,128)S(1)}, f32[3,64,512]{2,1,0:T(8,128)S(1)}, u32[]{:S(2)}, u32[]{:S(2)}) collective-permute-start(f32[3,64,512]{2,1,0:T(8,128)S(1)} %slice.32), channel_id=1, source_target_pairs={{0,32},{1,33},{2,34},{3,35},{4,36},{5,37},{6,38},{7,39},{8,40},{9,... | collective-permute-start | bytes 1179656 | tf_op jit(solution)/shard_map/ppermute | solution.py:34
  83.9 4.2 %copy-start.6 = (f32[192,1152]{1,0:T(8,128)S(1)}, f32[192,1152]{1,0:T(8,128)}, u32[]{:S(2)}) copy-start(f32[192,1152]{1,0:T(8,128)} %get-tuple-element.33) | copy-start | bytes 2654212
  84.2 38.4 %collective-permute-start.4 = (f32[4,1584,128]{2,1,0:T(8,128)S(1)}, f32[4,1584,128]{2,1,0:T(8,128)S(1)}, u32[]{:S(2)}, u32[]{:S(2)}) collective-permute-start(f32[4,1584,128]{2,1,0:T(8,128)S(1)} %pad_maximum_fusion.1.refs_0_), channel_id=1, source_target_pairs={{0,3},{1,0},{2,1},{3,2},{4,7},{5,4},{6,5},{7,6},{8,11},{9,8},{10,9... | collective-permute-start | bytes 9732104 | tf_op jit(solution)/shard_map/ppermute | solution.py:34
  84.3 39.7 %collective-permute-start.5 = (f32[4,1584,128]{2,1,0:T(8,128)S(1)}, f32[4,1584,128]{2,1,0:T(8,128)S(1)}, u32[]{:S(2)}, u32[]{:S(2)}) collective-permute-start(f32[4,1584,128]{2,1,0:T(8,128)S(1)} %pad_maximum_fusion.1.refs_0_), channel_id=1, source_target_pairs={{0,1},{1,2},{2,3},{3,0},{4,5},{5,6},{6,7},{7,4},{8,9},{9,10},{10,1... | collective-permute-start | bytes 9732104 | tf_op jit(solution)/shard_map/ppermute | solution.py:34
  88.4 4.3 %copy-start.5 = (f32[4,3,64,1152]{3,2,1,0:T(8,128)}, f32[4,3,64,1152]{3,2,1,0:T(8,128)S(1)}, u32[]{:S(2)}) copy-start(f32[4,3,64,1152]{3,2,1,0:T(8,128)S(1)} %pad_maximum_fusion.bmine) | copy-start | bytes 10616836
  88.4 50.9 %collective-permute-start.23 = (f32[4,3,64,1152]{3,2,1,0:T(8,128)S(1)}, f32[4,3,64,1152]{3,2,1,0:T(8,128)}, u32[]{:S(2)}, u32[]{:S(2)}) collective-permute-start(f32[4,3,64,1152]{3,2,1,0:T(8,128)S(1)} %pad_maximum_fusion.bmine), channel_id=1, source_target_pairs={{0,16},{1,17},{2,18},{3,19},{4,20},{5,21},{6,22},{7,23},{8,24},{9,... | collective-permute-start | bytes 10616840 | tf_op jit(solution)/shard_map/ppermute | solution.py:34
  92.7 44.9 %collective-permute-start.18 = (f32[4,6,64,512]{3,2,1,0:T(8,128)S(1)}, f32[4,6,64,512]{3,2,1,0:T(8,128)S(1)}, u32[]{:S(2)}, u32[]{:S(2)}) collective-permute-start(f32[4,6,64,512]{3,2,1,0:T(8,128)S(1)} %pad_maximum_fusion.2.mine), channel_id=1, source_target_pairs={{0,16},{1,17},{2,18},{3,19},{4,20},{5,21},{6,22},{7,23},{8,24},{9,... | collective-permute-start | bytes 9437192 | tf_op jit(solution)/shard_map/ppermute | solution.py:34
  122.7 39.2 %collective-permute-start.6 = (f32[2,1584,128]{2,1,0:T(8,128)S(1)}, f32[2,1584,128]{2,1,0:T(8,128)S(1)}, u32[]{:S(2)}, u32[]{:S(2)}) collective-permute-start(f32[2,1584,128]{2,1,0:T(8,128)S(1)} %slice.37), channel_id=1, source_target_pairs={{0,3},{1,0},{2,1},{3,2},{4,7},{5,4},{6,5},{7,6},{8,11},{9,8},{10,9... | collective-permute-start | bytes 4866056 | tf_op jit(solution)/shard_map/ppermute | solution.py:34
  124.1 37.8 %collective-permute-start.7 = (f32[2,1584,128]{2,1,0:T(8,128)S(1)}, f32[2,1584,128]{2,1,0:T(8,128)S(1)}, u32[]{:S(2)}, u32[]{:S(2)}) collective-permute-start(f32[2,1584,128]{2,1,0:T(8,128)S(1)} %slice.38), channel_id=1, source_target_pairs={{0,1},{1,2},{2,3},{3,0},{4,5},{5,6},{6,7},{7,4},{8,9},{9,10},{10,1... | collective-permute-start | bytes 4866056 | tf_op jit(solution)/shard_map/ppermute | solution.py:34
  128.8 7.6 %copy-start = (bf16[4,528,384]{2,1,0:T(8,128)(2,1)}, bf16[4,528,384]{2,1,0:T(8,128)(2,1)S(1)}, u32[]{:S(2)}) copy-start(bf16[4,528,384]{2,1,0:T(8,128)(2,1)S(1)} %get-tuple-element.26.refs_4_) | copy-start | bytes 4866052
  132.6 5.0 %copy-start.1 = (bf16[4,528,384]{2,1,0:T(8,128)(2,1)}, bf16[4,528,384]{2,1,0:T(8,128)(2,1)S(1)}, u32[]{:S(2)}) copy-start(bf16[4,528,384]{2,1,0:T(8,128)(2,1)S(1)} %get-tuple-element.27.refs_5_) | copy-start | bytes 4866052
  136.4 1.2 copy-start.2
  137.6 1.6 copy-start.8
  165.8 1.2 copy-start.3
  167.0 1.2 copy-start.4
where the time goes:
time: 201 us; the launch traced here: 200 us
  waiting for transfers between devices  82.7 us (41%)
  Pallas kernels  76.5 us (38%)
  starting transfers between devices  30.5 us (15%)
  local copies, waits for them, and re-layouts  8.19 us (4%)
  other arithmetic  2.16 us (1%)
    ppermute x24, waiting for transfers between devices, joint(): return lax.ppermute(v, ('row', 'col'), pairs)  82.7 us
    pallas_call x1, Pallas kernels, update(): pl.pallas_call(update_kernel, grid=(GROUPS,), out_shape=jax.ShapeDtypeStr...  32.2 us
    ppermute x24, starting transfers between devices, joint(): return lax.ppermute(v, ('row', 'col'), pairs)  30.5 us
    pallas_call x1, Pallas kernels, local(): pl.pallas_call(solve_kernel, out_shape=(jax.ShapeDtypeStruct((DEPTH, NCOL...  22.7 us
    pallas_call x4, Pallas kernels, assemble(): pl.pallas_call(assemble_kernel, grid=(GROUPS,), out_shape=(out, out), in_...  15.1 us
    unnamed x19, local copies, waits for them, and re-layouts  7.81 us
  transfers between devices with their start and end apart: 24, of which 12 were waited for; matrix products, arithmetic and copies ran while one was open for 1% of the time, Pallas kernels for 18%

commit v1 on v0

--- a/solution.py
+++ b/solution.py
@@ -14,6 +14,7 @@
 GROUPS = 4
 GR = TRAIL // GROUPS
 SLOTS = 6
+WR = 2 * PB
 MIB = 1024 * 1024
 GROUP_ORDER = (0, 1, 3, 2)
 
@@ -42,19 +43,17 @@
     return joint(v, lambda y, c, x, z: (y, c, x, z - d) if c == 0 else (y, c, x - d, z))
 
 
-def from_y(v, d):
-    return joint(v, lambda y, c, x, z: (y - d, c, x, z))
+def along_y(v):
+    return joint(v, lambda y, c, x, z: (y - 1 if c == 0 else y + 1, c, x, z))
 
 
 def from_core(v):
     return joint(v, lambda y, c, x, z: (y, 1 - c, x, z))
 
 
-def pack_kernel(f_ref, r_ref, l_ref, w_ref, b_ref, sem):
-    copy = pltpu.make_async_copy(r_ref.at[0:WIN, :], b_ref, sem)
-    copy.start()
-    for p in range(PANELS):
-        l_ref[p * GR : (p + 1) * GR, :] = jnp.concatenate(
+def pack_kernel(f_ref, l_ref):
+    for p in range(PANELS):
+        l_ref[WR + p * GR : WR + (p + 1) * GR, :] = jnp.concatenate(
             [
                 f_ref[WIN + g * GR : WIN + (g + 1) * GR, p * CB : (p + 1) * CB]
                 for g in range(GROUPS)
@@ -65,10 +64,9 @@
     def block(i, j):
         return f_ref[i * PB : (i + 1) * PB, j * CB : (j + 1) * CB]
 
-    w_ref[0:PB, :] = jnp.concatenate([block(0, 0), block(1, 1), block(2, 2), block(1, 0)], axis=1)
+    l_ref[0:PB, :] = jnp.concatenate([block(0, 0), block(1, 1), block(2, 2), block(1, 0)], axis=1)
     zero = jnp.zeros((PB, CB), F32)
-    w_ref[PB : 2 * PB, :] = jnp.concatenate([block(2, 0), block(2, 1), zero, zero], axis=1)
-    copy.wait()
+    l_ref[PB:WR, :] = jnp.concatenate([block(2, 0), block(2, 1), zero, zero], axis=1)
 
 
 def source(pos, i, j):
@@ -78,7 +76,7 @@
     return xs * NZ + zs
 
 
-def rows_kernel(pos, g0, g1, g2, g3, out, canon, diag):
+def rows_kernel(pos, g0, g1, g2, g3, _after, out, canon, diag):
     y, core = pos[0], pos[1]
     for i, ref in enumerate((g0, g1, g2, g3)):
         for j in range(4):
@@ -144,25 +142,31 @@
 
 
 def solve_kernel(
-    pos, mine, other, bmine, bother, xh, xl, base, mat, b_ref, lh, ll, oh, ol, rh, rl, ah, al, xs, own, sem, last
+    pos, m0, mc, mown, mgot, b0, bc, bown, bgot, xh, xl, base, mat, b_ref, lh, ll, oh, ol, rh, rl, ah, al, xs, own, sem, last
 ):
     y, core = pos[0], pos[1]
 
-    def copies(to, sources, sems):
+    near, far = 1 + 2 * core, 3 - 2 * core
+
+    def copies(to, own_rows, pair_rows, own3, got3, sems):
         made = []
-        for which, src in enumerate(sources):
-            c = core if which == 0 else 1 - core
-            for d in range(NY):
-                r = pl.multiple_of((y + d) % NY * 128 + c * PB, PB)
-                made.append(
-                    pltpu.make_async_copy(
-                        src.at[d], to.at[:, pl.ds(r, PB), :], sems.at[which * NY + d]
-                    )
-                )
+        plan = (
+            (own_rows, 0, core),
+            (pair_rows, 0, 1 - core),
+            (own3.at[0], near, core),
+            (own3.at[1], near, 1 - core),
+            (own3.at[2], 2, core),
+            (got3.at[0], far, 1 - core),
+            (got3.at[1], far, core),
+            (got3.at[2], 2, 1 - core),
+        )
+        for k, (src, d, c) in enumerate(plan):
+            r = pl.multiple_of((y + d) % NY * 128 + c * PB, PB)
+            made.append(pltpu.make_async_copy(src, to.at[:, pl.ds(r, PB), :], sems.at[k]))
         return made
 
-    mat_copies = copies(mat, (mine, other), sem.at[0])
-    b_copies = copies(b_ref, (bmine, bother), sem.at[1])
+    mat_copies = copies(mat, m0, mc, mown, mgot, sem.at[0])
+    b_copies = copies(b_ref, b0, bc, bown, bgot, sem.at[1])
     for copy in mat_copies + b_copies:
         copy.start()
     for copy in mat_copies:
@@ -203,12 +207,12 @@
             if p:
                 o = [jnp.concatenate([v[k] for k in left[p]], axis=1) for v in (oh, ol)]
                 rhs = rhs - dot3(o, [v[: p * PANEL, w] for v in (ah, al)])
-            rh[p, :, w], rl[p, :, w] = split(rhs)
+            rh[:, w], rl[:, w] = split(rhs)
         for w in COLS:
             for top, depth in ((0, half), (half, PANEL)):
                 x = dot3(
                     [v[p, top : top + half, :depth] for v in (lh, ll)],
-                    [v[p, :depth, w] for v in (rh, rl)],
+                    [v[:depth, w] for v in (rh, rl)],
                 )
                 part = slice(p * PANEL + top, p * PANEL + top + half)
                 xs[top : top + half, w] = x
@@ -226,8 +230,7 @@
     copy.wait()
 
 
-def assemble_kernel(*refs):
-    lrefs, (lh, ll) = refs[:-2], refs[-2:]
+def lanes_in_order(lrefs, lh, ll):
     g = pl.program_id(0)
     lane = lax.broadcasted_iota(jnp.int32, (GR, 128), 1) // CB
     blocks = [(ref, b) for ref in lrefs for b in range(ref.shape[0])]
@@ -240,9 +243,17 @@
         lh[:, k : k + 128], ll[:, k : k + 128] = split(total)
 
 
+def assemble_kernel(*refs):
+    lanes_in_order(refs[:-2], *refs[-2:])
+
+
 def update_kernel(*refs):
-    his, los, (xh, xl, r_ref, _base, out) = refs[:4], refs[4:8], refs[8:]
-    a = [jnp.concatenate([v[...] for v in part], axis=1) for part in (his, los)]
+    his, los, (qa, qb, xh, xl, r_ref, _base, out, lh, ll) = refs[:3], refs[3:6], refs[6:]
+    lanes_in_order((qa, qb), lh, ll)
+    a = [
+        jnp.concatenate([v[...] for v in (*part, last)], axis=1)
+        for part, last in ((his, lh), (los, ll))
+    ]
     for w in COLS:
         out[:, w] = r_ref[:, w] - dot3(a, (xh[:, w], xl[:, w]))
 
@@ -276,78 +287,123 @@
     )(*blocks)
 
 
-def update(rows_in, base, parts, xh, xl):
+def update(rows_in, base, parts, last, xh, xl):
     strip = pl.BlockSpec(
         (pl.Element(GR), pl.Element(NCOL)), lambda g: (pl.multiple_of(WIN + g * GR, 16), 0)
     )
     spec = pl.BlockSpec((None, GR, SUB), lambda g: (g, 0, 0))
-    whole = pl.BlockSpec((DEPTH, NCOL), lambda g: (0, 0))
     return pl.pallas_call(
         update_kernel,
         grid=(GROUPS,),
         out_shape=jax.ShapeDtypeStruct((ROWS, NCOL), F32),
-        in_specs=[spec] * 8 + [whole, whole, strip, ANY],
+        in_specs=[spec] * 6 + [VM] * 4 + [strip, ANY],
         out_specs=strip,
+        scratch_shapes=[pltpu.VMEM((GR, SUB), BF16)] * 2,
         input_output_aliases={11: 0},
-        compiler_params=params(48),
+        compiler_params=params(57),
         cost_estimate=cost(6 * TRAIL * DEPTH * NCOL, 30e6),
-    )(*[v[0] for v in parts], *[v[1] for v in parts], xh, xl, rows_in, base)
+    )(*[v[0] for v in parts], *[v[1] for v in parts], *last, xh, xl, rows_in, base)
+
+
+def moved(arrays, shapes, plan, limit):
+    def kernel(*refs):
+        sems = refs[-1]
+        outs = refs[len(arrays) : -1]
+        copies = []
+        for k, (i, take, o, put) in enumerate(plan):
+            src = refs[i] if take is None else refs[i].at[take]
+            dst = outs[o] if put is None else outs[o].at[put]
+            copies.append(pltpu.make_async_copy(src, dst, sems.at[k]))
+        for copy in copies:
+            copy.start()
+        for copy in copies:
+            copy.wait()
+
+    return pl.pallas_call(
+        kernel,
+        out_shape=[jax.ShapeDtypeStruct(v, F32) for v in shapes],
+        in_specs=[ANY] * len(arrays),
+        out_specs=[ANY] * len(shapes),
+        scratch_shapes=[pltpu.SemaphoreType.DMA((len(plan),))],
+        compiler_params=params(limit),
+    )(*arrays)
+
+
+def second_hop(hop, *after):
+    (kept,) = moved(
+        (hop, along_y(hop[:1]), *after),
+        [(3, *hop.shape[1:])],
+        [(0, None, 0, pl.ds(0, 2)), (1, None, 0, pl.ds(2, 1))],
+        30,
+    )
+    return kept, from_core(kept)
 
 
 def local(rhs_tile, factor):
     row_i, col_i = lax.axis_index("row"), lax.axis_index("col")
     pos = jnp.stack([row_i // 2, row_i % 2, col_i // NZ, col_i % NZ]).astype(jnp.int32)
 
-    packed, w, b0 = pl.pallas_call(
+    packed = pl.pallas_call(
         pack_kernel,
-        out_shape=(
-            jax.ShapeDtypeStruct((PANELS * GR, 128), F32),
-            jax.ShapeDtypeStruct((2 * PB, 128), F32),
-            jax.ShapeDtypeStruct((WIN, NCOL), F32),
-        ),
-        in_specs=[VM, ANY],
-        out_specs=(VM, VM, VM),
-        scratch_shapes=[pltpu.SemaphoreType.DMA],
-        compiler_params=params(57),
-    )(factor, rhs_tile)
-
-    w1 = jnp.stack([w] + [from_first(w, d) for d in (1, 2, 3)])
+        out_shape=jax.ShapeDtypeStruct((WR + PANELS * GR, 128), F32),
+        in_specs=[VM],
+        out_specs=VM,
+        compiler_params=params(8),
+    )(factor)
+    rows3 = (PANELS, PB, NCOL)
+    (b0,) = moved(
+        (rhs_tile,),
+        [rows3],
+        [(0, pl.ds(p * PB, PB), 0, p) for p in range(PANELS)],
+        55,
+    )
+    bc = from_core(b0)
+
+    u1, u3 = from_first(packed, 1), from_first(packed, 3)
+    total = WR + PANELS * GR
+    h = WR + PANELS * GR // 2
+    f1, f3, bpair = moved(
+        (u1, u3, b0, bc),
+        [(h, 128), (total - h, 128), (2, *rows3)],
+        [(0, pl.ds(0, h), 0, None), (1, pl.ds(h, total - h), 1, None), (2, None, 2, 0), (3, None, 2, 1)],
+        57,
+    )
+    o1, o3 = from_first(f1, 1), from_first(f3, 3)
+    bhop = along_y(bpair)
+
+    half = h - WR
+    w1, q0 = moved(
+        (packed, u1, o1, u3, o3),
+        [(4, WR, 128), (4, total - WR, 128)],
+        [(j, pl.ds(0, WR), 0, j) for j in range(4)]
+        + [(j, pl.ds(WR, total - WR), 1, j) for j in (0, 1, 3)]
+        + [
+            (2, pl.ds(WR, half), 1, (2, pl.ds(0, half))),
+            (4, None, 1, (2, pl.ds(half, half))),
+        ],
+        57,
+    )
     groups = [w1] + [from_second(w1, d) for d in (1, 2, 3)]
+    q1, q3 = from_second(q0, 1), from_second(q0, 3)
+    q2 = (from_second(q1[:2], 1), from_second(q3[2:], 3))
 
     mine = pl.pallas_call(
         rows_kernel,
         out_shape=jax.ShapeDtypeStruct((SLOTS, PB, PANEL), F32),
-        in_specs=[SM] + [VM] * 4,
+        in_specs=[SM] + [VM] * 4 + [ANY],
         out_specs=VM,
         scratch_shapes=[
             pltpu.VMEM((16, 2 * PB, 128), F32),
             pltpu.VMEM((PANELS, NX, PB, 128), F32),
         ],
         compiler_params=params(8),
-    )(pos, *groups)
-
-    b1, b3 = from_y(b0, 1), from_y(b0, 3)
-    hb = WIN // 2
-    b2 = jnp.concatenate([from_y(b1[:hb], 1), from_y(b3[hb:], 3)])
-    bchip = jnp.stack([b0, b1, b2, b3]).reshape(NY, PANELS, PB, NCOL)
-    bother = from_core(bchip)
-
-    u1, u3 = from_first(packed, 1), from_first(packed, 3)
-    h = PANELS * GR // 2
-    u2 = jnp.concatenate([from_first(u1[:h], 1), from_first(u3[h:], 3)])
-    q0 = jnp.stack([packed, u1, u2, u3])
-    q1, q3 = from_second(q0, 1), from_second(q0, 3)
-    q2 = (from_second(q1[:2], 1), from_second(q3[2:], 3))
-
-    m1, m3 = from_y(mine, 1), from_y(mine, 3)
-    m1, m3, _ = lax.optimization_barrier((m1, m3, q0[0, 0, 0]))
-    hs = SLOTS // 2
-    m2 = jnp.concatenate([from_y(m1[:hs], 1), from_y(m3[hs:], 3)])
-    chip = jnp.stack([mine, m1, m2, m3])
-    other = from_core(chip)
+    )(pos, *groups, bhop)
+
+    mc = from_core(mine)
+    rows = (mine, mc, *second_hop(along_y(jnp.stack([mine, mc])), q1, q3))
+    rhs_rows = (b0, bc, *second_hop(bhop))
 
     parts = [assemble(q0), assemble(q1), assemble(q3)]
-    pos_late, _, _ = lax.optimization_barrier((pos, q1[0, 0, 0], q3[0, 0, 0]))
     xh, xl, base = pl.pallas_call(
         solve_kernel,
         out_shape=(
@@ -355,14 +411,14 @@
             jax.ShapeDtypeStruct((DEPTH, NCOL), BF16),
             jax.ShapeDtypeStruct((ROWS, NCOL), F32),
         ),
-        in_specs=[SM, ANY, ANY, ANY, ANY],
+        in_specs=[SM] + [ANY] * 8,
         out_specs=(VM, VM, ANY),
         scratch_shapes=[
             pltpu.VMEM((SLOTS, PANEL, PANEL), F32),
             pltpu.VMEM((PANELS, PANEL, NCOL), F32),
         ]
         + [pltpu.VMEM((PANELS, PANEL, PANEL), BF16)] * 4
-        + [pltpu.VMEM((PANELS, PANEL, NCOL), BF16)] * 2
+        + [pltpu.VMEM((PANEL, NCOL), BF16)] * 2
         + [pltpu.VMEM((DEPTH, NCOL), BF16)] * 2
         + [
             pltpu.VMEM((PANEL, NCOL), F32),
@@ -370,11 +426,11 @@
             pltpu.SemaphoreType.DMA((2, 2 * NY)),
             pltpu.SemaphoreType.DMA,
         ],
-        compiler_params=params(48),
+        compiler_params=params(45),
         cost_estimate=cost(36 * PANEL * PANEL * NCOL, 20e6),
-    )(pos_late, chip, other, bchip, bother)
-
-    return update(rhs_tile, base, parts + [assemble(*q2)], xh, xl)
+    )(pos, *rows, *rhs_rows)
+
+    return update(rhs_tile, base, parts, q2, xh, xl)
 
 
 def solution(mesh):

time: 201 us -> 388 us (1.93)
  Pallas kernels: 76.5 us -> 289 us
  waiting for transfers between devices: 82.7 us -> 62.1 us
  starting transfers between devices: 30.5 us -> 24.3 us
    pallas_call x1 -> x6, Pallas kernels: 3.66 us -> 218 us  [the longest x5 217 us: moved(): pl.pallas_call(kernel, out_shape=[jax.ShapeDtypeStruct(v, F32) for v in s...]
    ppermute x24 -> x19, waiting for transfers between devices: 82.7 us -> 62.1 us  [joint(): return lax.ppermute(v, ('row', 'col'), pairs)]
    ppermute x24 -> x19, starting transfers between devices: 30.5 us -> 24.3 us  [joint(): return lax.ppermute(v, ('row', 'col'), pairs)]
    pallas_call x4 -> x3, Pallas kernels: 15.1 us -> 11.1 us  [assemble(): pl.pallas_call(assemble_kernel, grid=(GROUPS,), out_shape=(out, out), in_...]
    unnamed x19 -> x41, local copies, waits for them, and re-layouts: 7.81 us -> 11.2 us
  transfers between devices with their start and end apart: 24 -> 19, of which waited for: 12 -> 10; matrix products, arithmetic and copies ran while one was open for 1% -> 0% of each run, Pallas kernels for 18% -> 36%
where the time goes in v1:
time: 388 us; the launch traced here: 387 us
  Pallas kernels  289 us (74%)
  waiting for transfers between devices  62.1 us (16%)
  starting transfers between devices  24.3 us (6%)
  local copies, waits for them, and re-layouts  11.5 us (3%)
    pallas_call x5, Pallas kernels, moved(): pl.pallas_call(kernel, out_shape=[jax.ShapeDtypeStruct(v, F32) for v in s...  217 us
    ppermute x19, waiting for transfers between devices, joint(): return lax.ppermute(v, ('row', 'col'), pairs)  62.1 us
    pallas_call x1, Pallas kernels, update(): pl.pallas_call(update_kernel, grid=(GROUPS,), out_shape=jax.ShapeDtypeStr...  35.5 us
    ppermute x19, starting transfers between devices, joint(): return lax.ppermute(v, ('row', 'col'), pairs)  24.3 us
    pallas_call x1, Pallas kernels, local(): pl.pallas_call(solve_kernel, out_shape=(jax.ShapeDtypeStruct((DEPTH, NCOL...  21.3 us
    unnamed x41, local copies, waits for them, and re-layouts  11.2 us
    pallas_call x3, Pallas kernels, assemble(): pl.pallas_call(assemble_kernel, grid=(GROUPS,), out_shape=(out, out), in_...  11.1 us
  transfers between devices with their start and end apart: 19, of which 10 were waited for; matrix products, arithmetic and copies ran while one was open for 0% of the time, Pallas kernels for 36%

profile of v1, /device:TPU:0, one launch (start us, length us, event | category | flops | bytes accessed | tf_op | source)
XLA Modules:
  0.0 387.2 jit_solution(5326343264700840515)
XLA Ops:
  0.0 27.9 %shard_map.29.refs_2_.b0 = f32[3,64,1152]{2,1,0:T(8,128)} custom-call(f32[2304,1152]{1,0:T(8,128)} %refs_10_.1), custom_call_target="tpu_custom_call" | custom-call | tf_op jit(solution)/shard_map/pallas_call | solution.py:322
  28.0 0.4 copy.4.f_ref
  28.4 0.7 shard_map.28.refs_0_
  29.1 2.9 collective-permute-start
  32.0 10.5 %collective-permute-done.refs_0_.refs_1_ = f32[1712,128]{1,0:T(8,128)S(1)} collective-permute-done((f32[1712,128]{1,0:T(8,128)S(1)}, f32[1712,128]{1,0:T(8,128)S(1)}, u32[]{:S(2)}, u32[]{:S(2)}) %collective-permute-start) | collective-permute-done | bytes 876576 | tf_op jit(solution)/shard_map/ppermute | solution.py:35
  42.5 3.7 collective-permute-done.1.refs_1_.refs_3_
  46.2 0.9 copy-done.14
  47.1 0.9 copy-done.4
  48.1 81.3 %shard_map.30 = (f32[920,128]{1,0:T(8,128)}, f32[792,128]{1,0:T(8,128)}, f32[2,3,64,1152]{3,2,1,0:T(8,128)}) custom-call(f32[1712,128]{1,0:T(8,128)} %copy-done.13, f32[1712,128]{1,0:T(8,128)} %copy-done.14, f32[3,64,1152]{2,1,0:T(8,128)} %shard_map.29.refs_2_.b0, f32[3,64,1152]{2,1,0:T(8,128)} %copy-done.4), custom_call_target="tpu_custom_call" | custom-call | tf_op jit(solution)/shard_map/pallas_call | solution.py:322
  129.4 3.1 collective-permute-start.12
  132.5 0.3 collective-permute-start.3
  132.8 1.7 collective-permute-start.4
  134.5 7.6 %collective-permute-done.4.refs_4_ = f32[792,128]{1,0:T(8,128)S(1)} collective-permute-done((f32[792,128]{1,0:T(8,128)}, f32[792,128]{1,0:T(8,128)S(1)}, u32[]{:S(2)}, u32[]{:S(2)}) %collective-permute-start.4) | collective-permute-done | bytes 405536 | tf_op jit(solution)/shard_map/ppermute | solution.py:35
  142.1 0.7 copy-done.17
  142.9 0.8 copy-done.16
  143.7 107.4 %shard_map.31 = (f32[4,128,128]{2,1,0:T(8,128)}, f32[4,1584,128]{2,1,0:T(8,128)}) custom-call(f32[1712,128]{1,0:T(8,128)} %copy-done.1, f32[1712,128]{1,0:T(8,128)} %copy-done.13, f32[920,128]{1,0:T(8,128)} %copy-done.16, f32[1712,128]{1,0:T(8,128)} %copy-done.14, f32[792,128]{1,0:T(8,128)} %copy-done.17), custom_call_target="tpu_custom_call" | custom-call | tf_op jit(solution)/shard_map/pallas_call | solution.py:322
  251.1 4.0 %collective-permute-start.10 = (f32[4,128,128]{2,1,0:T(8,128)}, f32[4,128,128]{2,1,0:T(8,128)S(1)}, u32[]{:S(2)}, u32[]{:S(2)}) collective-permute-start(f32[4,128,128]{2,1,0:T(8,128)} %get-tuple-element.28.g0), channel_id=1, source_target_pairs={{0,2},{1,3},{2,0},{3,1},{4,6},{5,7},{6,4},{7,5},{8,10},{9,11},{10,... | collective-permute-start | bytes 786440 | tf_op jit(solution)/shard_map/ppermute | solution.py:35
  255.0 1.0 collective-permute-start.11
  256.0 2.2 collective-permute-start.9
  258.3 1.2 collective-permute-done.10.g2
  259.6 3.2 collective-permute-done.11.g3
  262.8 0.6 collective-permute-done.9.g1
  263.4 0.9 copy-done.6
  264.4 2.8 shard_map.35.m0
  267.3 2.7 collective-permute-start.5
  270.0 0.1 pad_maximum_fusion
  270.2 0.8 collective-permute-start.14
  271.1 0.5 collective-permute-start.17
  271.6 19.1 %collective-permute-done.14.refs_0_ = f32[2,6,64,512]{3,2,1,0:T(8,128)S(1)} collective-permute-done((f32[2,6,64,512]{3,2,1,0:T(8,128)S(1)}, f32[2,6,64,512]{3,2,1,0:T(8,128)S(1)}, u32[]{:S(2)}, u32[]{:S(2)}) %collective-permute-start.14) | collective-permute-done | bytes 1572896 | tf_op jit(solution)/shard_map/ppermute | solution.py:35
  290.7 2.0 collective-permute-start.15
  292.8 7.4 %collective-permute-done.17.refs_1_ = f32[1,3,64,1152]{3,2,1,0:T(8,128)S(1)} collective-permute-done((f32[1,3,64,1152]{3,2,1,0:T(8,128)S(1)}, f32[1,3,64,1152]{3,2,1,0:T(8,128)S(1)}, u32[]{:S(2)}, u32[]{:S(2)}) %collective-permute-start.17) | collective-permute-done | bytes 884768 | tf_op jit(solution)/shard_map/ppermute | solution.py:35
  300.1 0.6 shard_map.37.bown
  300.8 5.0 %collective-permute-done.5.refs_0_.refs_2_ = f32[4,1584,128]{2,1,0:T(8,128)S(1)} collective-permute-done((f32[4,1584,128]{2,1,0:T(8,128)S(1)}, f32[4,1584,128]{2,1,0:T(8,128)S(1)}, u32[]{:S(2)}, u32[]{:S(2)}) %collective-permute-start.5) | collective-permute-done | bytes 3244064 | tf_op jit(solution)/shard_map/ppermute | solution.py:35
  305.9 3.7 collective-permute-done.6.refs_0_.refs_3_
  309.6 0.2 shard_map.36.mown
  310.0 2.3 collective-permute-start.7
  312.4 0.3 collective-permute-start.8
  312.7 3.8 shard_map.32
  316.5 1.1 copy-done.7
  317.6 1.2 copy-done.8
  318.8 3.7 shard_map.33
  322.5 1.2 copy-done.9
  323.7 1.2 copy-done.10
  324.9 3.7 shard_map.34
  328.6 21.3 %shard_map.38 = (bf16[1536,1152]{1,0:T(8,128)(2,1)}, bf16[1536,1152]{1,0:T(8,128)(2,1)}, f32[2304,1152]{1,0:T(8,128)}) custom-call(s32[4]{0:T(128)S(1)} %pad_add_fusion.pos, f32[6,64,512]{2,1,0:T(8,128)S(1)} %shard_map.35.m0, f32[6,64,512]{2,1,0:T(8,128)S(1)} %collective-permute-done.13.mc, f32[3,6,64,512]{3,2,1,0:T(8,128)S(1)} %shard_map.36.mown, ...), custom_call_target="tpu_custom_call" | custom-call | flops 10871635968 | bytes 20000000 | tf_op jit(solution)/shard_map/pallas_call | solution.py:407
  350.0 1.2 copy-done.18
  351.2 0.5 copy-done.19
  351.7 35.5 %shard_map.39 = f32[2304,1152]{1,0:T(8,128)} custom-call(bf16[4,528,384]{2,1,0:T(8,128)(2,1)} %copy-done.7, bf16[4,528,384]{2,1,0:T(8,128)(2,1)} %copy-done.9, bf16[4,528,384]{2,1,0:T(8,128)(2,1)} %copy-done.11, bf16[4,528,384]{2,1,0:T(8,128)(2,1)} %copy-done.8, bf16[4,528,384]{2,1,0:T(8,128)(2,1)} %copy-done.10, ...), custom_call_target="tpu_custom_call", output_to_operand_aliasing={{}: (11, {})} | custom-call | flops 22422749184 | bytes 30000000 | tf_op jit(solution)/shard_map/pallas_call | solution.py:295
  (49 shorter events, 0.8 us)
Async XLA Ops:
  0.0 28.0 %copy-start.15 = (f32[2304,96]{0,1:T(8,128)S(1)}, f32[2304,96]{0,1:T(8,128)}, u32[]{:S(2)}) copy-start(f32[2304,96]{0,1:T(8,128)} %param.3) | copy-start | bytes 2654212
  27.9 18.3 %collective-permute-start.2 = (f32[3,64,1152]{2,1,0:T(8,128)}, f32[3,64,1152]{2,1,0:T(8,128)S(1)}, u32[]{:S(2)}, u32[]{:S(2)}) collective-permute-start(f32[3,64,1152]{2,1,0:T(8,128)} %shard_map.29.refs_2_.b0), channel_id=1, source_target_pairs={{0,16},{1,17},{2,18},{3,19},{4,20},{5,21},{6,22},{7,23},{8,24},{9,... | collective-permute-start | bytes 2654216 | tf_op jit(solution)/shard_map/ppermute | solution.py:35
  29.1 100.3 %copy-start.1 = (f32[1712,128]{1,0:T(8,128)}, f32[1712,128]{1,0:T(8,128)S(1)}, u32[]{:S(2)}) copy-start(f32[1712,128]{1,0:T(8,128)S(1)} %shard_map.28.refs_0_) | copy-start | bytes 2629636
  29.1 13.4 %collective-permute-start = (f32[1712,128]{1,0:T(8,128)S(1)}, f32[1712,128]{1,0:T(8,128)S(1)}, u32[]{:S(2)}, u32[]{:S(2)}) collective-permute-start(f32[1712,128]{1,0:T(8,128)S(1)} %shard_map.28.refs_0_), channel_id=1, source_target_pairs={{0,12},{1,13},{2,14},{3,15},{4,0},{5,1},{6,2},{7,3},{8,4},{9,5},{1... | collective-permute-start | bytes 2629640 | tf_op jit(solution)/shard_map/ppermute | solution.py:35
  32.0 14.2 %collective-permute-start.1 = (f32[1712,128]{1,0:T(8,128)S(1)}, f32[1712,128]{1,0:T(8,128)S(1)}, u32[]{:S(2)}, u32[]{:S(2)}) collective-permute-start(f32[1712,128]{1,0:T(8,128)S(1)} %shard_map.28.refs_0_), channel_id=1, source_target_pairs={{0,4},{1,5},{2,6},{3,7},{4,8},{5,9},{6,10},{7,11},{8,12},{9,13},{1... | collective-permute-start | bytes 2629640 | tf_op jit(solution)/shard_map/ppermute | solution.py:35
  42.5 3.7 copy-start.13
  46.2 0.9 copy-start.14
  47.1 0.9 copy-start.4
  129.4 134.0 %collective-permute-start.12 = (f32[2,3,64,1152]{3,2,1,0:T(8,128)}, f32[2,3,64,1152]{3,2,1,0:T(8,128)S(1)}, u32[]{:S(2)}, u32[]{:S(2)}) collective-permute-start(f32[2,3,64,1152]{3,2,1,0:T(8,128)} %get-tuple-element.29), channel_id=1, source_target_pairs={{0,96},{1,97},{2,98},{3,99},{4,100},{5,101},{6,102},{7,103},{8,104... | collective-permute-start | bytes 5308424 | tf_op jit(solution)/shard_map/ppermute | solution.py:35
  132.5 9.7 %collective-permute-start.3 = (f32[920,128]{1,0:T(8,128)}, f32[920,128]{1,0:T(8,128)S(1)}, u32[]{:S(2)}, u32[]{:S(2)}) collective-permute-start(f32[920,128]{1,0:T(8,128)} %get-tuple-element.19), channel_id=1, source_target_pairs={{0,12},{1,13},{2,14},{3,15},{4,0},{5,1},{6,2},{7,3},{8,4},{9,5},{1... | collective-permute-start | bytes 1413128 | tf_op jit(solution)/shard_map/ppermute | solution.py:35
  132.8 9.3 %collective-permute-start.4 = (f32[792,128]{1,0:T(8,128)}, f32[792,128]{1,0:T(8,128)S(1)}, u32[]{:S(2)}, u32[]{:S(2)}) collective-permute-start(f32[792,128]{1,0:T(8,128)} %get-tuple-element.20), channel_id=1, source_target_pairs={{0,4},{1,5},{2,6},{3,7},{4,8},{5,9},{6,10},{7,11},{8,12},{9,13},{1... | collective-permute-start | bytes 1216520 | tf_op jit(solution)/shard_map/ppermute | solution.py:35
  142.1 0.7 copy-start.17
  142.9 0.8 copy-start.16
  251.1 8.5 %collective-permute-start.10 = (f32[4,128,128]{2,1,0:T(8,128)}, f32[4,128,128]{2,1,0:T(8,128)S(1)}, u32[]{:S(2)}, u32[]{:S(2)}) collective-permute-start(f32[4,128,128]{2,1,0:T(8,128)} %get-tuple-element.28.g0), channel_id=1, source_target_pairs={{0,2},{1,3},{2,0},{3,1},{4,6},{5,7},{6,4},{7,5},{8,10},{9,11},{10,... | collective-permute-start | bytes 786440 | tf_op jit(solution)/shard_map/ppermute | solution.py:35
  255.0 7.8 %collective-permute-start.11 = (f32[4,128,128]{2,1,0:T(8,128)}, f32[4,128,128]{2,1,0:T(8,128)S(1)}, u32[]{:S(2)}, u32[]{:S(2)}) collective-permute-start(f32[4,128,128]{2,1,0:T(8,128)} %get-tuple-element.28.g0), channel_id=1, source_target_pairs={{0,1},{1,2},{2,3},{3,0},{4,5},{5,6},{6,7},{7,4},{8,9},{9,10},{10,1... | collective-permute-start | bytes 786440 | tf_op jit(solution)/shard_map/ppermute | solution.py:35
  256.0 7.4 %collective-permute-start.9 = (f32[4,128,128]{2,1,0:T(8,128)}, f32[4,128,128]{2,1,0:T(8,128)S(1)}, u32[]{:S(2)}, u32[]{:S(2)}) collective-permute-start(f32[4,128,128]{2,1,0:T(8,128)} %get-tuple-element.28.g0), channel_id=1, source_target_pairs={{0,3},{1,0},{2,1},{3,2},{4,7},{5,4},{6,5},{7,6},{8,11},{9,8},{10,9... | collective-permute-start | bytes 786440 | tf_op jit(solution)/shard_map/ppermute | solution.py:35
  258.3 8.9 %copy-start.2 = (f32[4,1584,128]{2,1,0:T(8,128)S(1)}, f32[4,1584,128]{2,1,0:T(8,128)}, u32[]{:S(2)}) copy-start(f32[4,1584,128]{2,1,0:T(8,128)} %get-tuple-element.21.refs_0_) | copy-start | bytes 9732100
  263.4 1.0 copy-start.6
  267.2 2.9 collective-permute-start.13
  267.3 38.6 %collective-permute-start.5 = (f32[4,1584,128]{2,1,0:T(8,128)S(1)}, f32[4,1584,128]{2,1,0:T(8,128)S(1)}, u32[]{:S(2)}, u32[]{:S(2)}) collective-permute-start(f32[4,1584,128]{2,1,0:T(8,128)S(1)} %copy-done.2), channel_id=1, source_target_pairs={{0,3},{1,0},{2,1},{3,2},{4,7},{5,4},{6,5},{7,6},{8,11},{9,8},{10,9... | collective-permute-start | bytes 9732104 | tf_op jit(solution)/shard_map/ppermute | solution.py:35
  270.0 39.5 %collective-permute-start.6 = (f32[4,1584,128]{2,1,0:T(8,128)S(1)}, f32[4,1584,128]{2,1,0:T(8,128)S(1)}, u32[]{:S(2)}, u32[]{:S(2)}) collective-permute-start(f32[4,1584,128]{2,1,0:T(8,128)S(1)} %copy-done.2), channel_id=1, source_target_pairs={{0,1},{1,2},{2,3},{3,0},{4,5},{5,6},{6,7},{7,4},{8,9},{9,10},{10,1... | collective-permute-start | bytes 9732104 | tf_op jit(solution)/shard_map/ppermute | solution.py:35
  270.2 20.5 %collective-permute-start.14 = (f32[2,6,64,512]{3,2,1,0:T(8,128)S(1)}, f32[2,6,64,512]{3,2,1,0:T(8,128)S(1)}, u32[]{:S(2)}, u32[]{:S(2)}) collective-permute-start(f32[2,6,64,512]{3,2,1,0:T(8,128)S(1)} %pad_maximum_fusion), channel_id=1, source_target_pairs={{0,96},{1,97},{2,98},{3,99},{4,100},{5,101},{6,102},{7,103},{8,104... | collective-permute-start | bytes 4718600 | tf_op jit(solution)/shard_map/ppermute | solution.py:35
  271.1 29.1 %collective-permute-start.17 = (f32[1,3,64,1152]{3,2,1,0:T(8,128)S(1)}, f32[1,3,64,1152]{3,2,1,0:T(8,128)S(1)}, u32[]{:S(2)}, u32[]{:S(2)}) collective-permute-start(f32[1,3,64,1152]{3,2,1,0:T(8,128)S(1)} %slice.19), channel_id=1, source_target_pairs={{0,96},{1,97},{2,98},{3,99},{4,100},{5,101},{6,102},{7,103},{8,104... | collective-permute-start | bytes 2654216 | tf_op jit(solution)/shard_map/ppermute | solution.py:35
  290.7 18.8 %collective-permute-start.15 = (f32[1,6,64,512]{3,2,1,0:T(8,128)S(1)}, f32[1,6,64,512]{3,2,1,0:T(8,128)S(1)}, u32[]{:S(2)}, u32[]{:S(2)}) collective-permute-start(f32[1,6,64,512]{3,2,1,0:T(8,128)S(1)} %slice.18), channel_id=1, source_target_pairs={{0,96},{1,97},{2,98},{3,99},{4,100},{5,101},{6,102},{7,103},{8,104... | collective-permute-start | bytes 2359304 | tf_op jit(solution)/shard_map/ppermute | solution.py:35
  300.7 9.0 %copy-start.3 = (f32[3,3,64,1152]{3,2,1,0:T(8,128)}, f32[3,3,64,1152]{3,2,1,0:T(8,128)S(1)}, u32[]{:S(2)}) copy-start(f32[3,3,64,1152]{3,2,1,0:T(8,128)S(1)} %shard_map.37.bown) | copy-start | bytes 7962628
  300.7 27.8 %collective-permute-start.18 = (f32[3,3,64,1152]{3,2,1,0:T(8,128)S(1)}, f32[3,3,64,1152]{3,2,1,0:T(8,128)}, u32[]{:S(2)}, u32[]{:S(2)}) collective-permute-start(f32[3,3,64,1152]{3,2,1,0:T(8,128)S(1)} %shard_map.37.bown), channel_id=1, source_target_pairs={{0,16},{1,17},{2,18},{3,19},{4,20},{5,21},{6,22},{7,23},{8,24},{9,... | collective-permute-start | bytes 7962632 | tf_op jit(solution)/shard_map/ppermute | solution.py:35
  309.8 18.8 %collective-permute-start.16 = (f32[3,6,64,512]{3,2,1,0:T(8,128)S(1)}, f32[3,6,64,512]{3,2,1,0:T(8,128)S(1)}, u32[]{:S(2)}, u32[]{:S(2)}) collective-permute-start(f32[3,6,64,512]{3,2,1,0:T(8,128)S(1)} %shard_map.36.mown), channel_id=1, source_target_pairs={{0,16},{1,17},{2,18},{3,19},{4,20},{5,21},{6,22},{7,23},{8,24},{9,... | collective-permute-start | bytes 7077896 | tf_op jit(solution)/shard_map/ppermute | solution.py:35
  310.0 40.0 %collective-permute-start.7 = (f32[2,1584,128]{2,1,0:T(8,128)S(1)}, f32[2,1584,128]{2,1,0:T(8,128)S(1)}, u32[]{:S(2)}, u32[]{:S(2)}) collective-permute-start(f32[2,1584,128]{2,1,0:T(8,128)S(1)} %slice.16), channel_id=1, source_target_pairs={{0,3},{1,0},{2,1},{3,2},{4,7},{5,4},{6,5},{7,6},{8,11},{9,8},{10,9... | collective-permute-start | bytes 4866056 | tf_op jit(solution)/shard_map/ppermute | solution.py:35
  312.4 37.5 %collective-permute-start.8 = (f32[2,1584,128]{2,1,0:T(8,128)S(1)}, f32[2,1584,128]{2,1,0:T(8,128)S(1)}, u32[]{:S(2)}, u32[]{:S(2)}) collective-permute-start(f32[2,1584,128]{2,1,0:T(8,128)S(1)} %slice.17), channel_id=1, source_target_pairs={{0,1},{1,2},{2,3},{3,0},{4,5},{5,6},{6,7},{7,4},{8,9},{9,10},{10,1... | collective-permute-start | bytes 4866056 | tf_op jit(solution)/shard_map/ppermute | solution.py:35
  316.4 1.2 copy-start.7
  317.6 1.2 copy-start.8
  322.5 1.2 copy-start.9
  323.7 1.2 copy-start.10
  324.8 3.7 copy-start
  324.9 3.7 copy-start.5
  328.5 21.4 %copy-start.11 = (bf16[4,528,384]{2,1,0:T(8,128)(2,1)}, bf16[4,528,384]{2,1,0:T(8,128)(2,1)S(1)}, u32[]{:S(2)}) copy-start(bf16[4,528,384]{2,1,0:T(8,128)(2,1)S(1)} %get-tuple-element.24.refs_2_) | copy-start | bytes 4866052
  328.6 21.4 %copy-start.12 = (bf16[4,528,384]{2,1,0:T(8,128)(2,1)}, bf16[4,528,384]{2,1,0:T(8,128)(2,1)S(1)}, u32[]{:S(2)}) copy-start(bf16[4,528,384]{2,1,0:T(8,128)(2,1)S(1)} %get-tuple-element.27.refs_5_) | copy-start | bytes 4866052
  349.9 1.2 copy-start.18
  349.9 1.8 copy-start.19

commit v2 on v1

--- a/solution.py
+++ b/solution.py
@@ -15,6 +15,8 @@
 GR = TRAIL // GROUPS
 SLOTS = 6
 WR = 2 * PB
+SUB = PANELS * 128
+CHUNK = GR // 3
 MIB = 1024 * 1024
 GROUP_ORDER = (0, 1, 3, 2)
 
@@ -76,7 +78,7 @@
     return xs * NZ + zs
 
 
-def rows_kernel(pos, g0, g1, g2, g3, _after, out, canon, diag):
+def rows_kernel(pos, g0, g1, g2, g3, out, canon, diag):
     y, core = pos[0], pos[1]
     for i, ref in enumerate((g0, g1, g2, g3)):
         for j in range(4):
@@ -230,28 +232,42 @@
     copy.wait()
 
 
-def lanes_in_order(lrefs, lh, ll):
-    g = pl.program_id(0)
-    lane = lax.broadcasted_iota(jnp.int32, (GR, 128), 1) // CB
-    blocks = [(ref, b) for ref in lrefs for b in range(ref.shape[0])]
-    for p in range(PANELS):
-        total = None
-        for j, (ref, b) in enumerate(blocks):
-            v = pltpu.roll(ref[b, p * GR : (p + 1) * GR, :], (j - g) % 4 * CB, 1)
-            total = v if total is None else jnp.where(lane == j, v, total)
-        k = p * 128
-        lh[:, k : k + 128], ll[:, k : k + 128] = split(total)
-
-
-def assemble_kernel(*refs):
-    lanes_in_order(refs[:-2], *refs[-2:])
+def lanes_in_order(block, rows, lh, ll):
+    lane = lax.broadcasted_iota(jnp.int32, (rows.size, 128), 1)
+    low64 = lane < 64
+    low32 = lane % 64 < 32
+    for p in range(PANELS):
+        v = [block(j, p) for j in range(4)]
+        for j in range(2):
+            a, b = v[j], v[j + 2]
+            v[j] = jnp.where(low64, a, pltpu.roll(b, 64, 1))
+            v[j + 2] = jnp.where(low64, pltpu.roll(a, 64, 1), b)
+        for j in (0, 2):
+            a, b = v[j], v[j + 1]
+            v[j] = jnp.where(low32, a, pltpu.roll(b, 32, 1))
+            v[j + 1] = jnp.where(low32, pltpu.roll(a, 96, 1), b)
+        for g in range(GROUPS):
+            k = slice(p * 128, (p + 1) * 128)
+            lh[g, rows, k], ll[g, rows, k] = split(v[g])
+
+
+def assemble_kernel(q, lh, ll):
+    lanes_in_order(lambda j, p: q[j, p], pl.ds(0, CHUNK), lh, ll)
 
 
 def update_kernel(*refs):
     his, los, (qa, qb, xh, xl, r_ref, _base, out, lh, ll) = refs[:3], refs[3:6], refs[6:]
-    lanes_in_order((qa, qb), lh, ll)
+    g = pl.program_id(0)
+
+    @pl.when(g == 0)
+    def _():
+        @pl.loop(0, GR // CHUNK)
+        def _(i):
+            rows = pl.ds(pl.multiple_of(i * CHUNK, 16), CHUNK)
+            lanes_in_order(lambda j, p: (qa, qb)[j // 2][j % 2, p, rows, :], rows, lh, ll)
+
     a = [
-        jnp.concatenate([v[...] for v in (*part, last)], axis=1)
+        jnp.concatenate([v[...] for v in part] + [last[g]], axis=1)
         for part, last in ((his, lh), (los, ll))
     ]
     for w in COLS:
@@ -261,7 +277,6 @@
 VM = pl.BlockSpec(memory_space=pltpu.VMEM)
 SM = pl.BlockSpec(memory_space=pltpu.SMEM)
 ANY = pl.BlockSpec(memory_space=pl.ANY)
-SUB = PANELS * 128
 DEPTH = PANELS * PANEL
 
 
@@ -273,18 +288,18 @@
     return pl.CostEstimate(flops=int(flops), bytes_accessed=int(moved), transcendentals=0)
 
 
-def assemble(*blocks):
+def assemble(q):
     out = jax.ShapeDtypeStruct((GROUPS, GR, SUB), BF16)
-    spec = pl.BlockSpec((None, GR, SUB), lambda g: (g, 0, 0))
+    spec = pl.BlockSpec((GROUPS, CHUNK, SUB), lambda i: (0, i, 0))
     return pl.pallas_call(
         assemble_kernel,
-        grid=(GROUPS,),
+        grid=(GR // CHUNK,),
         out_shape=(out, out),
-        in_specs=[pl.BlockSpec(v.shape, lambda g: (0, 0, 0)) for v in blocks],
+        in_specs=[pl.BlockSpec((4, PANELS, CHUNK, 128), lambda i: (0, 0, i, 0))],
         out_specs=(spec, spec),
-        compiler_params=params(20),
+        compiler_params=params(12),
         cost_estimate=cost(4e6, 7e6),
-    )(*blocks)
+    )(q.reshape(4, PANELS, GR, 128))
 
 
 def update(rows_in, base, parts, last, xh, xl):
@@ -298,11 +313,11 @@
         out_shape=jax.ShapeDtypeStruct((ROWS, NCOL), F32),
         in_specs=[spec] * 6 + [VM] * 4 + [strip, ANY],
         out_specs=strip,
-        scratch_shapes=[pltpu.VMEM((GR, SUB), BF16)] * 2,
+        scratch_shapes=[pltpu.VMEM((GROUPS, GR, SUB), BF16)] * 2,
         input_output_aliases={11: 0},
         compiler_params=params(57),
         cost_estimate=cost(6 * TRAIL * DEPTH * NCOL, 30e6),
-    )(*[v[0] for v in parts], *[v[1] for v in parts], *last, xh, xl, rows_in, base)
+    )(*[v[0] for v in parts], *[v[1] for v in parts], *[v.reshape(2, PANELS, GR, 128) for v in last], xh, xl, rows_in, base)
 
 
 def moved(arrays, shapes, plan, limit):
@@ -323,7 +338,7 @@
         kernel,
         out_shape=[jax.ShapeDtypeStruct(v, F32) for v in shapes],
         in_specs=[ANY] * len(arrays),
-        out_specs=[ANY] * len(shapes),
+        out_specs=[VM] * len(shapes),
         scratch_shapes=[pltpu.SemaphoreType.DMA((len(plan),))],
         compiler_params=params(limit),
     )(*arrays)
@@ -358,22 +373,23 @@
         55,
     )
     bc = from_core(b0)
+    (bpair,) = moved((b0, bc, packed), [(2, *rows3)], [(0, None, 0, 0), (1, None, 0, 1)], 8)
+    bhop = along_y(bpair)
 
     u1, u3 = from_first(packed, 1), from_first(packed, 3)
     total = WR + PANELS * GR
     h = WR + PANELS * GR // 2
-    f1, f3, bpair = moved(
-        (u1, u3, b0, bc),
-        [(h, 128), (total - h, 128), (2, *rows3)],
-        [(0, pl.ds(0, h), 0, None), (1, pl.ds(h, total - h), 1, None), (2, None, 2, 0), (3, None, 2, 1)],
-        57,
+    f1, f3 = moved(
+        (u1, u3),
+        [(h, 128), (total - h, 128)],
+        [(0, pl.ds(0, h), 0, None), (1, pl.ds(h, total - h), 1, None)],
+        8,
     )
     o1, o3 = from_first(f1, 1), from_first(f3, 3)
-    bhop = along_y(bpair)
 
     half = h - WR
     w1, q0 = moved(
-        (packed, u1, o1, u3, o3),
+        (packed, u1, o1, u3, o3, bhop),
         [(4, WR, 128), (4, total - WR, 128)],
         [(j, pl.ds(0, WR), 0, j) for j in range(4)]
         + [(j, pl.ds(WR, total - WR), 1, j) for j in (0, 1, 3)]
@@ -381,7 +397,7 @@
             (2, pl.ds(WR, half), 1, (2, pl.ds(0, half))),
             (4, None, 1, (2, pl.ds(half, half))),
         ],
-        57,
+        16,
     )
     groups = [w1] + [from_second(w1, d) for d in (1, 2, 3)]
     q1, q3 = from_second(q0, 1), from_second(q0, 3)
@@ -390,14 +406,14 @@
     mine = pl.pallas_call(
         rows_kernel,
         out_shape=jax.ShapeDtypeStruct((SLOTS, PB, PANEL), F32),
-        in_specs=[SM] + [VM] * 4 + [ANY],
+        in_specs=[SM] + [VM] * 4,
         out_specs=VM,
         scratch_shapes=[
             pltpu.VMEM((16, 2 * PB, 128), F32),
             pltpu.VMEM((PANELS, NX, PB, 128), F32),
         ],
         compiler_params=params(8),
-    )(pos, *groups, bhop)
+    )(pos, *groups)
 
     mc = from_core(mine)
     rows = (mine, mc, *second_hop(along_y(jnp.stack([mine, mc])), q1, q3))
@@ -426,7 +442,7 @@
             pltpu.SemaphoreType.DMA((2, 2 * NY)),
             pltpu.SemaphoreType.DMA,
         ],
-        compiler_params=params(45),
+        compiler_params=params(42),
         cost_estimate=cost(36 * PANEL * PANEL * NCOL, 20e6),
     )(pos, *rows, *rhs_rows)
 

time: 388 us -> 172 us (0.44)
  Pallas kernels: 289 us -> 74.4 us
    pallas_call x5 -> x6, Pallas kernels: 217 us -> 5.47 us  [moved(): pl.pallas_call(kernel, out_shape=[jax.ShapeDtypeStruct(v, F32) for v in s...]
    unnamed x41 -> x23, local copies, waits for them, and re-layouts: 11.2 us -> 8.52 us
  transfers between devices with their start and end apart: 19 -> 19, of which waited for: 10 -> 13; matrix products, arithmetic and copies ran while one was open for 0% -> 1% of each run, Pallas kernels for 36% -> 18%
where the time goes in v2:
time: 172 us; the launch traced here: 171 us
  Pallas kernels  74.4 us (43%)
  waiting for transfers between devices  65 us (38%)
  starting transfers between devices  22.1 us (13%)
  local copies, waits for them, and re-layouts  8.86 us (5%)
    ppermute x19, waiting for transfers between devices, joint(): return lax.ppermute(v, ('row', 'col'), pairs)  65 us
    pallas_call x1, Pallas kernels, update(): pl.pallas_call(update_kernel, grid=(GROUPS,), out_shape=jax.ShapeDtypeStr...  35.3 us
    ppermute x19, starting transfers between devices, joint(): return lax.ppermute(v, ('row', 'col'), pairs)  22.1 us
    pallas_call x1, Pallas kernels, local(): pl.pallas_call(solve_kernel, out_shape=(jax.ShapeDtypeStruct((DEPTH, NCOL...  21.5 us
    unnamed x23, local copies, waits for them, and re-layouts  8.52 us
    pallas_call x3, Pallas kernels, assemble(): pl.pallas_call(assemble_kernel, grid=(GR // CHUNK,), out_shape=(out, out)...  7.95 us
    pallas_call x6, Pallas kernels, moved(): pl.pallas_call(kernel, out_shape=[jax.ShapeDtypeStruct(v, F32) for v in s...  5.47 us
    pallas_call x1, Pallas kernels, local(): pl.pallas_call(rows_kernel, out_shape=jax.ShapeDtypeStruct((SLOTS, PB, PA...  3.46 us
  transfers between devices with their start and end apart: 19, of which 13 were waited for; matrix products, arithmetic and copies ran while one was open for 1% of the time, Pallas kernels for 18%

profile of v2, /device:TPU:0, one launch (start us, length us, event | category | flops | bytes accessed | tf_op | source)
XLA Modules:
  0.0 170.9 jit_solution(8885722056934462972)
XLA Ops:
  0.0 2.1 %shard_map.30.refs_0_.b0 = f32[3,64,1152]{2,1,0:T(8,128)} custom-call(f32[2304,1152]{1,0:T(8,128)} %refs_10_.1), custom_call_target="tpu_custom_call" | custom-call | tf_op jit(solution)/shard_map/pallas_call | solution.py:337
  2.2 1.6 copy.4.f_ref
  3.8 0.7 shard_map.28.refs_2_.refs_0_
  4.5 0.3 collective-permute-done.4.refs_1_.bc
  4.8 0.4 shard_map.31
  5.2 3.2 %collective-permute-start.5 = (f32[2,3,64,1152]{3,2,1,0:T(8,128)S(1)}, f32[2,3,64,1152]{3,2,1,0:T(8,128)S(1)}, u32[]{:S(2)}, u32[]{:S(2)}) collective-permute-start(f32[2,3,64,1152]{3,2,1,0:T(8,128)S(1)} %shard_map.31), channel_id=1, source_target_pairs={{0,96},{1,97},{2,98},{3,99},{4,100},{5,101},{6,102},{7,103},{8,104... | collective-permute-start | bytes 5308424 | tf_op jit(solution)/shard_map/ppermute | solution.py:37
  8.4 2.8 %collective-permute-start = (f32[1712,128]{1,0:T(8,128)S(1)}, f32[1712,128]{1,0:T(8,128)S(1)}, u32[]{:S(2)}, u32[]{:S(2)}) collective-permute-start(f32[1712,128]{1,0:T(8,128)S(1)} %shard_map.28.refs_2_.refs_0_), channel_id=1, source_target_pairs={{0,12},{1,13},{2,14},{3,15},{4,0},{5,1},{6,2},{7,3},{8,4},{9,5},{1... | collective-permute-start | bytes 2629640 | tf_op jit(solution)/shard_map/ppermute | solution.py:37
  11.1 10.5 %collective-permute-done.refs_0_.refs_1_ = f32[1712,128]{1,0:T(8,128)S(1)} collective-permute-done((f32[1712,128]{1,0:T(8,128)S(1)}, f32[1712,128]{1,0:T(8,128)S(1)}, u32[]{:S(2)}, u32[]{:S(2)}) %collective-permute-start) | collective-permute-done | bytes 876576 | tf_op jit(solution)/shard_map/ppermute | solution.py:37
  21.6 3.7 %collective-permute-done.1.refs_1_.refs_3_ = f32[1712,128]{1,0:T(8,128)S(1)} collective-permute-done((f32[1712,128]{1,0:T(8,128)S(1)}, f32[1712,128]{1,0:T(8,128)S(1)}, u32[]{:S(2)}, u32[]{:S(2)}) %collective-permute-start.1) | collective-permute-done | bytes 876576 | tf_op jit(solution)/shard_map/ppermute | solution.py:37
  25.3 0.5 shard_map.29
  25.9 2.0 %collective-permute-start.3 = (f32[792,128]{1,0:T(8,128)S(1)}, f32[792,128]{1,0:T(8,128)S(1)}, u32[]{:S(2)}, u32[]{:S(2)}) collective-permute-start(f32[792,128]{1,0:T(8,128)S(1)} %get-tuple-element.19), channel_id=1, source_target_pairs={{0,4},{1,5},{2,6},{3,7},{4,8},{5,9},{6,10},{7,11},{8,12},{9,13},{1... | collective-permute-start | bytes 1216520 | tf_op jit(solution)/shard_map/ppermute | solution.py:37
  27.9 7.2 %collective-permute-done.3.refs_4_ = f32[792,128]{1,0:T(8,128)S(1)} collective-permute-done((f32[792,128]{1,0:T(8,128)S(1)}, f32[792,128]{1,0:T(8,128)S(1)}, u32[]{:S(2)}, u32[]{:S(2)}) %collective-permute-start.3) | collective-permute-done | bytes 405536 | tf_op jit(solution)/shard_map/ppermute | solution.py:37
  35.1 1.8 %shard_map.32 = (f32[4,128,128]{2,1,0:T(8,128)}, f32[4,1584,128]{2,1,0:T(8,128)S(1)}) custom-call(f32[1712,128]{1,0:T(8,128)S(1)} %shard_map.28.refs_2_.refs_0_, f32[1712,128]{1,0:T(8,128)S(1)} %collective-permute-done.refs_0_.refs_1_, f32[920,128]{1,0:T(8,128)S(1)} %collective-permute-done.2.refs_2_, ...), custom_call_target="tpu_custom_call" | custom-call | tf_op jit(solution)/shard_map/pallas_call | solution.py:337
  36.9 1.7 copy-done.1
  38.6 4.0 %collective-permute-start.10 = (f32[4,128,128]{2,1,0:T(8,128)}, f32[4,128,128]{2,1,0:T(8,128)}, u32[]{:S(2)}, u32[]{:S(2)}) collective-permute-start(f32[4,128,128]{2,1,0:T(8,128)} %get-tuple-element.27.g0), channel_id=1, source_target_pairs={{0,3},{1,0},{2,1},{3,2},{4,7},{5,4},{6,5},{7,6},{8,11},{9,8},{10,9... | collective-permute-start | bytes 786440 | tf_op jit(solution)/shard_map/ppermute | solution.py:37
  42.6 1.3 collective-permute-start.12
  43.9 5.7 %collective-permute-done.10.g1 = f32[4,128,128]{2,1,0:T(8,128)} collective-permute-done((f32[4,128,128]{2,1,0:T(8,128)}, f32[4,128,128]{2,1,0:T(8,128)}, u32[]{:S(2)}, u32[]{:S(2)}) %collective-permute-start.10) | collective-permute-done | bytes 262176 | tf_op jit(solution)/shard_map/ppermute | solution.py:37
  49.6 1.3 collective-permute-done.11.g2
  50.9 2.4 %collective-permute-done.12.g3 = f32[4,128,128]{2,1,0:T(8,128)} collective-permute-done((f32[4,128,128]{2,1,0:T(8,128)}, f32[4,128,128]{2,1,0:T(8,128)}, u32[]{:S(2)}, u32[]{:S(2)}) %collective-permute-start.12) | collective-permute-done | bytes 262176 | tf_op jit(solution)/shard_map/ppermute | solution.py:37
  53.3 3.5 %shard_map.36.m0 = f32[6,64,512]{2,1,0:T(8,128)S(1)} custom-call(s32[4]{0:T(128)S(1)} %pad_add_fusion.pos, f32[4,128,128]{2,1,0:T(8,128)} %get-tuple-element.27.g0, f32[4,128,128]{2,1,0:T(8,128)} %collective-permute-done.10.g1, f32[4,128,128]{2,1,0:T(8,128)} %collective-permute-done.11.g2, f32[4,128,128]{2,1,0:T(8,128)} %collective-permute-done.12.g3), custom_call_target="tpu_custom_call" | custom-call | tf_op jit(solution)/shard_map/pallas_call | solution.py:406
  56.9 1.0 collective-permute-start.6
  57.8 1.1 collective-permute-start.7
  59.0 0.2 collective-permute-done.13.mc
  59.2 0.1 pad_maximum_fusion
  59.3 0.8 collective-permute-start.14
  60.2 0.5 collective-permute-start.17
  60.7 19.1 %collective-permute-done.14.refs_0_ = f32[2,6,64,512]{3,2,1,0:T(8,128)S(1)} collective-permute-done((f32[2,6,64,512]{3,2,1,0:T(8,128)S(1)}, f32[2,6,64,512]{3,2,1,0:T(8,128)S(1)}, u32[]{:S(2)}, u32[]{:S(2)}) %collective-permute-start.14) | collective-permute-done | bytes 1572896 | tf_op jit(solution)/shard_map/ppermute | solution.py:37
  79.9 2.0 %collective-permute-start.15 = (f32[1,6,64,512]{3,2,1,0:T(8,128)S(1)}, f32[1,6,64,512]{3,2,1,0:T(8,128)S(1)}, u32[]{:S(2)}, u32[]{:S(2)}) collective-permute-start(f32[1,6,64,512]{3,2,1,0:T(8,128)S(1)} %slice.18), channel_id=1, source_target_pairs={{0,96},{1,97},{2,98},{3,99},{4,100},{5,101},{6,102},{7,103},{8,104... | collective-permute-start | bytes 2359304 | tf_op jit(solution)/shard_map/ppermute | solution.py:37
  81.9 7.4 %collective-permute-done.17.refs_1_ = f32[1,3,64,1152]{3,2,1,0:T(8,128)S(1)} collective-permute-done((f32[1,3,64,1152]{3,2,1,0:T(8,128)S(1)}, f32[1,3,64,1152]{3,2,1,0:T(8,128)S(1)}, u32[]{:S(2)}, u32[]{:S(2)}) %collective-permute-start.17) | collective-permute-done | bytes 884768 | tf_op jit(solution)/shard_map/ppermute | solution.py:37
  89.3 0.6 shard_map.38.bown
  89.8 0.6 collective-permute-start.18
  90.4 5.1 %collective-permute-done.6.refs_2_ = f32[4,1584,128]{2,1,0:T(8,128)S(1)} collective-permute-done((f32[4,1584,128]{2,1,0:T(8,128)}, f32[4,1584,128]{2,1,0:T(8,128)S(1)}, u32[]{:S(2)}, u32[]{:S(2)}) %collective-permute-start.6) | collective-permute-done | bytes 3244064 | tf_op jit(solution)/shard_map/ppermute | solution.py:37
  95.5 2.1 %collective-permute-done.7.refs_3_ = f32[4,1584,128]{2,1,0:T(8,128)S(1)} collective-permute-done((f32[4,1584,128]{2,1,0:T(8,128)}, f32[4,1584,128]{2,1,0:T(8,128)S(1)}, u32[]{:S(2)}, u32[]{:S(2)}) %collective-permute-start.7) | collective-permute-done | bytes 3244064 | tf_op jit(solution)/shard_map/ppermute | solution.py:37
  97.6 0.1 collective-permute-done.15.refs_1_
  97.7 0.2 shard_map.37.mown
  97.9 0.3 collective-permute-start.16
  98.2 0.1 slice.16
  98.3 1.8 %collective-permute-start.8 = (f32[2,1584,128]{2,1,0:T(8,128)S(1)}, f32[2,1584,128]{2,1,0:T(8,128)S(1)}, u32[]{:S(2)}, u32[]{:S(2)}) collective-permute-start(f32[2,1584,128]{2,1,0:T(8,128)S(1)} %slice.16), channel_id=1, source_target_pairs={{0,3},{1,0},{2,1},{3,2},{4,7},{5,4},{6,5},{7,6},{8,11},{9,8},{10,9... | collective-permute-start | bytes 4866056 | tf_op jit(solution)/shard_map/ppermute | solution.py:37
  100.2 0.5 collective-permute-start.9
  100.7 2.6 %shard_map.33 = (bf16[4,528,384]{2,1,0:T(8,128)(2,1)S(1)}, bf16[4,528,384]{2,1,0:T(8,128)(2,1)S(1)}) custom-call(f32[4,3,528,128]{3,2,1,0:T(8,128)S(1)} %bitcast.13), custom_call_target="tpu_custom_call" | custom-call | flops 4000000 | bytes 7000000 | tf_op jit(solution)/shard_map/pallas_call | solution.py:294
  103.4 1.2 copy-done.3
  104.6 2.6 %shard_map.34 = (bf16[4,528,384]{2,1,0:T(8,128)(2,1)S(1)}, bf16[4,528,384]{2,1,0:T(8,128)(2,1)S(1)}) custom-call(f32[4,3,528,128]{3,2,1,0:T(8,128)S(1)} %bitcast.11), custom_call_target="tpu_custom_call" | custom-call | flops 4000000 | bytes 7000000 | tf_op jit(solution)/shard_map/pallas_call | solution.py:294
  107.2 1.2 copy-done.5
  108.5 2.6 %shard_map.35 = (bf16[4,528,384]{2,1,0:T(8,128)(2,1)S(1)}, bf16[4,528,384]{2,1,0:T(8,128)(2,1)S(1)}) custom-call(f32[4,3,528,128]{3,2,1,0:T(8,128)S(1)} %bitcast.12), custom_call_target="tpu_custom_call" | custom-call | flops 4000000 | bytes 7000000 | tf_op jit(solution)/shard_map/pallas_call | solution.py:294
  111.2 1.6 copy-done.9
  112.8 21.5 %shard_map.39 = (bf16[1536,1152]{1,0:T(8,128)(2,1)}, bf16[1536,1152]{1,0:T(8,128)(2,1)}, f32[2304,1152]{1,0:T(8,128)}) custom-call(s32[4]{0:T(128)S(1)} %pad_add_fusion.pos, f32[6,64,512]{2,1,0:T(8,128)S(1)} %shard_map.36.m0, f32[6,64,512]{2,1,0:T(8,128)S(1)} %collective-permute-done.13.mc, f32[3,6,64,512]{3,2,1,0:T(8,128)S(1)} %shard_map.37.mown, ...), custom_call_target="tpu_custom_call" | custom-call | flops 10871635968 | bytes 20000000 | tf_op jit(solution)/shard_map/pallas_call | solution.py:423
  134.3 1.2 copy-done.10
  135.5 35.3 %shard_map.40 = f32[2304,1152]{1,0:T(8,128)} custom-call(bf16[4,528,384]{2,1,0:T(8,128)(2,1)} %copy-done.3, bf16[4,528,384]{2,1,0:T(8,128)(2,1)} %copy-done.5, bf16[4,528,384]{2,1,0:T(8,128)(2,1)} %copy-done.7, bf16[4,528,384]{2,1,0:T(8,128)(2,1)} %copy-done.4, bf16[4,528,384]{2,1,0:T(8,128)(2,1)} %copy-done.6, ...), custom_call_target="tpu_custom_call", output_to_operand_aliasing={{}: (11, {})} | custom-call | flops 22422749184 | bytes 30000000 | tf_op jit(solution)/shard_map/pallas_call | solution.py:310
  (32 shorter events, 0.6 us)
Async XLA Ops:
  2.1 2.7 %copy-start = (f32[3,64,1152]{2,1,0:T(8,128)S(1)}, f32[3,64,1152]{2,1,0:T(8,128)}, u32[]{:S(2)}) copy-start(f32[3,64,1152]{2,1,0:T(8,128)} %shard_map.30.refs_0_.b0) | copy-start | bytes 2654212
  2.1 2.7 %collective-permute-start.4 = (f32[3,64,1152]{2,1,0:T(8,128)}, f32[3,64,1152]{2,1,0:T(8,128)S(1)}, u32[]{:S(2)}, u32[]{:S(2)}) collective-permute-start(f32[3,64,1152]{2,1,0:T(8,128)} %shard_map.30.refs_0_.b0), channel_id=1, source_target_pairs={{0,16},{1,17},{2,18},{3,19},{4,20},{5,21},{6,22},{7,23},{8,24},{9,... | collective-permute-start | bytes 2654216 | tf_op jit(solution)/shard_map/ppermute | solution.py:37
  5.2 29.9 %collective-permute-start.5 = (f32[2,3,64,1152]{3,2,1,0:T(8,128)S(1)}, f32[2,3,64,1152]{3,2,1,0:T(8,128)S(1)}, u32[]{:S(2)}, u32[]{:S(2)}) collective-permute-start(f32[2,3,64,1152]{3,2,1,0:T(8,128)S(1)} %shard_map.31), channel_id=1, source_target_pairs={{0,96},{1,97},{2,98},{3,99},{4,100},{5,101},{6,102},{7,103},{8,104... | collective-permute-start | bytes 5308424 | tf_op jit(solution)/shard_map/ppermute | solution.py:37
  8.4 13.2 %collective-permute-start = (f32[1712,128]{1,0:T(8,128)S(1)}, f32[1712,128]{1,0:T(8,128)S(1)}, u32[]{:S(2)}, u32[]{:S(2)}) collective-permute-start(f32[1712,128]{1,0:T(8,128)S(1)} %shard_map.28.refs_2_.refs_0_), channel_id=1, source_target_pairs={{0,12},{1,13},{2,14},{3,15},{4,0},{5,1},{6,2},{7,3},{8,4},{9,5},{1... | collective-permute-start | bytes 2629640 | tf_op jit(solution)/shard_map/ppermute | solution.py:37
  11.1 14.2 %collective-permute-start.1 = (f32[1712,128]{1,0:T(8,128)S(1)}, f32[1712,128]{1,0:T(8,128)S(1)}, u32[]{:S(2)}, u32[]{:S(2)}) collective-permute-start(f32[1712,128]{1,0:T(8,128)S(1)} %shard_map.28.refs_2_.refs_0_), channel_id=1, source_target_pairs={{0,4},{1,5},{2,6},{3,7},{4,8},{5,9},{6,10},{7,11},{8,12},{9,13},{1... | collective-permute-start | bytes 2629640 | tf_op jit(solution)/shard_map/ppermute | solution.py:37
  25.8 9.3 %collective-permute-start.2 = (f32[920,128]{1,0:T(8,128)S(1)}, f32[920,128]{1,0:T(8,128)S(1)}, u32[]{:S(2)}, u32[]{:S(2)}) collective-permute-start(f32[920,128]{1,0:T(8,128)S(1)} %get-tuple-element.18), channel_id=1, source_target_pairs={{0,12},{1,13},{2,14},{3,15},{4,0},{5,1},{6,2},{7,3},{8,4},{9,5},{1... | collective-permute-start | bytes 1413128 | tf_op jit(solution)/shard_map/ppermute | solution.py:37
  25.9 9.2 %collective-permute-start.3 = (f32[792,128]{1,0:T(8,128)S(1)}, f32[792,128]{1,0:T(8,128)S(1)}, u32[]{:S(2)}, u32[]{:S(2)}) collective-permute-start(f32[792,128]{1,0:T(8,128)S(1)} %get-tuple-element.19), channel_id=1, source_target_pairs={{0,4},{1,5},{2,6},{3,7},{4,8},{5,9},{6,10},{7,11},{8,12},{9,13},{1... | collective-permute-start | bytes 1216520 | tf_op jit(solution)/shard_map/ppermute | solution.py:37
  36.9 1.7 copy-start.1
  38.6 11.1 %collective-permute-start.10 = (f32[4,128,128]{2,1,0:T(8,128)}, f32[4,128,128]{2,1,0:T(8,128)}, u32[]{:S(2)}, u32[]{:S(2)}) collective-permute-start(f32[4,128,128]{2,1,0:T(8,128)} %get-tuple-element.27.g0), channel_id=1, source_target_pairs={{0,3},{1,0},{2,1},{3,2},{4,7},{5,4},{6,5},{7,6},{8,11},{9,8},{10,9... | collective-permute-start | bytes 786440 | tf_op jit(solution)/shard_map/ppermute | solution.py:37
  42.6 8.3 %collective-permute-start.11 = (f32[4,128,128]{2,1,0:T(8,128)}, f32[4,128,128]{2,1,0:T(8,128)}, u32[]{:S(2)}, u32[]{:S(2)}) collective-permute-start(f32[4,128,128]{2,1,0:T(8,128)} %get-tuple-element.27.g0), channel_id=1, source_target_pairs={{0,2},{1,3},{2,0},{3,1},{4,6},{5,7},{6,4},{7,5},{8,10},{9,11},{10,... | collective-permute-start | bytes 786440 | tf_op jit(solution)/shard_map/ppermute | solution.py:37
  42.6 10.7 %collective-permute-start.12 = (f32[4,128,128]{2,1,0:T(8,128)}, f32[4,128,128]{2,1,0:T(8,128)}, u32[]{:S(2)}, u32[]{:S(2)}) collective-permute-start(f32[4,128,128]{2,1,0:T(8,128)} %get-tuple-element.27.g0), channel_id=1, source_target_pairs={{0,1},{1,2},{2,3},{3,0},{4,5},{5,6},{6,7},{7,4},{8,9},{9,10},{10,1... | collective-permute-start | bytes 786440 | tf_op jit(solution)/shard_map/ppermute | solution.py:37
  56.8 2.4 %collective-permute-start.13 = (f32[6,64,512]{2,1,0:T(8,128)S(1)}, f32[6,64,512]{2,1,0:T(8,128)S(1)}, u32[]{:S(2)}, u32[]{:S(2)}) collective-permute-start(f32[6,64,512]{2,1,0:T(8,128)S(1)} %shard_map.36.m0), channel_id=1, source_target_pairs={{0,16},{1,17},{2,18},{3,19},{4,20},{5,21},{6,22},{7,23},{8,24},{9,... | collective-permute-start | bytes 2359304 | tf_op jit(solution)/shard_map/ppermute | solution.py:37
  56.9 38.6 %collective-permute-start.6 = (f32[4,1584,128]{2,1,0:T(8,128)}, f32[4,1584,128]{2,1,0:T(8,128)S(1)}, u32[]{:S(2)}, u32[]{:S(2)}) collective-permute-start(f32[4,1584,128]{2,1,0:T(8,128)} %copy-done.1), channel_id=1, source_target_pairs={{0,3},{1,0},{2,1},{3,2},{4,7},{5,4},{6,5},{7,6},{8,11},{9,8},{10,9... | collective-permute-start | bytes 9732104 | tf_op jit(solution)/shard_map/ppermute | solution.py:37
  57.8 39.7 %collective-permute-start.7 = (f32[4,1584,128]{2,1,0:T(8,128)}, f32[4,1584,128]{2,1,0:T(8,128)S(1)}, u32[]{:S(2)}, u32[]{:S(2)}) collective-permute-start(f32[4,1584,128]{2,1,0:T(8,128)} %copy-done.1), channel_id=1, source_target_pairs={{0,1},{1,2},{2,3},{3,0},{4,5},{5,6},{6,7},{7,4},{8,9},{9,10},{10,1... | collective-permute-start | bytes 9732104 | tf_op jit(solution)/shard_map/ppermute | solution.py:37
  59.3 20.5 %collective-permute-start.14 = (f32[2,6,64,512]{3,2,1,0:T(8,128)S(1)}, f32[2,6,64,512]{3,2,1,0:T(8,128)S(1)}, u32[]{:S(2)}, u32[]{:S(2)}) collective-permute-start(f32[2,6,64,512]{3,2,1,0:T(8,128)S(1)} %pad_maximum_fusion), channel_id=1, source_target_pairs={{0,96},{1,97},{2,98},{3,99},{4,100},{5,101},{6,102},{7,103},{8,104... | collective-permute-start | bytes 4718600 | tf_op jit(solution)/shard_map/ppermute | solution.py:37
  60.2 29.1 %collective-permute-start.17 = (f32[1,3,64,1152]{3,2,1,0:T(8,128)S(1)}, f32[1,3,64,1152]{3,2,1,0:T(8,128)S(1)}, u32[]{:S(2)}, u32[]{:S(2)}) collective-permute-start(f32[1,3,64,1152]{3,2,1,0:T(8,128)S(1)} %slice.19), channel_id=1, source_target_pairs={{0,96},{1,97},{2,98},{3,99},{4,100},{5,101},{6,102},{7,103},{8,104... | collective-permute-start | bytes 2654216 | tf_op jit(solution)/shard_map/ppermute | solution.py:37
  79.9 17.8 %collective-permute-start.15 = (f32[1,6,64,512]{3,2,1,0:T(8,128)S(1)}, f32[1,6,64,512]{3,2,1,0:T(8,128)S(1)}, u32[]{:S(2)}, u32[]{:S(2)}) collective-permute-start(f32[1,6,64,512]{3,2,1,0:T(8,128)S(1)} %slice.18), channel_id=1, source_target_pairs={{0,96},{1,97},{2,98},{3,99},{4,100},{5,101},{6,102},{7,103},{8,104... | collective-permute-start | bytes 2359304 | tf_op jit(solution)/shard_map/ppermute | solution.py:37
  89.8 21.3 %collective-permute-start.18 = (f32[3,3,64,1152]{3,2,1,0:T(8,128)S(1)}, f32[3,3,64,1152]{3,2,1,0:T(8,128)S(1)}, u32[]{:S(2)}, u32[]{:S(2)}) collective-permute-start(f32[3,3,64,1152]{3,2,1,0:T(8,128)S(1)} %shard_map.38.bown), channel_id=1, source_target_pairs={{0,16},{1,17},{2,18},{3,19},{4,20},{5,21},{6,22},{7,23},{8,24},{9,... | collective-permute-start | bytes 7962632 | tf_op jit(solution)/shard_map/ppermute | solution.py:37
  97.9 13.3 %collective-permute-start.16 = (f32[3,6,64,512]{3,2,1,0:T(8,128)S(1)}, f32[3,6,64,512]{3,2,1,0:T(8,128)S(1)}, u32[]{:S(2)}, u32[]{:S(2)}) collective-permute-start(f32[3,6,64,512]{3,2,1,0:T(8,128)S(1)} %shard_map.37.mown), channel_id=1, source_target_pairs={{0,16},{1,17},{2,18},{3,19},{4,20},{5,21},{6,22},{7,23},{8,24},{9,... | collective-permute-start | bytes 7077896 | tf_op jit(solution)/shard_map/ppermute | solution.py:37
  98.3 2.5 %copy-start.2 = (f32[4,1584,128]{2,1,0:T(8,128)S(1)}, f32[4,1584,128]{2,1,0:T(8,128)}, u32[]{:S(2)}) copy-start(f32[4,1584,128]{2,1,0:T(8,128)} %copy-done.1) | copy-start | bytes 9732100
  98.3 36.0 %collective-permute-start.8 = (f32[2,1584,128]{2,1,0:T(8,128)S(1)}, f32[2,1584,128]{2,1,0:T(8,128)S(1)}, u32[]{:S(2)}, u32[]{:S(2)}) collective-permute-start(f32[2,1584,128]{2,1,0:T(8,128)S(1)} %slice.16), channel_id=1, source_target_pairs={{0,3},{1,0},{2,1},{3,2},{4,7},{5,4},{6,5},{7,6},{8,11},{9,8},{10,9... | collective-permute-start | bytes 4866056 | tf_op jit(solution)/shard_map/ppermute | solution.py:37
  100.2 34.1 %collective-permute-start.9 = (f32[2,1584,128]{2,1,0:T(8,128)S(1)}, f32[2,1584,128]{2,1,0:T(8,128)}, u32[]{:S(2)}, u32[]{:S(2)}) collective-permute-start(f32[2,1584,128]{2,1,0:T(8,128)S(1)} %slice.17), channel_id=1, source_target_pairs={{0,1},{1,2},{2,3},{3,0},{4,5},{5,6},{6,7},{7,4},{8,9},{9,10},{10,1... | collective-permute-start | bytes 4866056 | tf_op jit(solution)/shard_map/ppermute | solution.py:37
  103.4 1.2 copy-start.3
  104.6 2.7 %copy-start.4 = (bf16[4,528,384]{2,1,0:T(8,128)(2,1)}, bf16[4,528,384]{2,1,0:T(8,128)(2,1)S(1)}, u32[]{:S(2)}) copy-start(bf16[4,528,384]{2,1,0:T(8,128)(2,1)S(1)} %get-tuple-element.24.refs_3_) | copy-start | bytes 4866052
  107.2 1.2 copy-start.5
  108.5 2.7 %copy-start.6 = (bf16[4,528,384]{2,1,0:T(8,128)(2,1)}, bf16[4,528,384]{2,1,0:T(8,128)(2,1)S(1)}, u32[]{:S(2)}) copy-start(bf16[4,528,384]{2,1,0:T(8,128)(2,1)S(1)} %get-tuple-element.25.refs_4_) | copy-start | bytes 4866052
  111.2 23.1 %copy-start.7 = (bf16[4,528,384]{2,1,0:T(8,128)(2,1)}, bf16[4,528,384]{2,1,0:T(8,128)(2,1)S(1)}, u32[]{:S(2)}) copy-start(bf16[4,528,384]{2,1,0:T(8,128)(2,1)S(1)} %get-tuple-element.23.refs_2_) | copy-start | bytes 4866052
  111.2 23.1 %copy-start.8 = (bf16[4,528,384]{2,1,0:T(8,128)(2,1)}, bf16[4,528,384]{2,1,0:T(8,128)(2,1)S(1)}, u32[]{:S(2)}) copy-start(bf16[4,528,384]{2,1,0:T(8,128)(2,1)S(1)} %get-tuple-element.26.refs_5_) | copy-start | bytes 4866052
  111.2 1.6 copy-start.9
  134.3 1.2 copy-start.10

commit v3 on v2

--- a/solution.py
+++ b/solution.py
@@ -344,9 +344,11 @@
     )(*arrays)
 
 
-def second_hop(hop, *after):
+def second_hop(hop, early=(), late=()):
+    shape = (1, *hop.shape[1:])
+    (first,) = moved((hop, *early), [shape], [(0, pl.ds(0, 1), 0, None)], 30)
     (kept,) = moved(
-        (hop, along_y(hop[:1]), *after),
+        (hop, along_y(first), *late),
         [(3, *hop.shape[1:])],
         [(0, None, 0, pl.ds(0, 2)), (1, None, 0, pl.ds(2, 1))],
         30,
@@ -415,11 +417,13 @@
         compiler_params=params(8),
     )(pos, *groups)
 
+    parts = [assemble(q0), assemble(q1), assemble(q3)]
     mc = from_core(mine)
-    rows = (mine, mc, *second_hop(along_y(jnp.stack([mine, mc])), q1, q3))
+    early = (q1, q3, parts[0][0])
+    late = (parts[1][0], parts[2][0])
+    rows = (mine, mc, *second_hop(along_y(jnp.stack([mine, mc])), early, late))
     rhs_rows = (b0, bc, *second_hop(bhop))
 
-    parts = [assemble(q0), assemble(q1), assemble(q3)]
     xh, xl, base = pl.pallas_call(
         solve_kernel,
         out_shape=(

time: 172 us -> 201 us (1.17)
  waiting for transfers between devices: 65 us -> 84.3 us
  Pallas kernels: 74.4 us -> 78.5 us
  starting transfers between devices: 22.1 us -> 25.6 us
  local copies, waits for them, and re-layouts: 8.86 us -> 10.9 us
    ppermute x19, waiting for transfers between devices: 65 us -> 84.3 us  [joint(): return lax.ppermute(v, ('row', 'col'), pairs)]
    ppermute x19, starting transfers between devices: 22.1 us -> 25.6 us  [joint(): return lax.ppermute(v, ('row', 'col'), pairs)]
    pallas_call x3, Pallas kernels: 7.95 us -> 10.8 us  [assemble(): pl.pallas_call(assemble_kernel, grid=(GR // CHUNK,), out_shape=(out, out)...]
    pallas_call x6 -> x8, Pallas kernels: 5.47 us -> 6.75 us  [moved(): pl.pallas_call(kernel, out_shape=[jax.ShapeDtypeStruct(v, F32) for v in s...]
    unnamed x23 -> x31, local copies, waits for them, and re-layouts: 8.52 us -> 9.3 us
  transfers between devices with their start and end apart: 19 -> 19, of which waited for: 13 -> 9; matrix products, arithmetic and copies ran while one was open for 1% -> 2% of each run, Pallas kernels for 18% -> 19%
where the time goes in v3:
time: 201 us; the launch traced here: 200 us
  waiting for transfers between devices  84.3 us (42%)
  Pallas kernels  78.5 us (39%)
  starting transfers between devices  25.6 us (13%)
  local copies, waits for them, and re-layouts  10.9 us (5%)
    ppermute x19, waiting for transfers between devices, joint(): return lax.ppermute(v, ('row', 'col'), pairs)  84.3 us
    pallas_call x1, Pallas kernels, update(): pl.pallas_call(update_kernel, grid=(GROUPS,), out_shape=jax.ShapeDtypeStr...  35.3 us
    ppermute x19, starting transfers between devices, joint(): return lax.ppermute(v, ('row', 'col'), pairs)  25.6 us
    pallas_call x1, Pallas kernels, local(): pl.pallas_call(solve_kernel, out_shape=(jax.ShapeDtypeStruct((DEPTH, NCOL...  21.5 us
    pallas_call x3, Pallas kernels, assemble(): pl.pallas_call(assemble_kernel, grid=(GR // CHUNK,), out_shape=(out, out)...  10.8 us
    unnamed x31, local copies, waits for them, and re-layouts  9.3 us
    pallas_call x8, Pallas kernels, moved(): pl.pallas_call(kernel, out_shape=[jax.ShapeDtypeStruct(v, F32) for v in s...  6.75 us
  transfers between devices with their start and end apart: 19, of which 9 were waited for; matrix products, arithmetic and copies ran while one was open for 2% of the time, Pallas kernels for 19%

profile of v3, /device:TPU:0, one launch (start us, length us, event | category | flops | bytes accessed | tf_op | source)
XLA Modules:
  0.0 199.8 jit_solution(15772797644089861055)
XLA Ops:
  0.0 2.1 %shard_map.30.refs_0_.b0 = f32[3,64,1152]{2,1,0:T(8,128)} custom-call(f32[2304,1152]{1,0:T(8,128)} %refs_10_.1), custom_call_target="tpu_custom_call" | custom-call | tf_op jit(solution)/shard_map/pallas_call | solution.py:337
  2.2 1.5 copy.4.f_ref
  3.7 0.7 shard_map.28.refs_2_.refs_0_
  4.5 0.3 collective-permute-done.4.refs_1_.bc
  4.9 0.4 shard_map.31
  5.3 0.9 copy-done.7
  6.2 3.1 %collective-permute-start.5 = (f32[2,3,64,1152]{3,2,1,0:T(8,128)S(1)}, f32[2,3,64,1152]{3,2,1,0:T(8,128)S(1)}, u32[]{:S(2)}, u32[]{:S(2)}) collective-permute-start(f32[2,3,64,1152]{3,2,1,0:T(8,128)S(1)} %shard_map.31), channel_id=1, source_target_pairs={{0,96},{1,97},{2,98},{3,99},{4,100},{5,101},{6,102},{7,103},{8,104... | collective-permute-start | bytes 5308424 | tf_op jit(solution)/shard_map/ppermute | solution.py:37
  9.3 1.5 collective-permute-start.1
  10.8 1.7 collective-permute-start
  12.6 10.9 %collective-permute-done.1.refs_1_.refs_3_ = f32[1712,128]{1,0:T(8,128)S(1)} collective-permute-done((f32[1712,128]{1,0:T(8,128)S(1)}, f32[1712,128]{1,0:T(8,128)S(1)}, u32[]{:S(2)}, u32[]{:S(2)}) %collective-permute-start.1) | collective-permute-done | bytes 876576 | tf_op jit(solution)/shard_map/ppermute | solution.py:37
  23.5 0.3 collective-permute-done.refs_0_.refs_1_
  23.8 0.5 shard_map.29
  24.3 3.0 %collective-permute-start.2 = (f32[920,128]{1,0:T(8,128)S(1)}, f32[920,128]{1,0:T(8,128)S(1)}, u32[]{:S(2)}, u32[]{:S(2)}) collective-permute-start(f32[920,128]{1,0:T(8,128)S(1)} %get-tuple-element.18), channel_id=1, source_target_pairs={{0,12},{1,13},{2,14},{3,15},{4,0},{5,1},{6,2},{7,3},{8,4},{9,5},{1... | collective-permute-start | bytes 1413128 | tf_op jit(solution)/shard_map/ppermute | solution.py:37
  27.3 9.1 %collective-permute-done.3.refs_4_ = f32[792,128]{1,0:T(8,128)S(1)} collective-permute-done((f32[792,128]{1,0:T(8,128)S(1)}, f32[792,128]{1,0:T(8,128)S(1)}, u32[]{:S(2)}, u32[]{:S(2)}) %collective-permute-start.3) | collective-permute-done | bytes 405536 | tf_op jit(solution)/shard_map/ppermute | solution.py:37
  36.4 2.8 %shard_map.32 = (f32[4,128,128]{2,1,0:T(8,128)S(1)}, f32[4,1584,128]{2,1,0:T(8,128)}) custom-call(f32[1712,128]{1,0:T(8,128)S(1)} %shard_map.28.refs_2_.refs_0_, f32[1712,128]{1,0:T(8,128)S(1)} %collective-permute-done.refs_0_.refs_1_, f32[920,128]{1,0:T(8,128)S(1)} %collective-permute-done.2.refs_2_, ...), custom_call_target="tpu_custom_call" | custom-call | tf_op jit(solution)/shard_map/pallas_call | solution.py:337
  39.2 2.0 collective-permute-start.7
  41.2 2.2 %collective-permute-start.6 = (f32[4,1584,128]{2,1,0:T(8,128)}, f32[4,1584,128]{2,1,0:T(8,128)S(1)}, u32[]{:S(2)}, u32[]{:S(2)}) collective-permute-start(f32[4,1584,128]{2,1,0:T(8,128)} %get-tuple-element.20), channel_id=1, source_target_pairs={{0,3},{1,0},{2,1},{3,2},{4,7},{5,4},{6,5},{7,6},{8,11},{9,8},{10,9... | collective-permute-start | bytes 9732104 | tf_op jit(solution)/shard_map/ppermute | solution.py:37
  43.4 3.4 %collective-permute-start.11 = (f32[4,128,128]{2,1,0:T(8,128)S(1)}, f32[4,128,128]{2,1,0:T(8,128)}, u32[]{:S(2)}, u32[]{:S(2)}) collective-permute-start(f32[4,128,128]{2,1,0:T(8,128)S(1)} %get-tuple-element.27.g0), channel_id=1, source_target_pairs={{0,2},{1,3},{2,0},{3,1},{4,6},{5,7},{6,4},{7,5},{8,10},{9,11},{10,... | collective-permute-start | bytes 786440 | tf_op jit(solution)/shard_map/ppermute | solution.py:37
  46.8 1.0 collective-permute-start.10
  47.9 34.9 %collective-permute-done.12.g3 = f32[4,128,128]{2,1,0:T(8,128)} collective-permute-done((f32[4,128,128]{2,1,0:T(8,128)S(1)}, f32[4,128,128]{2,1,0:T(8,128)}, u32[]{:S(2)}, u32[]{:S(2)}) %collective-permute-start.12) | collective-permute-done | bytes 262176 | tf_op jit(solution)/shard_map/ppermute | solution.py:37
  82.8 4.3 %collective-permute-done.11.g2 = f32[4,128,128]{2,1,0:T(8,128)} collective-permute-done((f32[4,128,128]{2,1,0:T(8,128)S(1)}, f32[4,128,128]{2,1,0:T(8,128)}, u32[]{:S(2)}, u32[]{:S(2)}) %collective-permute-start.11) | collective-permute-done | bytes 262176 | tf_op jit(solution)/shard_map/ppermute | solution.py:37
  87.1 3.4 %shard_map.36.m0 = f32[6,64,512]{2,1,0:T(8,128)S(1)} custom-call(s32[4]{0:T(128)S(1)} %pad_add_fusion.pos, f32[4,128,128]{2,1,0:T(8,128)S(1)} %get-tuple-element.27.g0, f32[4,128,128]{2,1,0:T(8,128)} %collective-permute-done.10.g1, f32[4,128,128]{2,1,0:T(8,128)} %collective-permute-done.11.g2, f32[4,128,128]{2,1,0:T(8,128)} %collective-permute-done.12.g3), custom_call_target="tpu_custom_call" | custom-call | tf_op jit(solution)/shard_map/pallas_call | solution.py:408
  90.5 2.3 %collective-permute-done.13.mc = f32[6,64,512]{2,1,0:T(8,128)S(1)} collective-permute-done((f32[6,64,512]{2,1,0:T(8,128)S(1)}, f32[6,64,512]{2,1,0:T(8,128)S(1)}, u32[]{:S(2)}, u32[]{:S(2)}) %collective-permute-start.13) | collective-permute-done | bytes 786464 | tf_op jit(solution)/shard_map/ppermute | solution.py:37
  92.8 0.1 pad_maximum_fusion
  92.9 0.8 collective-permute-start.14
  93.8 0.2 shard_map.39
  94.0 0.5 collective-permute-start.17
  94.5 4.1 %shard_map.33 = (bf16[4,528,384]{2,1,0:T(8,128)(2,1)S(1)}, bf16[4,528,384]{2,1,0:T(8,128)(2,1)S(1)}) custom-call(f32[4,3,528,128]{3,2,1,0:T(8,128)} %bitcast.q), custom_call_target="tpu_custom_call" | custom-call | flops 4000000 | bytes 7000000 | tf_op jit(solution)/shard_map/pallas_call | solution.py:294
  98.6 14.8 %collective-permute-done.14.refs_0_ = f32[2,6,64,512]{3,2,1,0:T(8,128)S(1)} collective-permute-done((f32[2,6,64,512]{3,2,1,0:T(8,128)S(1)}, f32[2,6,64,512]{3,2,1,0:T(8,128)S(1)}, u32[]{:S(2)}, u32[]{:S(2)}) %collective-permute-start.14) | collective-permute-done | bytes 1572896 | tf_op jit(solution)/shard_map/ppermute | solution.py:37
  113.5 2.0 %collective-permute-start.15 = (f32[1,6,64,512]{3,2,1,0:T(8,128)S(1)}, f32[1,6,64,512]{3,2,1,0:T(8,128)S(1)}, u32[]{:S(2)}, u32[]{:S(2)}) collective-permute-start(f32[1,6,64,512]{3,2,1,0:T(8,128)S(1)} %shard_map.37), channel_id=1, source_target_pairs={{0,96},{1,97},{2,98},{3,99},{4,100},{5,101},{6,102},{7,103},{8,104... | collective-permute-start | bytes 2359304 | tf_op jit(solution)/shard_map/ppermute | solution.py:37
  115.6 7.4 %collective-permute-done.17.refs_1_ = f32[1,3,64,1152]{3,2,1,0:T(8,128)S(1)} collective-permute-done((f32[1,3,64,1152]{3,2,1,0:T(8,128)S(1)}, f32[1,3,64,1152]{3,2,1,0:T(8,128)S(1)}, u32[]{:S(2)}, u32[]{:S(2)}) %collective-permute-start.17) | collective-permute-done | bytes 884768 | tf_op jit(solution)/shard_map/ppermute | solution.py:37
  122.9 0.6 shard_map.40.bown
  123.5 0.3 collective-permute-start.18
  123.8 4.1 %shard_map.35 = (bf16[4,528,384]{2,1,0:T(8,128)(2,1)S(1)}, bf16[4,528,384]{2,1,0:T(8,128)(2,1)S(1)}) custom-call(f32[4,3,528,128]{3,2,1,0:T(8,128)} %bitcast.2.q), custom_call_target="tpu_custom_call" | custom-call | flops 4000000 | bytes 7000000 | tf_op jit(solution)/shard_map/pallas_call | solution.py:294
  127.9 1.2 copy-done.10
  129.0 2.6 %shard_map.34 = (bf16[4,528,384]{2,1,0:T(8,128)(2,1)S(1)}, bf16[4,528,384]{2,1,0:T(8,128)(2,1)S(1)}) custom-call(f32[4,3,528,128]{3,2,1,0:T(8,128)S(1)} %bitcast.11), custom_call_target="tpu_custom_call" | custom-call | flops 4000000 | bytes 7000000 | tf_op jit(solution)/shard_map/pallas_call | solution.py:294
  131.7 1.2 copy-done.11
  132.9 0.2 shard_map.38.mown
  133.1 1.1 copy-done.6
  134.1 0.3 collective-permute-start.16
  134.4 1.5 slice.9
  136.0 0.6 collective-permute-start.9
  136.7 2.9 %collective-permute-start.8 = (f32[2,1584,128]{2,1,0:T(8,128)S(1)}, f32[2,1584,128]{2,1,0:T(8,128)S(1)}, u32[]{:S(2)}, u32[]{:S(2)}) collective-permute-start(f32[2,1584,128]{2,1,0:T(8,128)S(1)} %slice.8), channel_id=1, source_target_pairs={{0,3},{1,0},{2,1},{3,2},{4,7},{5,4},{6,5},{7,6},{8,11},{9,8},{10,9... | collective-permute-start | bytes 4866056 | tf_op jit(solution)/shard_map/ppermute | solution.py:37
  139.7 1.5 copy-done.12
  141.2 21.5 %shard_map.41 = (bf16[1536,1152]{1,0:T(8,128)(2,1)}, bf16[1536,1152]{1,0:T(8,128)(2,1)}, f32[2304,1152]{1,0:T(8,128)}) custom-call(s32[4]{0:T(128)S(1)} %pad_add_fusion.pos, f32[6,64,512]{2,1,0:T(8,128)S(1)} %shard_map.36.m0, f32[6,64,512]{2,1,0:T(8,128)S(1)} %collective-permute-done.13.mc, f32[3,6,64,512]{3,2,1,0:T(8,128)S(1)} %shard_map.38.mown, ...), custom_call_target="tpu_custom_call" | custom-call | flops 10871635968 | bytes 20000000 | tf_op jit(solution)/shard_map/pallas_call | solution.py:427
  162.7 1.1 copy-done.13
  163.9 0.6 copy-done.14
  164.5 35.3 %shard_map.42 = f32[2304,1152]{1,0:T(8,128)} custom-call(bf16[4,528,384]{2,1,0:T(8,128)(2,1)} %copy-done.4, bf16[4,528,384]{2,1,0:T(8,128)(2,1)} %copy-done.6, bf16[4,528,384]{2,1,0:T(8,128)(2,1)} %copy-done.5, bf16[4,528,384]{2,1,0:T(8,128)(2,1)} %copy-done.9, bf16[4,528,384]{2,1,0:T(8,128)(2,1)} %copy-done.11, ...), custom_call_target="tpu_custom_call", output_to_operand_aliasing={{}: (11, {})} | custom-call | flops 22422749184 | bytes 30000000 | tf_op jit(solution)/shard_map/pallas_call | solution.py:310
  (40 shorter events, 0.6 us)
Async XLA Ops:
  2.1 2.7 %collective-permute-start.4 = (f32[3,64,1152]{2,1,0:T(8,128)}, f32[3,64,1152]{2,1,0:T(8,128)S(1)}, u32[]{:S(2)}, u32[]{:S(2)}) collective-permute-start(f32[3,64,1152]{2,1,0:T(8,128)} %shard_map.30.refs_0_.b0), channel_id=1, source_target_pairs={{0,16},{1,17},{2,18},{3,19},{4,20},{5,21},{6,22},{7,23},{8,24},{9,... | collective-permute-start | bytes 2654216 | tf_op jit(solution)/shard_map/ppermute | solution.py:37
  3.7 1.2 copy-start.2
  5.3 0.9 copy-start.7
  6.2 30.2 %collective-permute-start.5 = (f32[2,3,64,1152]{3,2,1,0:T(8,128)S(1)}, f32[2,3,64,1152]{3,2,1,0:T(8,128)S(1)}, u32[]{:S(2)}, u32[]{:S(2)}) collective-permute-start(f32[2,3,64,1152]{3,2,1,0:T(8,128)S(1)} %shard_map.31), channel_id=1, source_target_pairs={{0,96},{1,97},{2,98},{3,99},{4,100},{5,101},{6,102},{7,103},{8,104... | collective-permute-start | bytes 5308424 | tf_op jit(solution)/shard_map/ppermute | solution.py:37
  9.3 14.2 %collective-permute-start.1 = (f32[1712,128]{1,0:T(8,128)S(1)}, f32[1712,128]{1,0:T(8,128)S(1)}, u32[]{:S(2)}, u32[]{:S(2)}) collective-permute-start(f32[1712,128]{1,0:T(8,128)S(1)} %shard_map.28.refs_2_.refs_0_), channel_id=1, source_target_pairs={{0,4},{1,5},{2,6},{3,7},{4,8},{5,9},{6,10},{7,11},{8,12},{9,13},{1... | collective-permute-start | bytes 2629640 | tf_op jit(solution)/shard_map/ppermute | solution.py:37
  10.8 13.0 %collective-permute-start = (f32[1712,128]{1,0:T(8,128)S(1)}, f32[1712,128]{1,0:T(8,128)S(1)}, u32[]{:S(2)}, u32[]{:S(2)}) collective-permute-start(f32[1712,128]{1,0:T(8,128)S(1)} %shard_map.28.refs_2_.refs_0_), channel_id=1, source_target_pairs={{0,12},{1,13},{2,14},{3,15},{4,0},{5,1},{6,2},{7,3},{8,4},{9,5},{1... | collective-permute-start | bytes 2629640 | tf_op jit(solution)/shard_map/ppermute | solution.py:37
  24.3 12.1 %collective-permute-start.2 = (f32[920,128]{1,0:T(8,128)S(1)}, f32[920,128]{1,0:T(8,128)S(1)}, u32[]{:S(2)}, u32[]{:S(2)}) collective-permute-start(f32[920,128]{1,0:T(8,128)S(1)} %get-tuple-element.18), channel_id=1, source_target_pairs={{0,12},{1,13},{2,14},{3,15},{4,0},{5,1},{6,2},{7,3},{8,4},{9,5},{1... | collective-permute-start | bytes 1413128 | tf_op jit(solution)/shard_map/ppermute | solution.py:37
  27.3 9.1 %collective-permute-start.3 = (f32[792,128]{1,0:T(8,128)S(1)}, f32[792,128]{1,0:T(8,128)S(1)}, u32[]{:S(2)}, u32[]{:S(2)}) collective-permute-start(f32[792,128]{1,0:T(8,128)S(1)} %get-tuple-element.19), channel_id=1, source_target_pairs={{0,4},{1,5},{2,6},{3,7},{4,8},{5,9},{6,10},{7,11},{8,12},{9,13},{1... | collective-permute-start | bytes 1216520 | tf_op jit(solution)/shard_map/ppermute | solution.py:37
  36.4 2.8 %copy-start = (f32[2,3,64,1152]{3,2,1,0:T(8,128)}, f32[2,3,64,1152]{3,2,1,0:T(8,128)S(1)}, u32[]{:S(2)}) copy-start(f32[2,3,64,1152]{3,2,1,0:T(8,128)S(1)} %collective-permute-done.5.refs_5_.refs_0_) | copy-start | bytes 5308420
  39.2 74.2 %collective-permute-start.7 = (f32[4,1584,128]{2,1,0:T(8,128)}, f32[4,1584,128]{2,1,0:T(8,128)}, u32[]{:S(2)}, u32[]{:S(2)}) collective-permute-start(f32[4,1584,128]{2,1,0:T(8,128)} %get-tuple-element.20), channel_id=1, source_target_pairs={{0,1},{1,2},{2,3},{3,0},{4,5},{5,6},{6,7},{7,4},{8,9},{9,10},{10,1... | collective-permute-start | bytes 9732104 | tf_op jit(solution)/shard_map/ppermute | solution.py:37
  41.2 72.2 %collective-permute-start.6 = (f32[4,1584,128]{2,1,0:T(8,128)}, f32[4,1584,128]{2,1,0:T(8,128)S(1)}, u32[]{:S(2)}, u32[]{:S(2)}) collective-permute-start(f32[4,1584,128]{2,1,0:T(8,128)} %get-tuple-element.20), channel_id=1, source_target_pairs={{0,3},{1,0},{2,1},{3,2},{4,7},{5,4},{6,5},{7,6},{8,11},{9,8},{10,9... | collective-permute-start | bytes 9732104 | tf_op jit(solution)/shard_map/ppermute | solution.py:37
  43.4 39.3 %collective-permute-start.12 = (f32[4,128,128]{2,1,0:T(8,128)S(1)}, f32[4,128,128]{2,1,0:T(8,128)}, u32[]{:S(2)}, u32[]{:S(2)}) collective-permute-start(f32[4,128,128]{2,1,0:T(8,128)S(1)} %get-tuple-element.27.g0), channel_id=1, source_target_pairs={{0,1},{1,2},{2,3},{3,0},{4,5},{5,6},{6,7},{7,4},{8,9},{9,10},{10,1... | collective-permute-start | bytes 786440 | tf_op jit(solution)/shard_map/ppermute | solution.py:37
  43.4 43.6 %collective-permute-start.11 = (f32[4,128,128]{2,1,0:T(8,128)S(1)}, f32[4,128,128]{2,1,0:T(8,128)}, u32[]{:S(2)}, u32[]{:S(2)}) collective-permute-start(f32[4,128,128]{2,1,0:T(8,128)S(1)} %get-tuple-element.27.g0), channel_id=1, source_target_pairs={{0,2},{1,3},{2,0},{3,1},{4,6},{5,7},{6,4},{7,5},{8,10},{9,11},{10,... | collective-permute-start | bytes 786440 | tf_op jit(solution)/shard_map/ppermute | solution.py:37
  46.8 40.2 %collective-permute-start.10 = (f32[4,128,128]{2,1,0:T(8,128)S(1)}, f32[4,128,128]{2,1,0:T(8,128)}, u32[]{:S(2)}, u32[]{:S(2)}) collective-permute-start(f32[4,128,128]{2,1,0:T(8,128)S(1)} %get-tuple-element.27.g0), channel_id=1, source_target_pairs={{0,3},{1,0},{2,1},{3,2},{4,7},{5,4},{6,5},{7,6},{8,11},{9,8},{10,9... | collective-permute-start | bytes 786440 | tf_op jit(solution)/shard_map/ppermute | solution.py:37
  90.4 3.3 %copy-start.1 = (f32[2,3,64,1152]{3,2,1,0:T(8,128)S(1)}, f32[2,3,64,1152]{3,2,1,0:T(8,128)}, u32[]{:S(2)}) copy-start(f32[2,3,64,1152]{3,2,1,0:T(8,128)} %copy-done) | copy-start | bytes 5308420
  90.5 2.4 %collective-permute-start.13 = (f32[6,64,512]{2,1,0:T(8,128)S(1)}, f32[6,64,512]{2,1,0:T(8,128)S(1)}, u32[]{:S(2)}, u32[]{:S(2)}) collective-permute-start(f32[6,64,512]{2,1,0:T(8,128)S(1)} %shard_map.36.m0), channel_id=1, source_target_pairs={{0,16},{1,17},{2,18},{3,19},{4,20},{5,21},{6,22},{7,23},{8,24},{9,... | collective-permute-start | bytes 2359304 | tf_op jit(solution)/shard_map/ppermute | solution.py:37
  92.9 20.5 %collective-permute-start.14 = (f32[2,6,64,512]{3,2,1,0:T(8,128)S(1)}, f32[2,6,64,512]{3,2,1,0:T(8,128)S(1)}, u32[]{:S(2)}, u32[]{:S(2)}) collective-permute-start(f32[2,6,64,512]{3,2,1,0:T(8,128)S(1)} %pad_maximum_fusion), channel_id=1, source_target_pairs={{0,96},{1,97},{2,98},{3,99},{4,100},{5,101},{6,102},{7,103},{8,104... | collective-permute-start | bytes 4718600 | tf_op jit(solution)/shard_map/ppermute | solution.py:37
  94.0 29.0 %collective-permute-start.17 = (f32[1,3,64,1152]{3,2,1,0:T(8,128)S(1)}, f32[1,3,64,1152]{3,2,1,0:T(8,128)S(1)}, u32[]{:S(2)}, u32[]{:S(2)}) collective-permute-start(f32[1,3,64,1152]{3,2,1,0:T(8,128)S(1)} %shard_map.39), channel_id=1, source_target_pairs={{0,96},{1,97},{2,98},{3,99},{4,100},{5,101},{6,102},{7,103},{8,104... | collective-permute-start | bytes 2654216 | tf_op jit(solution)/shard_map/ppermute | solution.py:37
  98.6 14.9 %copy-start.4 = (bf16[4,528,384]{2,1,0:T(8,128)(2,1)}, bf16[4,528,384]{2,1,0:T(8,128)(2,1)S(1)}, u32[]{:S(2)}) copy-start(bf16[4,528,384]{2,1,0:T(8,128)(2,1)S(1)} %get-tuple-element.21.refs_3_.refs_0_) | copy-start | bytes 4866052
  98.6 14.9 %copy-start.9 = (bf16[4,528,384]{2,1,0:T(8,128)(2,1)}, bf16[4,528,384]{2,1,0:T(8,128)(2,1)S(1)}, u32[]{:S(2)}) copy-start(bf16[4,528,384]{2,1,0:T(8,128)(2,1)S(1)} %get-tuple-element.24.refs_3_) | copy-start | bytes 4866052
  113.5 19.3 %collective-permute-start.15 = (f32[1,6,64,512]{3,2,1,0:T(8,128)S(1)}, f32[1,6,64,512]{3,2,1,0:T(8,128)S(1)}, u32[]{:S(2)}, u32[]{:S(2)}) collective-permute-start(f32[1,6,64,512]{3,2,1,0:T(8,128)S(1)} %shard_map.37), channel_id=1, source_target_pairs={{0,96},{1,97},{2,98},{3,99},{4,100},{5,101},{6,102},{7,103},{8,104... | collective-permute-start | bytes 2359304 | tf_op jit(solution)/shard_map/ppermute | solution.py:37
  123.5 16.2 %collective-permute-start.18 = (f32[3,3,64,1152]{3,2,1,0:T(8,128)S(1)}, f32[3,3,64,1152]{3,2,1,0:T(8,128)S(1)}, u32[]{:S(2)}, u32[]{:S(2)}) collective-permute-start(f32[3,3,64,1152]{3,2,1,0:T(8,128)S(1)} %shard_map.40.bown), channel_id=1, source_target_pairs={{0,16},{1,17},{2,18},{3,19},{4,20},{5,21},{6,22},{7,23},{8,24},{9,... | collective-permute-start | bytes 7962632 | tf_op jit(solution)/shard_map/ppermute | solution.py:37
  127.8 1.2 copy-start.10
  129.0 3.8 %copy-start.5 = (bf16[4,528,384]{2,1,0:T(8,128)(2,1)}, bf16[4,528,384]{2,1,0:T(8,128)(2,1)S(1)}, u32[]{:S(2)}) copy-start(bf16[4,528,384]{2,1,0:T(8,128)(2,1)S(1)} %get-tuple-element.23.refs_3_.refs_2_) | copy-start | bytes 4866052
  131.7 1.2 copy-start.11
  132.9 1.3 copy-start.6
  134.1 7.1 %collective-permute-start.16 = (f32[3,6,64,512]{3,2,1,0:T(8,128)S(1)}, f32[3,6,64,512]{3,2,1,0:T(8,128)S(1)}, u32[]{:S(2)}, u32[]{:S(2)}) collective-permute-start(f32[3,6,64,512]{3,2,1,0:T(8,128)S(1)} %shard_map.38.mown), channel_id=1, source_target_pairs={{0,16},{1,17},{2,18},{3,19},{4,20},{5,21},{6,22},{7,23},{8,24},{9,... | collective-permute-start | bytes 7077896 | tf_op jit(solution)/shard_map/ppermute | solution.py:37
  136.0 5.2 %copy-start.3 = (f32[3,64,1152]{2,1,0:T(8,128)S(1)}, f32[3,64,1152]{2,1,0:T(8,128)}, u32[]{:S(2)}) copy-start(f32[3,64,1152]{2,1,0:T(8,128)} %shard_map.30.refs_0_.b0) | copy-start | bytes 2654212
  136.0 5.2 %copy-start.8 = (f32[3,64,1152]{2,1,0:T(8,128)S(1)}, f32[3,64,1152]{2,1,0:T(8,128)}, u32[]{:S(2)}) copy-start(f32[3,64,1152]{2,1,0:T(8,128)} %copy-done.7) | copy-start | bytes 2654212
  136.0 26.7 %collective-permute-start.9 = (f32[2,1584,128]{2,1,0:T(8,128)S(1)}, f32[2,1584,128]{2,1,0:T(8,128)S(1)}, u32[]{:S(2)}, u32[]{:S(2)}) collective-permute-start(f32[2,1584,128]{2,1,0:T(8,128)S(1)} %slice.9), channel_id=1, source_target_pairs={{0,1},{1,2},{2,3},{3,0},{4,5},{5,6},{6,7},{7,4},{8,9},{9,10},{10,1... | collective-permute-start | bytes 4866056 | tf_op jit(solution)/shard_map/ppermute | solution.py:37
  136.7 26.0 %collective-permute-start.8 = (f32[2,1584,128]{2,1,0:T(8,128)S(1)}, f32[2,1584,128]{2,1,0:T(8,128)S(1)}, u32[]{:S(2)}, u32[]{:S(2)}) collective-permute-start(f32[2,1584,128]{2,1,0:T(8,128)S(1)} %slice.8), channel_id=1, source_target_pairs={{0,3},{1,0},{2,1},{3,2},{4,7},{5,4},{6,5},{7,6},{8,11},{9,8},{10,9... | collective-permute-start | bytes 4866056 | tf_op jit(solution)/shard_map/ppermute | solution.py:37
  139.7 1.6 copy-start.12
  162.7 1.2 copy-start.13
  162.7 1.8 copy-start.14

commit v4 on v3

--- a/solution.py
+++ b/solution.py
@@ -53,9 +53,9 @@
     return joint(v, lambda y, c, x, z: (y, 1 - c, x, z))
 
 
-def pack_kernel(f_ref, l_ref):
-    for p in range(PANELS):
-        l_ref[WR + p * GR : WR + (p + 1) * GR, :] = jnp.concatenate(
+def pack_kernel(f_ref, l_ref, w_ref):
+    for p in range(PANELS):
+        l_ref[p * GR : (p + 1) * GR, :] = jnp.concatenate(
             [
                 f_ref[WIN + g * GR : WIN + (g + 1) * GR, p * CB : (p + 1) * CB]
                 for g in range(GROUPS)
@@ -66,9 +66,9 @@
     def block(i, j):
         return f_ref[i * PB : (i + 1) * PB, j * CB : (j + 1) * CB]
 
-    l_ref[0:PB, :] = jnp.concatenate([block(0, 0), block(1, 1), block(2, 2), block(1, 0)], axis=1)
+    w_ref[0:PB, :] = jnp.concatenate([block(0, 0), block(1, 1), block(2, 2), block(1, 0)], axis=1)
     zero = jnp.zeros((PB, CB), F32)
-    l_ref[PB:WR, :] = jnp.concatenate([block(2, 0), block(2, 1), zero, zero], axis=1)
+    w_ref[PB:WR, :] = jnp.concatenate([block(2, 0), block(2, 1), zero, zero], axis=1)
 
 
 def source(pos, i, j):
@@ -78,7 +78,7 @@
     return xs * NZ + zs
 
 
-def rows_kernel(pos, g0, g1, g2, g3, out, canon, diag):
+def rows_kernel(pos, g0, g1, g2, g3, _after, out, canon, diag):
     y, core = pos[0], pos[1]
     for i, ref in enumerate((g0, g1, g2, g3)):
         for j in range(4):
@@ -251,12 +251,18 @@
             lh[g, rows, k], ll[g, rows, k] = split(v[g])
 
 
-def assemble_kernel(q, lh, ll):
-    lanes_in_order(lambda j, p: q[j, p], pl.ds(0, CHUNK), lh, ll)
+def assemble_kernel(q, *refs):
+    lanes_in_order(lambda j, p: q[j, p], pl.ds(0, CHUNK), *refs[-2:])
 
 
 def update_kernel(*refs):
-    his, los, (qa, qb, xh, xl, r_ref, _base, out, lh, ll) = refs[:3], refs[3:6], refs[6:]
+    his, los, (xh, xl, r_ref, _base, out) = refs[:3], refs[3:6], refs[6:]
+    a = [jnp.concatenate([v[...] for v in part], axis=1) for part in (his, los)]
+    for w in COLS:
+        out[:, w] = r_ref[:, w] - dot3(a, (xh[:, w], xl[:, w]))
+
+
+def update_last_kernel(qa, qb, xh, xl, r_ref, out, lh, ll):
     g = pl.program_id(0)
 
     @pl.when(g == 0)
@@ -266,12 +272,8 @@
             rows = pl.ds(pl.multiple_of(i * CHUNK, 16), CHUNK)
             lanes_in_order(lambda j, p: (qa, qb)[j // 2][j % 2, p, rows, :], rows, lh, ll)
 
-    a = [
-        jnp.concatenate([v[...] for v in part] + [last[g]], axis=1)
-        for part, last in ((his, lh), (los, ll))
-    ]
     for w in COLS:
-        out[:, w] = r_ref[:, w] - dot3(a, (xh[:, w], xl[:, w]))
+        out[:, w] = r_ref[:, w] - dot3((lh[g], ll[g]), (xh[:, w], xl[:, w]))
 
 
 VM = pl.BlockSpec(memory_space=pltpu.VMEM)
@@ -288,36 +290,54 @@
     return pl.CostEstimate(flops=int(flops), bytes_accessed=int(moved), transcendentals=0)
 
 
-def assemble(q):
+def assemble(q, *after):
     out = jax.ShapeDtypeStruct((GROUPS, GR, SUB), BF16)
     spec = pl.BlockSpec((GROUPS, CHUNK, SUB), lambda i: (0, i, 0))
     return pl.pallas_call(
         assemble_kernel,
         grid=(GR // CHUNK,),
         out_shape=(out, out),
-        in_specs=[pl.BlockSpec((4, PANELS, CHUNK, 128), lambda i: (0, 0, i, 0))],
+        in_specs=[pl.BlockSpec((4, PANELS, CHUNK, 128), lambda i: (0, 0, i, 0))]
+        + [ANY] * len(after),
         out_specs=(spec, spec),
         compiler_params=params(12),
         cost_estimate=cost(4e6, 7e6),
-    )(q.reshape(4, PANELS, GR, 128))
-
-
-def update(rows_in, base, parts, last, xh, xl):
-    strip = pl.BlockSpec(
-        (pl.Element(GR), pl.Element(NCOL)), lambda g: (pl.multiple_of(WIN + g * GR, 16), 0)
-    )
+    )(q.reshape(4, PANELS, GR, 128), *after)
+
+
+STRIP = pl.BlockSpec(
+    (pl.Element(GR), pl.Element(NCOL)), lambda g: (pl.multiple_of(WIN + g * GR, 16), 0)
+)
+
+
+def update(rows_in, base, parts, xh, xl):
     spec = pl.BlockSpec((None, GR, SUB), lambda g: (g, 0, 0))
+    xs = pl.BlockSpec((3 * SUB, NCOL), lambda g: (0, 0))
     return pl.pallas_call(
         update_kernel,
         grid=(GROUPS,),
         out_shape=jax.ShapeDtypeStruct((ROWS, NCOL), F32),
-        in_specs=[spec] * 6 + [VM] * 4 + [strip, ANY],
-        out_specs=strip,
+        in_specs=[spec] * 6 + [xs, xs, STRIP, ANY],
+        out_specs=STRIP,
+        input_output_aliases={9: 0},
+        compiler_params=params(48),
+        cost_estimate=cost(6 * TRAIL * 3 * SUB * NCOL, 30e6),
+    )(*[v[0] for v in parts], *[v[1] for v in parts], xh, xl, rows_in, base)
+
+
+def update_last(base, last, xh, xl):
+    xs = pl.BlockSpec((SUB, NCOL), lambda g: (3, 0))
+    return pl.pallas_call(
+        update_last_kernel,
+        grid=(GROUPS,),
+        out_shape=jax.ShapeDtypeStruct((ROWS, NCOL), F32),
+        in_specs=[VM, VM, xs, xs, STRIP],
+        out_specs=STRIP,
         scratch_shapes=[pltpu.VMEM((GROUPS, GR, SUB), BF16)] * 2,
-        input_output_aliases={11: 0},
-        compiler_params=params(57),
-        cost_estimate=cost(6 * TRAIL * DEPTH * NCOL, 30e6),
-    )(*[v[0] for v in parts], *[v[1] for v in parts], *[v.reshape(2, PANELS, GR, 128) for v in last], xh, xl, rows_in, base)
+        input_output_aliases={4: 0},
+        compiler_params=params(48),
+        cost_estimate=cost(6 * TRAIL * SUB * NCOL, 25e6),
+    )(*[v.reshape(2, PANELS, GR, 128) for v in last], xh, xl, base)
 
 
 def moved(arrays, shapes, plan, limit):
@@ -360,11 +380,14 @@
     row_i, col_i = lax.axis_index("row"), lax.axis_index("col")
     pos = jnp.stack([row_i // 2, row_i % 2, col_i // NZ, col_i % NZ]).astype(jnp.int32)
 
-    packed = pl.pallas_call(
+    packed, w = pl.pallas_call(
         pack_kernel,
-        out_shape=jax.ShapeDtypeStruct((WR + PANELS * GR, 128), F32),
+        out_shape=(
+            jax.ShapeDtypeStruct((PANELS * GR, 128), F32),
+            jax.ShapeDtypeStruct((WR, 128), F32),
+        ),
         in_specs=[VM],
-        out_specs=VM,
+        out_specs=(VM, VM),
         compiler_params=params(8),
     )(factor)
     rows3 = (PANELS, PB, NCOL)
@@ -378,50 +401,54 @@
     (bpair,) = moved((b0, bc, packed), [(2, *rows3)], [(0, None, 0, 0), (1, None, 0, 1)], 8)
     bhop = along_y(bpair)
 
+    (w1,) = moved(
+        (w, *[from_first(w, d) for d in (1, 2, 3)], bpair),
+        [(4, WR, 128)],
+        [(j, None, 0, j) for j in range(4)],
+        8,
+    )
+    groups = [w1] + [from_second(w1, d) for d in (1, 2, 3)]
+
+    total = PANELS * GR
+    h = total // 2
+    (packed,) = moved((packed, *groups[1:]), [(total, 128)], [(0, None, 0, None)], 8)
     u1, u3 = from_first(packed, 1), from_first(packed, 3)
-    total = WR + PANELS * GR
-    h = WR + PANELS * GR // 2
     f1, f3 = moved(
         (u1, u3),
-        [(h, 128), (total - h, 128)],
-        [(0, pl.ds(0, h), 0, None), (1, pl.ds(h, total - h), 1, None)],
+        [(h, 128), (h, 128)],
+        [(0, pl.ds(0, h), 0, None), (1, pl.ds(h, h), 1, None)],
         8,
     )
     o1, o3 = from_first(f1, 1), from_first(f3, 3)
-
-    half = h - WR
-    w1, q0 = moved(
-        (packed, u1, o1, u3, o3, bhop),
-        [(4, WR, 128), (4, total - WR, 128)],
-        [(j, pl.ds(0, WR), 0, j) for j in range(4)]
-        + [(j, pl.ds(WR, total - WR), 1, j) for j in (0, 1, 3)]
-        + [
-            (2, pl.ds(WR, half), 1, (2, pl.ds(0, half))),
-            (4, None, 1, (2, pl.ds(half, half))),
+    (q0,) = moved(
+        (packed, u1, o1, u3, o3),
+        [(4, total, 128)],
+        [
+            (0, None, 0, 0),
+            (1, None, 0, 1),
+            (2, None, 0, (2, pl.ds(0, h))),
+            (3, None, 0, 3),
+            (4, None, 0, (2, pl.ds(h, h))),
         ],
         16,
     )
-    groups = [w1] + [from_second(w1, d) for d in (1, 2, 3)]
     q1, q3 = from_second(q0, 1), from_second(q0, 3)
-    q2 = (from_second(q1[:2], 1), from_second(q3[2:], 3))
 
     mine = pl.pallas_call(
         rows_kernel,
         out_shape=jax.ShapeDtypeStruct((SLOTS, PB, PANEL), F32),
-        in_specs=[SM] + [VM] * 4,
+        in_specs=[SM] + [VM] * 4 + [ANY],
         out_specs=VM,
         scratch_shapes=[
             pltpu.VMEM((16, 2 * PB, 128), F32),
             pltpu.VMEM((PANELS, NX, PB, 128), F32),
         ],
         compiler_params=params(8),
-    )(pos, *groups)
-
-    parts = [assemble(q0), assemble(q1), assemble(q3)]
+    )(pos, *groups, bhop)
+
     mc = from_core(mine)
-    early = (q1, q3, parts[0][0])
-    late = (parts[1][0], parts[2][0])
-    rows = (mine, mc, *second_hop(along_y(jnp.stack([mine, mc])), early, late))
+    first = assemble(q0)
+    rows = (mine, mc, *second_hop(along_y(jnp.stack([mine, mc])), late=(first[0],)))
     rhs_rows = (b0, bc, *second_hop(bhop))
 
     xh, xl, base = pl.pallas_call(
@@ -447,10 +474,19 @@
             pltpu.SemaphoreType.DMA,
         ],
         compiler_params=params(42),
-        cost_estimate=cost(36 * PANEL * PANEL * NCOL, 20e6),
+        cost_estimate=cost(1e6, 1e6),
     )(pos, *rows, *rhs_rows)
 
-    return update(rhs_tile, base, parts, q2, xh, xl)
+    f1, f3 = moved(
+        (q1, q3, xh),
+        [(2, total, 128), (2, total, 128)],
+        [(0, pl.ds(0, 2), 0, None), (1, pl.ds(2, 2), 1, None)],
+        16,
+    )
+    q2 = (from_second(f1, 1), from_second(f3, 3))
+    parts = [first, assemble(q1, xh), assemble(q3, xh)]
+    base = update(rhs_tile, base, parts, xh, xl)
+    return update_last(base, q2, xh, xl)
 
 
 def solution(mesh):

time: 201 us -> 170 us (0.85)
  waiting for transfers between devices: 84.3 us -> 40.4 us
  Pallas kernels: 78.5 us -> 85 us
  starting transfers between devices: 25.6 us -> 30.7 us
    ppermute x19 -> x22, waiting for transfers between devices: 84.3 us -> 40.4 us  [joint(): return lax.ppermute(v, ('row', 'col'), pairs)]
    pallas_call x1 -> x2, Pallas kernels: 0.72 us -> 15 us  [the longest x1 14.3 us: update_last(): pl.pallas_call(update_last_kernel, grid=(GROUPS,), out_shape=jax.ShapeDty...]
    pallas_call x1, Pallas kernels: 35.3 us -> 25.7 us  [update(): pl.pallas_call(update_kernel, grid=(GROUPS,), out_shape=jax.ShapeDtypeStr...]
    ppermute x19 -> x22, starting transfers between devices: 25.6 us -> 30.7 us  [joint(): return lax.ppermute(v, ('row', 'col'), pairs)]
    unnamed x31 -> x33, local copies, waits for them, and re-layouts: 9.3 us -> 12.5 us
    pallas_call x8 -> x11, Pallas kernels: 6.75 us -> 9.06 us  [moved(): pl.pallas_call(kernel, out_shape=[jax.ShapeDtypeStruct(v, F32) for v in s...]
  transfers between devices with their start and end apart: 19 -> 22, of which waited for: 9 -> 12; matrix products, arithmetic and copies ran while one was open for 2% -> 1% of each run, Pallas kernels for 19% -> 37%
where the time goes in v4:
time: 170 us; the launch traced here: 169 us
  Pallas kernels  85 us (50%)
  waiting for transfers between devices  40.4 us (24%)
  starting transfers between devices  30.7 us (18%)
  local copies, waits for them, and re-layouts  12.5 us (7%)
    ppermute x22, waiting for transfers between devices, joint(): return lax.ppermute(v, ('row', 'col'), pairs)  40.4 us
    ppermute x22, starting transfers between devices, joint(): return lax.ppermute(v, ('row', 'col'), pairs)  30.7 us
    pallas_call x1, Pallas kernels, update(): pl.pallas_call(update_kernel, grid=(GROUPS,), out_shape=jax.ShapeDtypeStr...  25.7 us
    pallas_call x1, Pallas kernels, local(): pl.pallas_call(solve_kernel, out_shape=(jax.ShapeDtypeStruct((DEPTH, NCOL...  21.6 us
    pallas_call x1, Pallas kernels, update_last(): pl.pallas_call(update_last_kernel, grid=(GROUPS,), out_shape=jax.ShapeDty...  14.3 us
    unnamed x33, local copies, waits for them, and re-layouts  12.5 us
    pallas_call x3, Pallas kernels, assemble(): pl.pallas_call(assemble_kernel, grid=(GR // CHUNK,), out_shape=(out, out)...  10.2 us
    pallas_call x11, Pallas kernels, moved(): pl.pallas_call(kernel, out_shape=[jax.ShapeDtypeStruct(v, F32) for v in s...  9.06 us
  transfers between devices with their start and end apart: 22, of which 12 were waited for; matrix products, arithmetic and copies ran while one was open for 1% of the time, Pallas kernels for 37%

profile of v4, /device:TPU:0, one launch (start us, length us, event | category | flops | bytes accessed | tf_op | source)
XLA Modules:
  0.0 169.2 jit_solution(6763542074504598493)
XLA Ops:
  0.0 2.1 %shard_map.29.refs_0_.b0 = f32[3,64,1152]{2,1,0:T(8,128)} custom-call(f32[2304,1152]{1,0:T(8,128)} %refs_8_.1), custom_call_target="tpu_custom_call" | custom-call | tf_op jit(solution)/shard_map/pallas_call | solution.py:357
  2.2 1.6 copy.5.f_ref
  3.8 0.7 shard_map.28
  4.5 0.3 collective-permute-done.3.refs_1_.bc
  4.8 1.6 shard_map.30.refs_4_
  6.4 3.2 %collective-permute-start.13 = (f32[2,3,64,1152]{3,2,1,0:T(8,128)}, f32[2,3,64,1152]{3,2,1,0:T(8,128)S(1)}, u32[]{:S(2)}, u32[]{:S(2)}) collective-permute-start(f32[2,3,64,1152]{3,2,1,0:T(8,128)} %shard_map.30.refs_4_), channel_id=1, source_target_pairs={{0,96},{1,97},{2,98},{3,99},{4,100},{5,101},{6,102},{7,103},{8,104... | collective-permute-start | bytes 5308424 | tf_op jit(solution)/shard_map/ppermute | solution.py:37
  9.6 1.5 collective-permute-start.2
  11.1 2.7 %collective-permute-start.1 = (f32[128,128]{1,0:T(8,128)S(1)}, f32[128,128]{1,0:T(8,128)S(1)}, u32[]{:S(2)}, u32[]{:S(2)}) collective-permute-start(f32[128,128]{1,0:T(8,128)S(1)} %get-tuple-element.21.refs_0_), channel_id=1, source_target_pairs={{0,8},{1,9},{2,10},{3,11},{4,12},{5,13},{6,14},{7,15},{8,0},{9,1},... | collective-permute-start | bytes 196616 | tf_op jit(solution)/shard_map/ppermute | solution.py:37
  13.8 1.4 collective-permute-start
  15.2 1.6 collective-permute-done.1.refs_2_
  16.8 1.2 collective-permute-done.refs_1_
  18.1 1.1 shard_map.31.g0
  19.1 2.0 %collective-permute-start.6 = (f32[4,128,128]{2,1,0:T(8,128)}, f32[4,128,128]{2,1,0:T(8,128)}, u32[]{:S(2)}, u32[]{:S(2)}) collective-permute-start(f32[4,128,128]{2,1,0:T(8,128)} %shard_map.31.g0), channel_id=1, source_target_pairs={{0,1},{1,2},{2,3},{3,0},{4,5},{5,6},{6,7},{7,4},{8,9},{9,10},{10,1... | collective-permute-start | bytes 786440 | tf_op jit(solution)/shard_map/ppermute | solution.py:37
  21.1 3.6 %collective-permute-start.5 = (f32[4,128,128]{2,1,0:T(8,128)}, f32[4,128,128]{2,1,0:T(8,128)}, u32[]{:S(2)}, u32[]{:S(2)}) collective-permute-start(f32[4,128,128]{2,1,0:T(8,128)} %shard_map.31.g0), channel_id=1, source_target_pairs={{0,2},{1,3},{2,0},{3,1},{4,6},{5,7},{6,4},{7,5},{8,10},{9,11},{10,... | collective-permute-start | bytes 786440 | tf_op jit(solution)/shard_map/ppermute | solution.py:37
  24.7 1.0 collective-permute-start.4
  25.8 2.1 %collective-permute-done.6.refs_3_.g3 = f32[4,128,128]{2,1,0:T(8,128)} collective-permute-done((f32[4,128,128]{2,1,0:T(8,128)}, f32[4,128,128]{2,1,0:T(8,128)}, u32[]{:S(2)}, u32[]{:S(2)}) %collective-permute-start.6) | collective-permute-done | bytes 262176 | tf_op jit(solution)/shard_map/ppermute | solution.py:37
  27.9 4.3 %collective-permute-done.5.refs_2_.g2 = f32[4,128,128]{2,1,0:T(8,128)} collective-permute-done((f32[4,128,128]{2,1,0:T(8,128)}, f32[4,128,128]{2,1,0:T(8,128)}, u32[]{:S(2)}, u32[]{:S(2)}) %collective-permute-start.5) | collective-permute-done | bytes 262176 | tf_op jit(solution)/shard_map/ppermute | solution.py:37
  32.2 3.5 %shard_map.35.m0 = f32[6,64,512]{2,1,0:T(8,128)S(1)} custom-call(s32[4]{0:T(128)S(1)} %pad_add_fusion.pos, f32[4,128,128]{2,1,0:T(8,128)} %shard_map.31.g0, f32[4,128,128]{2,1,0:T(8,128)} %collective-permute-done.4.refs_1_.g1, f32[4,128,128]{2,1,0:T(8,128)} %collective-permute-done.5.refs_2_.g2, f32[4,128,128]{2,1,0:T(8,128)} %collective-permute-done.6.refs_3_.g3, ...), custom_call_target="tpu_custom_call" | custom-call | tf_op jit(solution)/shard_map/pallas_call | solution.py:437
  35.8 2.3 %collective-permute-done.14.mc = f32[6,64,512]{2,1,0:T(8,128)S(1)} collective-permute-done((f32[6,64,512]{2,1,0:T(8,128)S(1)}, f32[6,64,512]{2,1,0:T(8,128)S(1)}, u32[]{:S(2)}, u32[]{:S(2)}) %collective-permute-start.14) | collective-permute-done | bytes 786464 | tf_op jit(solution)/shard_map/ppermute | solution.py:37
  38.2 1.4 collective-permute-start.15
  39.7 1.6 collective-permute-start.8
  41.3 1.7 %collective-permute-start.7 = (f32[1584,128]{1,0:T(8,128)S(1)}, f32[1584,128]{1,0:T(8,128)S(1)}, u32[]{:S(2)}, u32[]{:S(2)}) collective-permute-start(f32[1584,128]{1,0:T(8,128)S(1)} %shard_map.32.refs_0_), channel_id=1, source_target_pairs={{0,12},{1,13},{2,14},{3,15},{4,0},{5,1},{6,2},{7,3},{8,4},{9,5},{1... | collective-permute-start | bytes 2433032 | tf_op jit(solution)/shard_map/ppermute | solution.py:37
  43.0 10.2 %collective-permute-done.8.refs_1_.refs_3_ = f32[1584,128]{1,0:T(8,128)S(1)} collective-permute-done((f32[1584,128]{1,0:T(8,128)S(1)}, f32[1584,128]{1,0:T(8,128)S(1)}, u32[]{:S(2)}, u32[]{:S(2)}) %collective-permute-start.8) | collective-permute-done | bytes 811040 | tf_op jit(solution)/shard_map/ppermute | solution.py:37
  53.5 0.4 shard_map.33
  53.9 3.0 %collective-permute-start.9 = (f32[792,128]{1,0:T(8,128)S(1)}, f32[792,128]{1,0:T(8,128)S(1)}, u32[]{:S(2)}, u32[]{:S(2)}) collective-permute-start(f32[792,128]{1,0:T(8,128)S(1)} %get-tuple-element.22), channel_id=1, source_target_pairs={{0,12},{1,13},{2,14},{3,15},{4,0},{5,1},{6,2},{7,3},{8,4},{9,5},{1... | collective-permute-start | bytes 1216520 | tf_op jit(solution)/shard_map/ppermute | solution.py:37
  57.3 5.1 %collective-permute-done.9.refs_2_ = f32[792,128]{1,0:T(8,128)S(1)} collective-permute-done((f32[792,128]{1,0:T(8,128)S(1)}, f32[792,128]{1,0:T(8,128)S(1)}, u32[]{:S(2)}, u32[]{:S(2)}) %collective-permute-start.9) | collective-permute-done | bytes 405536 | tf_op jit(solution)/shard_map/ppermute | solution.py:37
  62.4 3.7 %collective-permute-done.10.refs_4_ = f32[792,128]{1,0:T(8,128)S(1)} collective-permute-done((f32[792,128]{1,0:T(8,128)S(1)}, f32[792,128]{1,0:T(8,128)S(1)}, u32[]{:S(2)}, u32[]{:S(2)}) %collective-permute-start.10) | collective-permute-done | bytes 405536 | tf_op jit(solution)/shard_map/ppermute | solution.py:37
  66.1 2.5 %shard_map.34 = f32[4,1584,128]{2,1,0:T(8,128)} custom-call(f32[1584,128]{1,0:T(8,128)S(1)} %shard_map.32.refs_0_, f32[1584,128]{1,0:T(8,128)S(1)} %collective-permute-done.7.refs_0_.refs_1_, f32[792,128]{1,0:T(8,128)S(1)} %collective-permute-done.9.refs_2_, f32[1584,128]{1,0:T(8,128)S(1)} %collective-permute-done.8.refs_1_.refs_3_, ...), custom_call_target="tpu_custom_call" | custom-call | tf_op jit(solution)/shard_map/pallas_call | solution.py:357
  68.6 2.0 %collective-permute-start.12 = (f32[4,1584,128]{2,1,0:T(8,128)}, f32[4,1584,128]{2,1,0:T(8,128)S(1)}, u32[]{:S(2)}, u32[]{:S(2)}) collective-permute-start(f32[4,1584,128]{2,1,0:T(8,128)} %shard_map.34), channel_id=1, source_target_pairs={{0,1},{1,2},{2,3},{3,0},{4,5},{5,6},{6,7},{7,4},{8,9},{9,10},{10,1... | collective-permute-start | bytes 9732104 | tf_op jit(solution)/shard_map/ppermute | solution.py:37
  70.6 3.1 %collective-permute-start.11 = (f32[4,1584,128]{2,1,0:T(8,128)}, f32[4,1584,128]{2,1,0:T(8,128)S(1)}, u32[]{:S(2)}, u32[]{:S(2)}) collective-permute-start(f32[4,1584,128]{2,1,0:T(8,128)} %shard_map.34), channel_id=1, source_target_pairs={{0,3},{1,0},{2,1},{3,2},{4,7},{5,4},{6,5},{7,6},{8,11},{9,8},{10,9... | collective-permute-start | bytes 9732104 | tf_op jit(solution)/shard_map/ppermute | solution.py:37
  73.8 0.6 shard_map.40.bown
  74.5 4.9 %shard_map.37 = (bf16[4,528,384]{2,1,0:T(8,128)(2,1)S(1)}, bf16[4,528,384]{2,1,0:T(8,128)(2,1)S(1)}) custom-call(f32[4,3,528,128]{3,2,1,0:T(8,128)} %bitcast.6.q), custom_call_target="tpu_custom_call" | custom-call | flops 4000000 | bytes 7000000 | tf_op jit(solution)/shard_map/pallas_call | solution.py:296
  79.4 6.3 %collective-permute-done.16.refs_1_ = f32[1,6,64,512]{3,2,1,0:T(8,128)S(1)} collective-permute-done((f32[1,6,64,512]{3,2,1,0:T(8,128)S(1)}, f32[1,6,64,512]{3,2,1,0:T(8,128)S(1)}, u32[]{:S(2)}, u32[]{:S(2)}) %collective-permute-start.16) | collective-permute-done | bytes 786464 | tf_op jit(solution)/shard_map/ppermute | solution.py:37
  86.0 1.2 copy-done.10
  87.1 1.6 copy-done.15
  88.7 2.9 %collective-permute-done.17.mgot = f32[3,6,64,512]{3,2,1,0:T(8,128)S(1)} collective-permute-done((f32[3,6,64,512]{3,2,1,0:T(8,128)S(1)}, f32[3,6,64,512]{3,2,1,0:T(8,128)S(1)}, u32[]{:S(2)}, u32[]{:S(2)}) %collective-permute-start.17) | collective-permute-done | bytes 2359328 | tf_op jit(solution)/shard_map/ppermute | solution.py:37
  91.7 21.6 %shard_map.41 = (bf16[1536,1152]{1,0:T(8,128)(2,1)}, bf16[1536,1152]{1,0:T(8,128)(2,1)}, f32[2304,1152]{1,0:T(8,128)}) custom-call(s32[4]{0:T(128)S(1)} %pad_add_fusion.pos, f32[6,64,512]{2,1,0:T(8,128)S(1)} %shard_map.35.m0, f32[6,64,512]{2,1,0:T(8,128)S(1)} %collective-permute-done.14.mc, f32[3,6,64,512]{3,2,1,0:T(8,128)S(1)} %shard_map.38.mown, ...), custom_call_target="tpu_custom_call" | custom-call | flops 1000000 | bytes 1000000 | tf_op jit(solution)/shard_map/pallas_call | solution.py:454
  113.3 1.8 %copy-done.2 = f32[4,1584,128]{2,1,0:T(8,128)} copy-done((f32[4,1584,128]{2,1,0:T(8,128)}, f32[4,1584,128]{2,1,0:T(8,128)S(1)}, u32[]{:S(2)}) %copy-start.2) | copy-done | bytes 3244056
  115.1 2.0 %copy-done = bf16[1536,1152]{1,0:T(8,128)(2,1)S(1)} copy-done((bf16[1536,1152]{1,0:T(8,128)(2,1)S(1)}, bf16[1536,1152]{1,0:T(8,128)(2,1)}, u32[]{:S(2)}) %copy-start) | copy-done | bytes 3538968
  117.1 1.9 %copy-done.3 = f32[4,1584,128]{2,1,0:T(8,128)S(1)} copy-done((f32[4,1584,128]{2,1,0:T(8,128)S(1)}, f32[4,1584,128]{2,1,0:T(8,128)}, u32[]{:S(2)}) %copy-start.3) | copy-done | bytes 3244056
  119.0 0.4 shard_map.42
  119.4 2.0 %collective-permute-start.20 = (f32[2,1584,128]{2,1,0:T(8,128)S(1)}, f32[2,1584,128]{2,1,0:T(8,128)S(1)}, u32[]{:S(2)}, u32[]{:S(2)}) collective-permute-start(f32[2,1584,128]{2,1,0:T(8,128)S(1)} %get-tuple-element.26), channel_id=1, source_target_pairs={{0,3},{1,0},{2,1},{3,2},{4,7},{5,4},{6,5},{7,6},{8,11},{9,8},{10,9... | collective-permute-start | bytes 4866056 | tf_op jit(solution)/shard_map/ppermute | solution.py:37
  121.5 2.6 %shard_map.44 = (bf16[4,528,384]{2,1,0:T(8,128)(2,1)S(1)}, bf16[4,528,384]{2,1,0:T(8,128)(2,1)S(1)}) custom-call(f32[4,3,528,128]{3,2,1,0:T(8,128)S(1)} %bitcast.11, bf16[1536,1152]{1,0:T(8,128)(2,1)S(1)} %copy-done.1), custom_call_target="tpu_custom_call" | custom-call | flops 4000000 | bytes 7000000 | tf_op jit(solution)/shard_map/pallas_call | solution.py:296
  124.2 1.2 copy-done.13
  125.3 2.6 %shard_map.43 = (bf16[4,528,384]{2,1,0:T(8,128)(2,1)S(1)}, bf16[4,528,384]{2,1,0:T(8,128)(2,1)S(1)}) custom-call(f32[4,3,528,128]{3,2,1,0:T(8,128)S(1)} %bitcast.12, bf16[1536,1152]{1,0:T(8,128)(2,1)S(1)} %copy-done.1), custom_call_target="tpu_custom_call" | custom-call | flops 4000000 | bytes 7000000 | tf_op jit(solution)/shard_map/pallas_call | solution.py:296
  128.0 1.2 copy-done.14
  129.2 25.7 %shard_map.45.r_ref = f32[2304,1152]{1,0:T(8,128)} custom-call(bf16[4,528,384]{2,1,0:T(8,128)(2,1)S(1)} %copy-done.11, bf16[4,528,384]{2,1,0:T(8,128)(2,1)S(1)} %get-tuple-element.29.refs_1_, bf16[4,528,384]{2,1,0:T(8,128)(2,1)S(1)} %get-tuple-element.30.refs_2_, bf16[4,528,384]{2,1,0:T(8,128)(2,1)} %copy-done.12, ...), custom_call_target="tpu_custom_call", output_to_operand_aliasing={{}: (9, {})} | custom-call | flops 16817061888 | bytes 30000000 | tf_op jit(solution)/shard_map/pallas_call | solution.py:316
  154.9 14.3 %shard_map.46 = f32[2304,1152]{1,0:T(8,128)} custom-call(f32[2,3,528,128]{3,2,1,0:T(8,128)S(1)} %bitcast.15, f32[2,3,528,128]{3,2,1,0:T(8,128)S(1)} %bitcast.16, bf16[1536,1152]{1,0:T(8,128)(2,1)} %get-tuple-element.25.refs_2_.refs_0_.refs_6_.xh, bf16[1536,1152]{1,0:T(8,128)(2,1)} %get-tuple-element.28.refs_7_.xl, ...), custom_call_target="tpu_custom_call", output_to_operand_aliasing={{}: (4, {})} | custom-call | flops 5605687296 | bytes 25000000 | tf_op jit(solution)/shard_map/pallas_call | solution.py:330
  (50 shorter events, 1.6 us)
Async XLA Ops:
  2.1 2.7 %copy-start.7 = (f32[3,64,1152]{2,1,0:T(8,128)S(1)}, f32[3,64,1152]{2,1,0:T(8,128)}, u32[]{:S(2)}) copy-start(f32[3,64,1152]{2,1,0:T(8,128)} %shard_map.29.refs_0_.b0) | copy-start | bytes 2654212
  2.1 2.7 %collective-permute-start.3 = (f32[3,64,1152]{2,1,0:T(8,128)}, f32[3,64,1152]{2,1,0:T(8,128)S(1)}, u32[]{:S(2)}, u32[]{:S(2)}) collective-permute-start(f32[3,64,1152]{2,1,0:T(8,128)} %shard_map.29.refs_0_.b0), channel_id=1, source_target_pairs={{0,16},{1,17},{2,18},{3,19},{4,20},{5,21},{6,22},{7,23},{8,24},{9,... | collective-permute-start | bytes 2654216 | tf_op jit(solution)/shard_map/ppermute | solution.py:37
  4.5 1.9 %copy-start.8 = (f32[1584,128]{1,0:T(8,128)}, f32[1584,128]{1,0:T(8,128)S(1)}, u32[]{:S(2)}) copy-start(f32[1584,128]{1,0:T(8,128)S(1)} %get-tuple-element.20.refs_2_.refs_0_) | copy-start | bytes 2433028
  6.4 25.8 %collective-permute-start.13 = (f32[2,3,64,1152]{3,2,1,0:T(8,128)}, f32[2,3,64,1152]{3,2,1,0:T(8,128)S(1)}, u32[]{:S(2)}, u32[]{:S(2)}) collective-permute-start(f32[2,3,64,1152]{3,2,1,0:T(8,128)} %shard_map.30.refs_4_), channel_id=1, source_target_pairs={{0,96},{1,97},{2,98},{3,99},{4,100},{5,101},{6,102},{7,103},{8,104... | collective-permute-start | bytes 5308424 | tf_op jit(solution)/shard_map/ppermute | solution.py:37
  9.6 5.7 %collective-permute-start.2 = (f32[128,128]{1,0:T(8,128)S(1)}, f32[128,128]{1,0:T(8,128)S(1)}, u32[]{:S(2)}, u32[]{:S(2)}) collective-permute-start(f32[128,128]{1,0:T(8,128)S(1)} %get-tuple-element.21.refs_0_), channel_id=1, source_target_pairs={{0,4},{1,5},{2,6},{3,7},{4,8},{5,9},{6,10},{7,11},{8,12},{9,13},{1... | collective-permute-start | bytes 196616 | tf_op jit(solution)/shard_map/ppermute | solution.py:37
  11.1 5.8 %collective-permute-start.1 = (f32[128,128]{1,0:T(8,128)S(1)}, f32[128,128]{1,0:T(8,128)S(1)}, u32[]{:S(2)}, u32[]{:S(2)}) collective-permute-start(f32[128,128]{1,0:T(8,128)S(1)} %get-tuple-element.21.refs_0_), channel_id=1, source_target_pairs={{0,8},{1,9},{2,10},{3,11},{4,12},{5,13},{6,14},{7,15},{8,0},{9,1},... | collective-permute-start | bytes 196616 | tf_op jit(solution)/shard_map/ppermute | solution.py:37
  13.8 4.3 %collective-permute-start = (f32[128,128]{1,0:T(8,128)S(1)}, f32[128,128]{1,0:T(8,128)S(1)}, u32[]{:S(2)}, u32[]{:S(2)}) collective-permute-start(f32[128,128]{1,0:T(8,128)S(1)} %get-tuple-element.21.refs_0_), channel_id=1, source_target_pairs={{0,12},{1,13},{2,14},{3,15},{4,0},{5,1},{6,2},{7,3},{8,4},{9,5},{1... | collective-permute-start | bytes 196616 | tf_op jit(solution)/shard_map/ppermute | solution.py:37
  19.1 8.8 %collective-permute-start.6 = (f32[4,128,128]{2,1,0:T(8,128)}, f32[4,128,128]{2,1,0:T(8,128)}, u32[]{:S(2)}, u32[]{:S(2)}) collective-permute-start(f32[4,128,128]{2,1,0:T(8,128)} %shard_map.31.g0), channel_id=1, source_target_pairs={{0,1},{1,2},{2,3},{3,0},{4,5},{5,6},{6,7},{7,4},{8,9},{9,10},{10,1... | collective-permute-start | bytes 786440 | tf_op jit(solution)/shard_map/ppermute | solution.py:37
  21.1 11.1 %collective-permute-start.5 = (f32[4,128,128]{2,1,0:T(8,128)}, f32[4,128,128]{2,1,0:T(8,128)}, u32[]{:S(2)}, u32[]{:S(2)}) collective-permute-start(f32[4,128,128]{2,1,0:T(8,128)} %shard_map.31.g0), channel_id=1, source_target_pairs={{0,2},{1,3},{2,0},{3,1},{4,6},{5,7},{6,4},{7,5},{8,10},{9,11},{10,... | collective-permute-start | bytes 786440 | tf_op jit(solution)/shard_map/ppermute | solution.py:37
  24.7 7.5 %collective-permute-start.4 = (f32[4,128,128]{2,1,0:T(8,128)}, f32[4,128,128]{2,1,0:T(8,128)}, u32[]{:S(2)}, u32[]{:S(2)}) collective-permute-start(f32[4,128,128]{2,1,0:T(8,128)} %shard_map.31.g0), channel_id=1, source_target_pairs={{0,3},{1,0},{2,1},{3,2},{4,7},{5,4},{6,5},{7,6},{8,11},{9,8},{10,9... | collective-permute-start | bytes 786440 | tf_op jit(solution)/shard_map/ppermute | solution.py:37
  35.7 4.0 %copy-start.9 = (f32[1584,128]{1,0:T(8,128)S(1)}, f32[1584,128]{1,0:T(8,128)}, u32[]{:S(2)}) copy-start(f32[1584,128]{1,0:T(8,128)} %copy-done.8) | copy-start | bytes 2433028
  35.7 2.4 %collective-permute-start.14 = (f32[6,64,512]{2,1,0:T(8,128)S(1)}, f32[6,64,512]{2,1,0:T(8,128)S(1)}, u32[]{:S(2)}, u32[]{:S(2)}) collective-permute-start(f32[6,64,512]{2,1,0:T(8,128)S(1)} %shard_map.35.m0), channel_id=1, source_target_pairs={{0,16},{1,17},{2,18},{3,19},{4,20},{5,21},{6,22},{7,23},{8,24},{9,... | collective-permute-start | bytes 2359304 | tf_op jit(solution)/shard_map/ppermute | solution.py:37
  38.2 35.4 %collective-permute-start.15 = (f32[2,6,64,512]{3,2,1,0:T(8,128)S(1)}, f32[2,6,64,512]{3,2,1,0:T(8,128)S(1)}, u32[]{:S(2)}, u32[]{:S(2)}) collective-permute-start(f32[2,6,64,512]{3,2,1,0:T(8,128)S(1)} %pad_maximum_fusion), channel_id=1, source_target_pairs={{0,96},{1,97},{2,98},{3,99},{4,100},{5,101},{6,102},{7,103},{8,104... | collective-permute-start | bytes 4718600 | tf_op jit(solution)/shard_map/ppermute | solution.py:37
  39.7 13.5 %collective-permute-start.8 = (f32[1584,128]{1,0:T(8,128)S(1)}, f32[1584,128]{1,0:T(8,128)S(1)}, u32[]{:S(2)}, u32[]{:S(2)}) collective-permute-start(f32[1584,128]{1,0:T(8,128)S(1)} %shard_map.32.refs_0_), channel_id=1, source_target_pairs={{0,4},{1,5},{2,6},{3,7},{4,8},{5,9},{6,10},{7,11},{8,12},{9,13},{1... | collective-permute-start | bytes 2433032 | tf_op jit(solution)/shard_map/ppermute | solution.py:37
  41.3 12.3 %collective-permute-start.7 = (f32[1584,128]{1,0:T(8,128)S(1)}, f32[1584,128]{1,0:T(8,128)S(1)}, u32[]{:S(2)}, u32[]{:S(2)}) collective-permute-start(f32[1584,128]{1,0:T(8,128)S(1)} %shard_map.32.refs_0_), channel_id=1, source_target_pairs={{0,12},{1,13},{2,14},{3,15},{4,0},{5,1},{6,2},{7,3},{8,4},{9,5},{1... | collective-permute-start | bytes 2433032 | tf_op jit(solution)/shard_map/ppermute | solution.py:37
  53.9 8.5 %collective-permute-start.9 = (f32[792,128]{1,0:T(8,128)S(1)}, f32[792,128]{1,0:T(8,128)S(1)}, u32[]{:S(2)}, u32[]{:S(2)}) collective-permute-start(f32[792,128]{1,0:T(8,128)S(1)} %get-tuple-element.22), channel_id=1, source_target_pairs={{0,12},{1,13},{2,14},{3,15},{4,0},{5,1},{6,2},{7,3},{8,4},{9,5},{1... | collective-permute-start | bytes 1216520 | tf_op jit(solution)/shard_map/ppermute | solution.py:37
  57.0 9.1 %collective-permute-start.10 = (f32[792,128]{1,0:T(8,128)S(1)}, f32[792,128]{1,0:T(8,128)S(1)}, u32[]{:S(2)}, u32[]{:S(2)}) collective-permute-start(f32[792,128]{1,0:T(8,128)S(1)} %get-tuple-element.23), channel_id=1, source_target_pairs={{0,4},{1,5},{2,6},{3,7},{4,8},{5,9},{6,10},{7,11},{8,12},{9,13},{1... | collective-permute-start | bytes 1216520 | tf_op jit(solution)/shard_map/ppermute | solution.py:37
  57.2 16.6 %collective-permute-start.18 = (f32[1,3,64,1152]{3,2,1,0:T(8,128)S(1)}, f32[1,3,64,1152]{3,2,1,0:T(8,128)S(1)}, u32[]{:S(2)}, u32[]{:S(2)}) collective-permute-start(f32[1,3,64,1152]{3,2,1,0:T(8,128)S(1)} %shard_map.39), channel_id=1, source_target_pairs={{0,96},{1,97},{2,98},{3,99},{4,100},{5,101},{6,102},{7,103},{8,104... | collective-permute-start | bytes 2654216 | tf_op jit(solution)/shard_map/ppermute | solution.py:37
  68.6 44.7 %collective-permute-start.12 = (f32[4,1584,128]{2,1,0:T(8,128)}, f32[4,1584,128]{2,1,0:T(8,128)S(1)}, u32[]{:S(2)}, u32[]{:S(2)}) collective-permute-start(f32[4,1584,128]{2,1,0:T(8,128)} %shard_map.34), channel_id=1, source_target_pairs={{0,1},{1,2},{2,3},{3,0},{4,5},{5,6},{6,7},{7,4},{8,9},{9,10},{10,1... | collective-permute-start | bytes 9732104 | tf_op jit(solution)/shard_map/ppermute | solution.py:37
  70.6 42.7 %collective-permute-start.11 = (f32[4,1584,128]{2,1,0:T(8,128)}, f32[4,1584,128]{2,1,0:T(8,128)S(1)}, u32[]{:S(2)}, u32[]{:S(2)}) collective-permute-start(f32[4,1584,128]{2,1,0:T(8,128)} %shard_map.34), channel_id=1, source_target_pairs={{0,3},{1,0},{2,1},{3,2},{4,7},{5,4},{6,5},{7,6},{8,11},{9,8},{10,9... | collective-permute-start | bytes 9732104 | tf_op jit(solution)/shard_map/ppermute | solution.py:37
  73.7 12.1 %collective-permute-start.16 = (f32[1,6,64,512]{3,2,1,0:T(8,128)S(1)}, f32[1,6,64,512]{3,2,1,0:T(8,128)S(1)}, u32[]{:S(2)}, u32[]{:S(2)}) collective-permute-start(f32[1,6,64,512]{3,2,1,0:T(8,128)S(1)} %shard_map.36), channel_id=1, source_target_pairs={{0,96},{1,97},{2,98},{3,99},{4,100},{5,101},{6,102},{7,103},{8,104... | collective-permute-start | bytes 2359304 | tf_op jit(solution)/shard_map/ppermute | solution.py:37
  74.4 5.0 %copy-start.5 = (f32[3,3,64,1152]{3,2,1,0:T(8,128)}, f32[3,3,64,1152]{3,2,1,0:T(8,128)S(1)}, u32[]{:S(2)}) copy-start(f32[3,3,64,1152]{3,2,1,0:T(8,128)S(1)} %shard_map.40.bown) | copy-start | bytes 7962628
  74.4 12.8 %collective-permute-start.19 = (f32[3,3,64,1152]{3,2,1,0:T(8,128)S(1)}, f32[3,3,64,1152]{3,2,1,0:T(8,128)S(1)}, u32[]{:S(2)}, u32[]{:S(2)}) collective-permute-start(f32[3,3,64,1152]{3,2,1,0:T(8,128)S(1)} %shard_map.40.bown), channel_id=1, source_target_pairs={{0,16},{1,17},{2,18},{3,19},{4,20},{5,21},{6,22},{7,23},{8,24},{9,... | collective-permute-start | bytes 7962632 | tf_op jit(solution)/shard_map/ppermute | solution.py:37
  79.4 6.5 %copy-start.12 = (bf16[4,528,384]{2,1,0:T(8,128)(2,1)}, bf16[4,528,384]{2,1,0:T(8,128)(2,1)S(1)}, u32[]{:S(2)}) copy-start(bf16[4,528,384]{2,1,0:T(8,128)(2,1)S(1)} %get-tuple-element.31.refs_3_) | copy-start | bytes 4866052
  85.8 5.9 %copy-start.6 = (f32[3,3,64,1152]{3,2,1,0:T(8,128)S(1)}, f32[3,3,64,1152]{3,2,1,0:T(8,128)}, u32[]{:S(2)}) copy-start(f32[3,3,64,1152]{3,2,1,0:T(8,128)} %copy-done.5) | copy-start | bytes 7962628
  86.0 1.2 copy-start.10
  87.1 4.5 %collective-permute-start.17 = (f32[3,6,64,512]{3,2,1,0:T(8,128)S(1)}, f32[3,6,64,512]{3,2,1,0:T(8,128)S(1)}, u32[]{:S(2)}, u32[]{:S(2)}) collective-permute-start(f32[3,6,64,512]{3,2,1,0:T(8,128)S(1)} %shard_map.38.mown), channel_id=1, source_target_pairs={{0,16},{1,17},{2,18},{3,19},{4,20},{5,21},{6,22},{7,23},{8,24},{9,... | collective-permute-start | bytes 7077896 | tf_op jit(solution)/shard_map/ppermute | solution.py:37
  87.1 1.6 copy-start.15
  113.3 1.8 %copy-start.2 = (f32[4,1584,128]{2,1,0:T(8,128)}, f32[4,1584,128]{2,1,0:T(8,128)S(1)}, u32[]{:S(2)}) copy-start(f32[4,1584,128]{2,1,0:T(8,128)S(1)} %collective-permute-done.11.refs_0_) | copy-start | bytes 9732100
  115.1 2.0 %copy-start = (bf16[1536,1152]{1,0:T(8,128)(2,1)S(1)}, bf16[1536,1152]{1,0:T(8,128)(2,1)}, u32[]{:S(2)}) copy-start(bf16[1536,1152]{1,0:T(8,128)(2,1)} %get-tuple-element.25.refs_2_.refs_0_.refs_6_.xh) | copy-start | bytes 10616836
  117.1 1.9 %copy-start.3 = (f32[4,1584,128]{2,1,0:T(8,128)S(1)}, f32[4,1584,128]{2,1,0:T(8,128)}, u32[]{:S(2)}) copy-start(f32[4,1584,128]{2,1,0:T(8,128)} %copy-done.2) | copy-start | bytes 9732100
  119.0 2.5 %copy-start.1 = (bf16[1536,1152]{1,0:T(8,128)(2,1)S(1)}, bf16[1536,1152]{1,0:T(8,128)(2,1)}, u32[]{:S(2)}) copy-start(bf16[1536,1152]{1,0:T(8,128)(2,1)} %get-tuple-element.25.refs_2_.refs_0_.refs_6_.xh) | copy-start | bytes 10616836
  119.4 35.5 %collective-permute-start.20 = (f32[2,1584,128]{2,1,0:T(8,128)S(1)}, f32[2,1584,128]{2,1,0:T(8,128)S(1)}, u32[]{:S(2)}, u32[]{:S(2)}) collective-permute-start(f32[2,1584,128]{2,1,0:T(8,128)S(1)} %get-tuple-element.26), channel_id=1, source_target_pairs={{0,3},{1,0},{2,1},{3,2},{4,7},{5,4},{6,5},{7,6},{8,11},{9,8},{10,9... | collective-permute-start | bytes 4866056 | tf_op jit(solution)/shard_map/ppermute | solution.py:37
  121.4 33.5 %collective-permute-start.21 = (f32[2,1584,128]{2,1,0:T(8,128)S(1)}, f32[2,1584,128]{2,1,0:T(8,128)S(1)}, u32[]{:S(2)}, u32[]{:S(2)}) collective-permute-start(f32[2,1584,128]{2,1,0:T(8,128)S(1)} %get-tuple-element.27), channel_id=1, source_target_pairs={{0,1},{1,2},{2,3},{3,0},{4,5},{5,6},{6,7},{7,4},{8,9},{9,10},{10,1... | collective-permute-start | bytes 4866056 | tf_op jit(solution)/shard_map/ppermute | solution.py:37
  121.5 3.8 %copy-start.4 = (f32[4,1584,128]{2,1,0:T(8,128)S(1)}, f32[4,1584,128]{2,1,0:T(8,128)}, u32[]{:S(2)}) copy-start(f32[4,1584,128]{2,1,0:T(8,128)} %copy-done.2) | copy-start | bytes 9732100
  124.2 1.2 copy-start.13
  125.3 3.9 %copy-start.11 = (bf16[4,528,384]{2,1,0:T(8,128)(2,1)S(1)}, bf16[4,528,384]{2,1,0:T(8,128)(2,1)}, u32[]{:S(2)}) copy-start(bf16[4,528,384]{2,1,0:T(8,128)(2,1)} %copy-done.10) | copy-start | bytes 4866052
  128.0 1.2 copy-start.14

commit v5 on v4

--- a/solution.py
+++ b/solution.py
@@ -78,7 +78,7 @@
     return xs * NZ + zs
 
 
-def rows_kernel(pos, g0, g1, g2, g3, _after, out, canon, diag):
+def rows_kernel(pos, g0, g1, g2, g3, _hop, _packed, out, canon, diag):
     y, core = pos[0], pos[1]
     for i, ref in enumerate((g0, g1, g2, g3)):
         for j in range(4):
@@ -144,7 +144,7 @@
 
 
 def solve_kernel(
-    pos, m0, mc, mown, mgot, b0, bc, bown, bgot, xh, xl, base, mat, b_ref, lh, ll, oh, ol, rh, rl, ah, al, xs, own, sem, last
+    pos, m0, mc, mown, mgot, b0, bc, bown, bgot, xh, xl, base, token, mat, b_ref, lh, ll, oh, ol, rh, rl, ah, al, xs, own, sem, last
 ):
     y, core = pos[0], pos[1]
 
@@ -227,6 +227,7 @@
                 dst = (k * PANELS + p) * 128 + j * CB
                 xh[dst : dst + CB, :] = ah[pl.ds(src, CB), :]
                 xl[dst : dst + CB, :] = al[pl.ds(src, CB), :]
+    token[...] = xs[0:8, 0:128]
     copy = pltpu.make_async_copy(own, base.at[0:WIN, :], last)
     copy.start()
     copy.wait()
@@ -320,7 +321,7 @@
         in_specs=[spec] * 6 + [xs, xs, STRIP, ANY],
         out_specs=STRIP,
         input_output_aliases={9: 0},
-        compiler_params=params(48),
+        compiler_params=params(57),
         cost_estimate=cost(6 * TRAIL * 3 * SUB * NCOL, 30e6),
     )(*[v[0] for v in parts], *[v[1] for v in parts], xh, xl, rows_in, base)
 
@@ -335,7 +336,7 @@
         out_specs=STRIP,
         scratch_shapes=[pltpu.VMEM((GROUPS, GR, SUB), BF16)] * 2,
         input_output_aliases={4: 0},
-        compiler_params=params(48),
+        compiler_params=params(57),
         cost_estimate=cost(6 * TRAIL * SUB * NCOL, 25e6),
     )(*[v.reshape(2, PANELS, GR, 128) for v in last], xh, xl, base)
 
@@ -364,11 +365,9 @@
     )(*arrays)
 
 
-def second_hop(hop, early=(), late=()):
-    shape = (1, *hop.shape[1:])
-    (first,) = moved((hop, *early), [shape], [(0, pl.ds(0, 1), 0, None)], 30)
+def joined(hop, hop2):
     (kept,) = moved(
-        (hop, along_y(first), *late),
+        (hop, hop2),
         [(3, *hop.shape[1:])],
         [(0, None, 0, pl.ds(0, 2)), (1, None, 0, pl.ds(2, 1))],
         30,
@@ -412,16 +411,40 @@
     total = PANELS * GR
     h = total // 2
     (packed,) = moved((packed, *groups[1:]), [(total, 128)], [(0, None, 0, None)], 8)
+    mine = pl.pallas_call(
+        rows_kernel,
+        out_shape=jax.ShapeDtypeStruct((SLOTS, PB, PANEL), F32),
+        in_specs=[SM] + [VM] * 4 + [ANY] * 2,
+        out_specs=VM,
+        scratch_shapes=[
+            pltpu.VMEM((16, 2 * PB, 128), F32),
+            pltpu.VMEM((PANELS, NX, PB, 128), F32),
+        ],
+        compiler_params=params(8),
+    )(pos, *groups, bhop, packed)
+
+    mc = from_core(mine)
+    (bfirst,) = moved((bhop,), [(1, *rows3)], [(0, pl.ds(0, 1), 0, None)], 8)
+    bhop2 = along_y(bfirst)
+    tile = (SLOTS, PB, PANEL)
+    (wpair,) = moved((mine, mc, bhop2), [(2, *tile)], [(0, None, 0, 0), (1, None, 0, 1)], 16)
+    whop = along_y(wpair)
+
     u1, u3 = from_first(packed, 1), from_first(packed, 3)
-    f1, f3 = moved(
-        (u1, u3),
-        [(h, 128), (h, 128)],
-        [(0, pl.ds(0, h), 0, None), (1, pl.ds(h, h), 1, None)],
+    f1, f3, wfirst = moved(
+        (u1, u3, whop),
+        [(h, 128), (h, 128), (1, *tile)],
+        [
+            (0, pl.ds(0, h), 0, None),
+            (1, pl.ds(h, h), 1, None),
+            (2, pl.ds(0, 1), 2, None),
+        ],
         8,
     )
+    whop2 = along_y(wfirst)
     o1, o3 = from_first(f1, 1), from_first(f3, 3)
     (q0,) = moved(
-        (packed, u1, o1, u3, o3),
+        (packed, u1, o1, u3, o3, whop2),
         [(4, total, 128)],
         [
             (0, None, 0, 0),
@@ -434,32 +457,20 @@
     )
     q1, q3 = from_second(q0, 1), from_second(q0, 3)
 
-    mine = pl.pallas_call(
-        rows_kernel,
-        out_shape=jax.ShapeDtypeStruct((SLOTS, PB, PANEL), F32),
-        in_specs=[SM] + [VM] * 4 + [ANY],
-        out_specs=VM,
-        scratch_shapes=[
-            pltpu.VMEM((16, 2 * PB, 128), F32),
-            pltpu.VMEM((PANELS, NX, PB, 128), F32),
-        ],
-        compiler_params=params(8),
-    )(pos, *groups, bhop)
-
-    mc = from_core(mine)
     first = assemble(q0)
-    rows = (mine, mc, *second_hop(along_y(jnp.stack([mine, mc])), late=(first[0],)))
-    rhs_rows = (b0, bc, *second_hop(bhop))
-
-    xh, xl, base = pl.pallas_call(
+    rows = (mine, mc, *joined(whop, whop2))
+    rhs_rows = (b0, bc, *joined(bhop, bhop2))
+
+    xh, xl, base, token = pl.pallas_call(
         solve_kernel,
         out_shape=(
             jax.ShapeDtypeStruct((DEPTH, NCOL), BF16),
             jax.ShapeDtypeStruct((DEPTH, NCOL), BF16),
             jax.ShapeDtypeStruct((ROWS, NCOL), F32),
+            jax.ShapeDtypeStruct((8, 128), F32),
         ),
         in_specs=[SM] + [ANY] * 8,
-        out_specs=(VM, VM, ANY),
+        out_specs=(VM, VM, ANY, VM),
         scratch_shapes=[
             pltpu.VMEM((SLOTS, PANEL, PANEL), F32),
             pltpu.VMEM((PANELS, PANEL, NCOL), F32),
@@ -478,13 +489,13 @@
     )(pos, *rows, *rhs_rows)
 
     f1, f3 = moved(
-        (q1, q3, xh),
+        (q1, q3, token),
         [(2, total, 128), (2, total, 128)],
         [(0, pl.ds(0, 2), 0, None), (1, pl.ds(2, 2), 1, None)],
         16,
     )
     q2 = (from_second(f1, 1), from_second(f3, 3))
-    parts = [first, assemble(q1, xh), assemble(q3, xh)]
+    parts = [first, assemble(q1, token), assemble(q3, token)]
     base = update(rhs_tile, base, parts, xh, xl)
     return update_last(base, q2, xh, xl)
 

time: 170 us -> 188 us (1.11)
  waiting for transfers between devices: 40.4 us -> 53.5 us
  starting transfers between devices: 30.7 us -> 36.1 us
    ppermute x22, waiting for transfers between devices: 40.4 us -> 53.5 us  [joint(): return lax.ppermute(v, ('row', 'col'), pairs)]
    ppermute x22, starting transfers between devices: 30.7 us -> 36.1 us  [joint(): return lax.ppermute(v, ('row', 'col'), pairs)]
    unnamed x33 -> x27, local copies, waits for them, and re-layouts: 12.5 us -> 12.1 us
  transfers between devices with their start and end apart: 22 -> 22, of which waited for: 12 -> 17; matrix products, arithmetic and copies ran while one was open for 1% -> 1% of each run, Pallas kernels for 37% -> 34%
where the time goes in v5:
time: 188 us
  Pallas kernels  85.8 us (46%)
  waiting for transfers between devices  53.5 us (28%)
  starting transfers between devices  36.1 us (19%)
  local copies, waits for them, and re-layouts  12.1 us (6%)
    ppermute x22, waiting for transfers between devices, joint(): return lax.ppermute(v, ('row', 'col'), pairs)  53.5 us
    ppermute x22, starting transfers between devices, joint(): return lax.ppermute(v, ('row', 'col'), pairs)  36.1 us
    pallas_call x1, Pallas kernels, update(): pl.pallas_call(update_kernel, grid=(GROUPS,), out_shape=jax.ShapeDtypeStr...  26.1 us
    pallas_call x1, Pallas kernels, local(): pl.pallas_call(solve_kernel, out_shape=(jax.ShapeDtypeStruct((DEPTH, NCOL...  21.6 us
    pallas_call x1, Pallas kernels, update_last(): pl.pallas_call(update_last_kernel, grid=(GROUPS,), out_shape=jax.ShapeDty...  15.2 us
    unnamed x27, local copies, waits for them, and re-layouts  12.1 us
    pallas_call x3, Pallas kernels, assemble(): pl.pallas_call(assemble_kernel, grid=(GR // CHUNK,), out_shape=(out, out)...  9.97 us
    pallas_call x11, Pallas kernels, moved(): pl.pallas_call(kernel, out_shape=[jax.ShapeDtypeStruct(v, F32) for v in s...  8.64 us
  transfers between devices with their start and end apart: 22, of which 17 were waited for; matrix products, arithmetic and copies ran while one was open for 1% of the time, Pallas kernels for 34%

profile of v5, /device:TPU:0, one launch (start us, length us, event | category | flops | bytes accessed | tf_op | source)
XLA Modules:
  0.0 187.9 jit_solution(10840260439799083244)
XLA Ops:
  0.0 2.1 %shard_map.29.refs_0_.b0 = f32[3,64,1152]{2,1,0:T(8,128)} custom-call(f32[2304,1152]{1,0:T(8,128)} %refs_8_.1), custom_call_target="tpu_custom_call" | custom-call | tf_op jit(solution)/shard_map/pallas_call | solution.py:358
  2.2 1.6 copy.5.f_ref
  4.8 1.6 shard_map.30.refs_4_
  6.4 3.2 %collective-permute-start.9 = (f32[2,3,64,1152]{3,2,1,0:T(8,128)}, f32[2,3,64,1152]{3,2,1,0:T(8,128)S(1)}, u32[]{:S(2)}, u32[]{:S(2)}) collective-permute-start(f32[2,3,64,1152]{3,2,1,0:T(8,128)} %shard_map.30.refs_4_), channel_id=1, source_target_pairs={{0,96},{1,97},{2,98},{3,99},{4,100},{5,101},{6,102},{7,103},{8,104... | collective-permute-start | bytes 5308424 | tf_op jit(solution)/shard_map/ppermute | solution.py:37
  9.6 2.8 %collective-permute-start = (f32[128,128]{1,0:T(8,128)S(1)}, f32[128,128]{1,0:T(8,128)S(1)}, u32[]{:S(2)}, u32[]{:S(2)}) collective-permute-start(f32[128,128]{1,0:T(8,128)S(1)} %get-tuple-element.23.refs_0_), channel_id=1, source_target_pairs={{0,12},{1,13},{2,14},{3,15},{4,0},{5,1},{6,2},{7,3},{8,4},{9,5},{1... | collective-permute-start | bytes 196616 | tf_op jit(solution)/shard_map/ppermute | solution.py:37
  12.3 0.8 collective-permute-start.1
  13.1 0.9 collective-permute-start.2
  14.2 3.9 %collective-permute-done.1.refs_2_ = f32[128,128]{1,0:T(8,128)S(1)} collective-permute-done((f32[128,128]{1,0:T(8,128)S(1)}, f32[128,128]{1,0:T(8,128)S(1)}, u32[]{:S(2)}, u32[]{:S(2)}) %collective-permute-start.1) | collective-permute-done | bytes 65568 | tf_op jit(solution)/shard_map/ppermute | solution.py:37
  18.8 1.0 shard_map.31.g0
  19.9 4.1 %collective-permute-start.4 = (f32[4,128,128]{2,1,0:T(8,128)}, f32[4,128,128]{2,1,0:T(8,128)}, u32[]{:S(2)}, u32[]{:S(2)}) collective-permute-start(f32[4,128,128]{2,1,0:T(8,128)} %shard_map.31.g0), channel_id=1, source_target_pairs={{0,3},{1,0},{2,1},{3,2},{4,7},{5,4},{6,5},{7,6},{8,11},{9,8},{10,9... | collective-permute-start | bytes 786440 | tf_op jit(solution)/shard_map/ppermute | solution.py:37
  24.0 1.3 collective-permute-start.6
  25.2 4.7 %collective-permute-done.9._hop.refs_0_ = f32[2,3,64,1152]{3,2,1,0:T(8,128)S(1)} collective-permute-done((f32[2,3,64,1152]{3,2,1,0:T(8,128)}, f32[2,3,64,1152]{3,2,1,0:T(8,128)S(1)}, u32[]{:S(2)}, u32[]{:S(2)}) %collective-permute-start.9) | collective-permute-done | bytes 1769504 | tf_op jit(solution)/shard_map/ppermute | solution.py:37
  30.1 3.7 %collective-permute-start.11 = (f32[1,3,64,1152]{3,2,1,0:T(8,128)S(1)}, f32[1,3,64,1152]{3,2,1,0:T(8,128)S(1)}, u32[]{:S(2)}, u32[]{:S(2)}) collective-permute-start(f32[1,3,64,1152]{3,2,1,0:T(8,128)S(1)} %shard_map.34), channel_id=1, source_target_pairs={{0,96},{1,97},{2,98},{3,99},{4,100},{5,101},{6,102},{7,103},{8,104... | collective-permute-start | bytes 2654216 | tf_op jit(solution)/shard_map/ppermute | solution.py:37
  33.9 0.8 collective-permute-done.6.refs_3_.g3
  34.8 3.5 %shard_map.33.refs_0_.m0 = f32[6,64,512]{2,1,0:T(8,128)S(1)} custom-call(s32[4]{0:T(128)S(1)} %pad_add_fusion.pos, f32[4,128,128]{2,1,0:T(8,128)} %shard_map.31.g0, f32[4,128,128]{2,1,0:T(8,128)} %collective-permute-done.4.refs_1_.g1, f32[4,128,128]{2,1,0:T(8,128)} %collective-permute-done.5.refs_2_.g2, f32[4,128,128]{2,1,0:T(8,128)} %collective-permute-done.6.refs_3_.g3, ...), custom_call_target="tpu_custom_call" | custom-call | tf_op jit(solution)/shard_map/pallas_call | solution.py:414
  38.3 2.3 %collective-permute-done.10.refs_1_.mc = f32[6,64,512]{2,1,0:T(8,128)S(1)} collective-permute-done((f32[6,64,512]{2,1,0:T(8,128)S(1)}, f32[6,64,512]{2,1,0:T(8,128)S(1)}, u32[]{:S(2)}, u32[]{:S(2)}) %collective-permute-start.10) | collective-permute-done | bytes 786464 | tf_op jit(solution)/shard_map/ppermute | solution.py:37
  40.6 3.7 %collective-permute-done.11.refs_2_.refs_1_ = f32[1,3,64,1152]{3,2,1,0:T(8,128)S(1)} collective-permute-done((f32[1,3,64,1152]{3,2,1,0:T(8,128)S(1)}, f32[1,3,64,1152]{3,2,1,0:T(8,128)S(1)}, u32[]{:S(2)}, u32[]{:S(2)}) %collective-permute-start.11) | collective-permute-done | bytes 884768 | tf_op jit(solution)/shard_map/ppermute | solution.py:37
  44.5 3.8 %collective-permute-start.12 = (f32[2,6,64,512]{3,2,1,0:T(8,128)S(1)}, f32[2,6,64,512]{3,2,1,0:T(8,128)S(1)}, u32[]{:S(2)}, u32[]{:S(2)}) collective-permute-start(f32[2,6,64,512]{3,2,1,0:T(8,128)S(1)} %shard_map.35), channel_id=1, source_target_pairs={{0,96},{1,97},{2,98},{3,99},{4,100},{5,101},{6,102},{7,103},{8,104... | collective-permute-start | bytes 4718600 | tf_op jit(solution)/shard_map/ppermute | solution.py:37
  48.2 2.8 %collective-permute-start.7 = (f32[1584,128]{1,0:T(8,128)S(1)}, f32[1584,128]{1,0:T(8,128)S(1)}, u32[]{:S(2)}, u32[]{:S(2)}) collective-permute-start(f32[1584,128]{1,0:T(8,128)S(1)} %shard_map.32._packed.refs_0_), channel_id=1, source_target_pairs={{0,12},{1,13},{2,14},{3,15},{4,0},{5,1},{6,2},{7,3},{8,4},{9,5},{1... | collective-permute-start | bytes 2433032 | tf_op jit(solution)/shard_map/ppermute | solution.py:37
  51.0 9.8 %collective-permute-done.7.refs_0_.refs_1_ = f32[1584,128]{1,0:T(8,128)S(1)} collective-permute-done((f32[1584,128]{1,0:T(8,128)S(1)}, f32[1584,128]{1,0:T(8,128)S(1)}, u32[]{:S(2)}, u32[]{:S(2)}) %collective-permute-start.7) | collective-permute-done | bytes 811040 | tf_op jit(solution)/shard_map/ppermute | solution.py:37
  60.8 3.7 %collective-permute-done.8.refs_1_.refs_3_ = f32[1584,128]{1,0:T(8,128)S(1)} collective-permute-done((f32[1584,128]{1,0:T(8,128)S(1)}, f32[1584,128]{1,0:T(8,128)S(1)}, u32[]{:S(2)}, u32[]{:S(2)}) %collective-permute-start.8) | collective-permute-done | bytes 811040 | tf_op jit(solution)/shard_map/ppermute | solution.py:37
  64.5 1.7 collective-permute-done.12.refs_2_.refs_0_
  66.7 3.8 %collective-permute-start.15 = (f32[1,6,64,512]{3,2,1,0:T(8,128)S(1)}, f32[1,6,64,512]{3,2,1,0:T(8,128)S(1)}, u32[]{:S(2)}, u32[]{:S(2)}) collective-permute-start(f32[1,6,64,512]{3,2,1,0:T(8,128)S(1)} %get-tuple-element.26), channel_id=1, source_target_pairs={{0,96},{1,97},{2,98},{3,99},{4,100},{5,101},{6,102},{7,103},{8,104... | collective-permute-start | bytes 2359304 | tf_op jit(solution)/shard_map/ppermute | solution.py:37
  70.4 2.8 %collective-permute-start.13 = (f32[792,128]{1,0:T(8,128)S(1)}, f32[792,128]{1,0:T(8,128)S(1)}, u32[]{:S(2)}, u32[]{:S(2)}) collective-permute-start(f32[792,128]{1,0:T(8,128)S(1)} %get-tuple-element.24), channel_id=1, source_target_pairs={{0,12},{1,13},{2,14},{3,15},{4,0},{5,1},{6,2},{7,3},{8,4},{9,5},{1... | collective-permute-start | bytes 1216520 | tf_op jit(solution)/shard_map/ppermute | solution.py:37
  73.2 5.4 %collective-permute-done.13.refs_2_ = f32[792,128]{1,0:T(8,128)S(1)} collective-permute-done((f32[792,128]{1,0:T(8,128)S(1)}, f32[792,128]{1,0:T(8,128)S(1)}, u32[]{:S(2)}, u32[]{:S(2)}) %collective-permute-start.13) | collective-permute-done | bytes 405536 | tf_op jit(solution)/shard_map/ppermute | solution.py:37
  78.6 3.7 %collective-permute-done.14.refs_4_ = f32[792,128]{1,0:T(8,128)S(1)} collective-permute-done((f32[792,128]{1,0:T(8,128)S(1)}, f32[792,128]{1,0:T(8,128)S(1)}, u32[]{:S(2)}, u32[]{:S(2)}) %collective-permute-start.14) | collective-permute-done | bytes 405536 | tf_op jit(solution)/shard_map/ppermute | solution.py:37
  82.3 0.7 shard_map.37
  83.0 4.1 %collective-permute-start.16 = (f32[4,1584,128]{2,1,0:T(8,128)S(1)}, f32[4,1584,128]{2,1,0:T(8,128)S(1)}, u32[]{:S(2)}, u32[]{:S(2)}) collective-permute-start(f32[4,1584,128]{2,1,0:T(8,128)S(1)} %shard_map.37), channel_id=1, source_target_pairs={{0,3},{1,0},{2,1},{3,2},{4,7},{5,4},{6,5},{7,6},{8,11},{9,8},{10,9... | collective-permute-start | bytes 9732104 | tf_op jit(solution)/shard_map/ppermute | solution.py:37
  88.0 1.2 copy-done
  89.2 3.5 %collective-permute-done.19.bgot = f32[3,3,64,1152]{3,2,1,0:T(8,128)S(1)} collective-permute-done((f32[3,3,64,1152]{3,2,1,0:T(8,128)S(1)}, f32[3,3,64,1152]{3,2,1,0:T(8,128)S(1)}, u32[]{:S(2)}, u32[]{:S(2)}) %collective-permute-start.19) | collective-permute-done | bytes 2654240 | tf_op jit(solution)/shard_map/ppermute | solution.py:37
  92.8 1.6 copy-done.11
  94.3 1.8 collective-permute-done.18.mgot
  96.1 1.7 copy-done.1
  97.9 21.6 %shard_map.40 = (bf16[1536,1152]{1,0:T(8,128)(2,1)}, bf16[1536,1152]{1,0:T(8,128)(2,1)}, f32[2304,1152]{1,0:T(8,128)}, f32[8,128]{1,0:T(8,128)S(1)}) custom-call(s32[4]{0:T(128)S(1)} %pad_add_fusion.pos, f32[6,64,512]{2,1,0:T(8,128)S(1)} %shard_map.33.refs_0_.m0, f32[6,64,512]{2,1,0:T(8,128)S(1)} %collective-permute-done.10.refs_1_.mc, ...), custom_call_target="tpu_custom_call" | custom-call | flops 1000000 | bytes 1000000 | tf_op jit(solution)/shard_map/pallas_call | solution.py:464
  119.5 3.5 %collective-permute-done.16.refs_0_ = f32[4,1584,128]{2,1,0:T(8,128)S(1)} collective-permute-done((f32[4,1584,128]{2,1,0:T(8,128)S(1)}, f32[4,1584,128]{2,1,0:T(8,128)S(1)}, u32[]{:S(2)}, u32[]{:S(2)}) %collective-permute-start.16) | collective-permute-done | bytes 3244064 | tf_op jit(solution)/shard_map/ppermute | solution.py:37
  123.0 3.8 %collective-permute-done.17.refs_1_ = f32[4,1584,128]{2,1,0:T(8,128)} collective-permute-done((f32[4,1584,128]{2,1,0:T(8,128)S(1)}, f32[4,1584,128]{2,1,0:T(8,128)}, u32[]{:S(2)}, u32[]{:S(2)}) %collective-permute-start.17) | collective-permute-done | bytes 3244064 | tf_op jit(solution)/shard_map/ppermute | solution.py:37
  126.8 1.6 shard_map.41
  128.5 2.0 %collective-permute-start.21 = (f32[2,1584,128]{2,1,0:T(8,128)S(1)}, f32[2,1584,128]{2,1,0:T(8,128)}, u32[]{:S(2)}, u32[]{:S(2)}) collective-permute-start(f32[2,1584,128]{2,1,0:T(8,128)S(1)} %get-tuple-element.29), channel_id=1, source_target_pairs={{0,1},{1,2},{2,3},{3,0},{4,5},{5,6},{6,7},{7,4},{8,9},{9,10},{10,1... | collective-permute-start | bytes 4866056 | tf_op jit(solution)/shard_map/ppermute | solution.py:37
  130.5 2.6 %shard_map.42 = (bf16[4,528,384]{2,1,0:T(8,128)(2,1)S(1)}, bf16[4,528,384]{2,1,0:T(8,128)(2,1)S(1)}) custom-call(f32[4,3,528,128]{3,2,1,0:T(8,128)S(1)} %bitcast.9), custom_call_target="tpu_custom_call" | custom-call | flops 4000000 | bytes 7000000 | tf_op jit(solution)/shard_map/pallas_call | solution.py:297
  133.2 1.2 copy-done.5
  134.4 2.6 %shard_map.43 = (bf16[4,528,384]{2,1,0:T(8,128)(2,1)S(1)}, bf16[4,528,384]{2,1,0:T(8,128)(2,1)S(1)}) custom-call(f32[4,3,528,128]{3,2,1,0:T(8,128)S(1)} %bitcast.10, f32[8,128]{1,0:T(8,128)S(1)} %get-tuple-element.27.refs_2_.refs_0_), custom_call_target="tpu_custom_call" | custom-call | flops 4000000 | bytes 7000000 | tf_op jit(solution)/shard_map/pallas_call | solution.py:297
  137.0 1.2 copy-done.7
  138.2 4.7 %shard_map.44 = (bf16[4,528,384]{2,1,0:T(8,128)(2,1)S(1)}, bf16[4,528,384]{2,1,0:T(8,128)(2,1)S(1)}) custom-call(f32[4,3,528,128]{3,2,1,0:T(8,128)} %bitcast.8.q, f32[8,128]{1,0:T(8,128)S(1)} %get-tuple-element.27.refs_2_.refs_0_), custom_call_target="tpu_custom_call" | custom-call | flops 4000000 | bytes 7000000 | tf_op jit(solution)/shard_map/pallas_call | solution.py:297
  142.9 1.2 copy-done.9
  144.1 1.2 copy-done.10
  145.3 26.1 %shard_map.45.r_ref = f32[2304,1152]{1,0:T(8,128)} custom-call(bf16[4,528,384]{2,1,0:T(8,128)(2,1)} %copy-done.5, bf16[4,528,384]{2,1,0:T(8,128)(2,1)} %copy-done.7, bf16[4,528,384]{2,1,0:T(8,128)(2,1)} %copy-done.9, bf16[4,528,384]{2,1,0:T(8,128)(2,1)} %copy-done.6, bf16[4,528,384]{2,1,0:T(8,128)(2,1)} %copy-done.8, ...), custom_call_target="tpu_custom_call", output_to_operand_aliasing={{}: (9, {})} | custom-call | flops 16817061888 | bytes 30000000 | tf_op jit(solution)/shard_map/pallas_call | solution.py:317
  171.4 1.2 copy-done.12
  172.7 15.2 %shard_map.46 = f32[2304,1152]{1,0:T(8,128)} custom-call(f32[2,3,528,128]{3,2,1,0:T(8,128)} %bitcast.11, f32[2,3,528,128]{3,2,1,0:T(8,128)} %bitcast.5.qb, bf16[1536,1152]{1,0:T(8,128)(2,1)} %get-tuple-element.30.refs_6_.xh, bf16[1536,1152]{1,0:T(8,128)(2,1)} %get-tuple-element.31.refs_7_.xl, ...), custom_call_target="tpu_custom_call", output_to_operand_aliasing={{}: (4, {})} | custom-call | flops 5605687296 | bytes 25000000 | tf_op jit(solution)/shard_map/pallas_call | solution.py:331
  (43 shorter events, 4.0 us)
Async XLA Ops:
  2.1 2.7 %copy-start.2 = (f32[3,64,1152]{2,1,0:T(8,128)S(1)}, f32[3,64,1152]{2,1,0:T(8,128)}, u32[]{:S(2)}) copy-start(f32[3,64,1152]{2,1,0:T(8,128)} %shard_map.29.refs_0_.b0) | copy-start | bytes 2654212
  2.1 2.7 %collective-permute-start.3 = (f32[3,64,1152]{2,1,0:T(8,128)}, f32[3,64,1152]{2,1,0:T(8,128)S(1)}, u32[]{:S(2)}, u32[]{:S(2)}) collective-permute-start(f32[3,64,1152]{2,1,0:T(8,128)} %shard_map.29.refs_0_.b0), channel_id=1, source_target_pairs={{0,16},{1,17},{2,18},{3,19},{4,20},{5,21},{6,22},{7,23},{8,24},{9,... | collective-permute-start | bytes 2654216 | tf_op jit(solution)/shard_map/ppermute | solution.py:37
  4.5 1.9 %copy-start.3 = (f32[1584,128]{1,0:T(8,128)}, f32[1584,128]{1,0:T(8,128)S(1)}, u32[]{:S(2)}) copy-start(f32[1584,128]{1,0:T(8,128)S(1)} %get-tuple-element.22.refs_2_.refs_0_) | copy-start | bytes 2433028
  6.4 23.5 %collective-permute-start.9 = (f32[2,3,64,1152]{3,2,1,0:T(8,128)}, f32[2,3,64,1152]{3,2,1,0:T(8,128)S(1)}, u32[]{:S(2)}, u32[]{:S(2)}) collective-permute-start(f32[2,3,64,1152]{3,2,1,0:T(8,128)} %shard_map.30.refs_4_), channel_id=1, source_target_pairs={{0,96},{1,97},{2,98},{3,99},{4,100},{5,101},{6,102},{7,103},{8,104... | collective-permute-start | bytes 5308424 | tf_op jit(solution)/shard_map/ppermute | solution.py:37
  9.6 4.7 %collective-permute-start = (f32[128,128]{1,0:T(8,128)S(1)}, f32[128,128]{1,0:T(8,128)S(1)}, u32[]{:S(2)}, u32[]{:S(2)}) collective-permute-start(f32[128,128]{1,0:T(8,128)S(1)} %get-tuple-element.23.refs_0_), channel_id=1, source_target_pairs={{0,12},{1,13},{2,14},{3,15},{4,0},{5,1},{6,2},{7,3},{8,4},{9,5},{1... | collective-permute-start | bytes 196616 | tf_op jit(solution)/shard_map/ppermute | solution.py:37
  12.3 5.8 %collective-permute-start.1 = (f32[128,128]{1,0:T(8,128)S(1)}, f32[128,128]{1,0:T(8,128)S(1)}, u32[]{:S(2)}, u32[]{:S(2)}) collective-permute-start(f32[128,128]{1,0:T(8,128)S(1)} %get-tuple-element.23.refs_0_), channel_id=1, source_target_pairs={{0,8},{1,9},{2,10},{3,11},{4,12},{5,13},{6,14},{7,15},{8,0},{9,1},... | collective-permute-start | bytes 196616 | tf_op jit(solution)/shard_map/ppermute | solution.py:37
  13.1 5.7 %collective-permute-start.2 = (f32[128,128]{1,0:T(8,128)S(1)}, f32[128,128]{1,0:T(8,128)S(1)}, u32[]{:S(2)}, u32[]{:S(2)}) collective-permute-start(f32[128,128]{1,0:T(8,128)S(1)} %get-tuple-element.23.refs_0_), channel_id=1, source_target_pairs={{0,4},{1,5},{2,6},{3,7},{4,8},{5,9},{6,10},{7,11},{8,12},{9,13},{1... | collective-permute-start | bytes 196616 | tf_op jit(solution)/shard_map/ppermute | solution.py:37
  19.9 14.0 %collective-permute-start.4 = (f32[4,128,128]{2,1,0:T(8,128)}, f32[4,128,128]{2,1,0:T(8,128)}, u32[]{:S(2)}, u32[]{:S(2)}) collective-permute-start(f32[4,128,128]{2,1,0:T(8,128)} %shard_map.31.g0), channel_id=1, source_target_pairs={{0,3},{1,0},{2,1},{3,2},{4,7},{5,4},{6,5},{7,6},{8,11},{9,8},{10,9... | collective-permute-start | bytes 786440 | tf_op jit(solution)/shard_map/ppermute | solution.py:37
  24.0 9.9 %collective-permute-start.5 = (f32[4,128,128]{2,1,0:T(8,128)}, f32[4,128,128]{2,1,0:T(8,128)}, u32[]{:S(2)}, u32[]{:S(2)}) collective-permute-start(f32[4,128,128]{2,1,0:T(8,128)} %shard_map.31.g0), channel_id=1, source_target_pairs={{0,2},{1,3},{2,0},{3,1},{4,6},{5,7},{6,4},{7,5},{8,10},{9,11},{10,... | collective-permute-start | bytes 786440 | tf_op jit(solution)/shard_map/ppermute | solution.py:37
  24.0 10.7 %collective-permute-start.6 = (f32[4,128,128]{2,1,0:T(8,128)}, f32[4,128,128]{2,1,0:T(8,128)}, u32[]{:S(2)}, u32[]{:S(2)}) collective-permute-start(f32[4,128,128]{2,1,0:T(8,128)} %shard_map.31.g0), channel_id=1, source_target_pairs={{0,1},{1,2},{2,3},{3,0},{4,5},{5,6},{6,7},{7,4},{8,9},{9,10},{10,1... | collective-permute-start | bytes 786440 | tf_op jit(solution)/shard_map/ppermute | solution.py:37
  25.2 9.5 %copy-start.4 = (f32[1584,128]{1,0:T(8,128)S(1)}, f32[1584,128]{1,0:T(8,128)}, u32[]{:S(2)}) copy-start(f32[1584,128]{1,0:T(8,128)} %copy-done.3) | copy-start | bytes 2433028
  30.1 14.2 %collective-permute-start.11 = (f32[1,3,64,1152]{3,2,1,0:T(8,128)S(1)}, f32[1,3,64,1152]{3,2,1,0:T(8,128)S(1)}, u32[]{:S(2)}, u32[]{:S(2)}) collective-permute-start(f32[1,3,64,1152]{3,2,1,0:T(8,128)S(1)} %shard_map.34), channel_id=1, source_target_pairs={{0,96},{1,97},{2,98},{3,99},{4,100},{5,101},{6,102},{7,103},{8,104... | collective-permute-start | bytes 2654216 | tf_op jit(solution)/shard_map/ppermute | solution.py:37
  38.3 2.4 %collective-permute-start.10 = (f32[6,64,512]{2,1,0:T(8,128)S(1)}, f32[6,64,512]{2,1,0:T(8,128)S(1)}, u32[]{:S(2)}, u32[]{:S(2)}) collective-permute-start(f32[6,64,512]{2,1,0:T(8,128)S(1)} %shard_map.33.refs_0_.m0), channel_id=1, source_target_pairs={{0,16},{1,17},{2,18},{3,19},{4,20},{5,21},{6,22},{7,23},{8,24},{9,... | collective-permute-start | bytes 2359304 | tf_op jit(solution)/shard_map/ppermute | solution.py:37
  44.5 21.7 %collective-permute-start.12 = (f32[2,6,64,512]{3,2,1,0:T(8,128)S(1)}, f32[2,6,64,512]{3,2,1,0:T(8,128)S(1)}, u32[]{:S(2)}, u32[]{:S(2)}) collective-permute-start(f32[2,6,64,512]{3,2,1,0:T(8,128)S(1)} %shard_map.35), channel_id=1, source_target_pairs={{0,96},{1,97},{2,98},{3,99},{4,100},{5,101},{6,102},{7,103},{8,104... | collective-permute-start | bytes 4718600 | tf_op jit(solution)/shard_map/ppermute | solution.py:37
  48.2 12.5 %collective-permute-start.7 = (f32[1584,128]{1,0:T(8,128)S(1)}, f32[1584,128]{1,0:T(8,128)S(1)}, u32[]{:S(2)}, u32[]{:S(2)}) collective-permute-start(f32[1584,128]{1,0:T(8,128)S(1)} %shard_map.32._packed.refs_0_), channel_id=1, source_target_pairs={{0,12},{1,13},{2,14},{3,15},{4,0},{5,1},{6,2},{7,3},{8,4},{9,5},{1... | collective-permute-start | bytes 2433032 | tf_op jit(solution)/shard_map/ppermute | solution.py:37
  51.0 13.5 %collective-permute-start.8 = (f32[1584,128]{1,0:T(8,128)S(1)}, f32[1584,128]{1,0:T(8,128)S(1)}, u32[]{:S(2)}, u32[]{:S(2)}) collective-permute-start(f32[1584,128]{1,0:T(8,128)S(1)} %shard_map.32._packed.refs_0_), channel_id=1, source_target_pairs={{0,4},{1,5},{2,6},{3,7},{4,8},{5,9},{6,10},{7,11},{8,12},{9,13},{1... | collective-permute-start | bytes 2433032 | tf_op jit(solution)/shard_map/ppermute | solution.py:37
  66.7 15.6 %collective-permute-start.15 = (f32[1,6,64,512]{3,2,1,0:T(8,128)S(1)}, f32[1,6,64,512]{3,2,1,0:T(8,128)S(1)}, u32[]{:S(2)}, u32[]{:S(2)}) collective-permute-start(f32[1,6,64,512]{3,2,1,0:T(8,128)S(1)} %get-tuple-element.26), channel_id=1, source_target_pairs={{0,96},{1,97},{2,98},{3,99},{4,100},{5,101},{6,102},{7,103},{8,104... | collective-permute-start | bytes 2359304 | tf_op jit(solution)/shard_map/ppermute | solution.py:37
  70.4 8.2 %collective-permute-start.13 = (f32[792,128]{1,0:T(8,128)S(1)}, f32[792,128]{1,0:T(8,128)S(1)}, u32[]{:S(2)}, u32[]{:S(2)}) collective-permute-start(f32[792,128]{1,0:T(8,128)S(1)} %get-tuple-element.24), channel_id=1, source_target_pairs={{0,12},{1,13},{2,14},{3,15},{4,0},{5,1},{6,2},{7,3},{8,4},{9,5},{1... | collective-permute-start | bytes 1216520 | tf_op jit(solution)/shard_map/ppermute | solution.py:37
  73.2 9.1 %collective-permute-start.14 = (f32[792,128]{1,0:T(8,128)S(1)}, f32[792,128]{1,0:T(8,128)S(1)}, u32[]{:S(2)}, u32[]{:S(2)}) collective-permute-start(f32[792,128]{1,0:T(8,128)S(1)} %get-tuple-element.25), channel_id=1, source_target_pairs={{0,4},{1,5},{2,6},{3,7},{4,8},{5,9},{6,10},{7,11},{8,12},{9,13},{1... | collective-permute-start | bytes 1216520 | tf_op jit(solution)/shard_map/ppermute | solution.py:37
  83.0 39.9 %collective-permute-start.16 = (f32[4,1584,128]{2,1,0:T(8,128)S(1)}, f32[4,1584,128]{2,1,0:T(8,128)S(1)}, u32[]{:S(2)}, u32[]{:S(2)}) collective-permute-start(f32[4,1584,128]{2,1,0:T(8,128)S(1)} %shard_map.37), channel_id=1, source_target_pairs={{0,3},{1,0},{2,1},{3,2},{4,7},{5,4},{6,5},{7,6},{8,11},{9,8},{10,9... | collective-permute-start | bytes 9732104 | tf_op jit(solution)/shard_map/ppermute | solution.py:37
  87.1 39.6 %collective-permute-start.17 = (f32[4,1584,128]{2,1,0:T(8,128)S(1)}, f32[4,1584,128]{2,1,0:T(8,128)}, u32[]{:S(2)}, u32[]{:S(2)}) collective-permute-start(f32[4,1584,128]{2,1,0:T(8,128)S(1)} %shard_map.37), channel_id=1, source_target_pairs={{0,1},{1,2},{2,3},{3,0},{4,5},{5,6},{6,7},{7,4},{8,9},{9,10},{10,1... | collective-permute-start | bytes 9732104 | tf_op jit(solution)/shard_map/ppermute | solution.py:37
  87.7 1.5 copy-start
  87.7 5.0 %collective-permute-start.19 = (f32[3,3,64,1152]{3,2,1,0:T(8,128)S(1)}, f32[3,3,64,1152]{3,2,1,0:T(8,128)S(1)}, u32[]{:S(2)}, u32[]{:S(2)}) collective-permute-start(f32[3,3,64,1152]{3,2,1,0:T(8,128)S(1)} %shard_map.39.bown), channel_id=1, source_target_pairs={{0,16},{1,17},{2,18},{3,19},{4,20},{5,21},{6,22},{7,23},{8,24},{9,... | collective-permute-start | bytes 7962632 | tf_op jit(solution)/shard_map/ppermute | solution.py:37
  89.2 6.9 %collective-permute-start.18 = (f32[3,6,64,512]{3,2,1,0:T(8,128)S(1)}, f32[3,6,64,512]{3,2,1,0:T(8,128)S(1)}, u32[]{:S(2)}, u32[]{:S(2)}) collective-permute-start(f32[3,6,64,512]{3,2,1,0:T(8,128)S(1)} %shard_map.38.mown), channel_id=1, source_target_pairs={{0,16},{1,17},{2,18},{3,19},{4,20},{5,21},{6,22},{7,23},{8,24},{9,... | collective-permute-start | bytes 7077896 | tf_op jit(solution)/shard_map/ppermute | solution.py:37
  92.8 1.6 copy-start.11
  96.1 1.8 copy-start.1
  128.4 43.0 %collective-permute-start.20 = (f32[2,1584,128]{2,1,0:T(8,128)S(1)}, f32[2,1584,128]{2,1,0:T(8,128)S(1)}, u32[]{:S(2)}, u32[]{:S(2)}) collective-permute-start(f32[2,1584,128]{2,1,0:T(8,128)S(1)} %get-tuple-element.28), channel_id=1, source_target_pairs={{0,3},{1,0},{2,1},{3,2},{4,7},{5,4},{6,5},{7,6},{8,11},{9,8},{10,9... | collective-permute-start | bytes 4866056 | tf_op jit(solution)/shard_map/ppermute | solution.py:37
  128.5 43.0 %collective-permute-start.21 = (f32[2,1584,128]{2,1,0:T(8,128)S(1)}, f32[2,1584,128]{2,1,0:T(8,128)}, u32[]{:S(2)}, u32[]{:S(2)}) collective-permute-start(f32[2,1584,128]{2,1,0:T(8,128)S(1)} %get-tuple-element.29), channel_id=1, source_target_pairs={{0,1},{1,2},{2,3},{3,0},{4,5},{5,6},{6,7},{7,4},{8,9},{9,10},{10,1... | collective-permute-start | bytes 4866056 | tf_op jit(solution)/shard_map/ppermute | solution.py:37
  133.1 1.2 copy-start.5
  134.4 8.5 %copy-start.6 = (bf16[4,528,384]{2,1,0:T(8,128)(2,1)}, bf16[4,528,384]{2,1,0:T(8,128)(2,1)S(1)}, u32[]{:S(2)}) copy-start(bf16[4,528,384]{2,1,0:T(8,128)(2,1)S(1)} %get-tuple-element.35.refs_3_) | copy-start | bytes 4866052
  137.0 1.2 copy-start.7
  138.2 7.1 %copy-start.8 = (bf16[4,528,384]{2,1,0:T(8,128)(2,1)}, bf16[4,528,384]{2,1,0:T(8,128)(2,1)S(1)}, u32[]{:S(2)}) copy-start(bf16[4,528,384]{2,1,0:T(8,128)(2,1)S(1)} %get-tuple-element.36.refs_4_) | copy-start | bytes 4866052
  142.9 1.2 copy-start.9
  144.1 1.2 copy-start.10
  171.4 1.2 copy-start.12
